TPU v7x, 512 devices: a whole 4x4x16 slice. The times are simulated.
512 devices in a mesh: row: 32 (over y, z_hi, core), col: 16 (over z_lo, x).
Axes of the slice: x: 4, y: 4, z: 16 (z_hi: 4, z_lo: 4; z = z_hi * 4 + z_lo), core: 2. Of those that a mesh axis runs over, the one named last changes fastest.
Arguments:
- atoms: bfloat16 [4, 65536, 128], P(None, ('row', 'col')), may hold values from -6 to 6
- cotangent: bfloat16 [4, 65536, 128], P(None, ('row', 'col')), may hold values from -6 to 6
- project: bfloat16 [128, 512], replicated, may hold values from -0.5 to 0.5
- combine: bfloat16 [128, 128], replicated, may hold values from -0.5 to 0.5
- atom_gain: float32 [128], replicated, may hold values from 0.5 to 1.5
- pair_band: bfloat16 [8192, 48, 128], P('row', 'col'), may hold values from -6 to 6
- pair_gain: float32 [128], replicated, may hold values from 0.5 to 1.5
- pair_weight: bfloat16 [128, 4], replicated, may hold values from -1.06066017 to 1.06066017
- atom_token: int32 [65536], P(('row', 'col')), may hold values from 0 to 8191, as said below
- key_range: int32 [2048, 2], P(('row', 'col')), may hold values from 0 to 65536, as said below
Outputs:
- atoms_grad: bfloat16 [4, 65536, 128], P(None, ('row', 'col'))
- project_grad: bfloat16 [128, 512], replicated
- combine_grad: bfloat16 [128, 128], replicated
- scale_grad: float32 [128], replicated
- band_grad: bfloat16 [8192, 48, 128], P('row', 'col')
- weight_grad: bfloat16 [128, 4], replicated
- gain_grad: float32 [128], replicated
Inputs may be any that keep to these rules, and one draw needn't show every extreme that they name: `atom_token`: Nondecreasing; the atoms d * 128 to (d + 1) * 128 - 1 name exactly the tokens d * 16 to (d + 1) * 16 - 1, each at least once. For window w: max(0, w * 32 - 48) <= key_range[w, 0] <= w * 32 and w * 32 + 32 <= key_range[w, 1] <= min(65536, w * 32 + 80); both outer limits are taken by some windows.
All inputs are finite; a program needn't handle non-finite values.
Results may differ from a plain program's by a relative error of at most 0.013.
The roundings to bfloat16 on the way count: a program that leaves them out, or rounds other values in their place, can miss the bound.
Values may be sent and summed in bfloat16 or wider, within the bound.
No kernel may reach another device: no remote copies, remote signals or barrier semaphores. Data moves between devices by JAX's collectives and lax.ppermute only.
A program may use at most 64 MiB of HBM per device.

v0:
```python
import math

import jax
import jax.numpy as jnp
from jax import lax
from jax.sharding import PartitionSpec as P

QW = 32
KW = 128
RIM = 48


EPSILON = 1e-05
NEG_FILL = -1e30
FINEST = lax.Precision.HIGHEST


def padded_2(x, sides, width):
    for axis, dim in sides:
        peers, length = (lax.axis_size(axis), x.shape[dim])
        up = [(i, (i + 1) % peers) for i in range(peers - 1)]
        down = [(j, i) for i, j in up]
        last = lax.slice_in_dim(x, length - width, length, axis=dim)
        leading = lax.slice_in_dim(x, 0, width, axis=dim)
        before = lax.ppermute(last, axis, up)
        after = lax.ppermute(leading, axis, down)
        x = jnp.concatenate([before, x, after], axis=dim)
    return x


def layer_stats(values):
    mean_value = jnp.mean(values, axis=-1, keepdims=True)
    centred = values - mean_value
    inv_std = lax.rsqrt(jnp.mean(centred * centred, axis=-1, keepdims=True) + EPSILON)
    return (centred * inv_std, inv_std)


def layer_back(grad_hat, normal, inv_std):
    first_mean = jnp.mean(grad_hat, axis=-1, keepdims=True)
    second_mean = jnp.mean(grad_hat * normal, axis=-1, keepdims=True)
    return inv_std * (grad_hat - first_mean - normal * second_mean)


def one_hot(indices, columns):
    return (indices[:, None] == jnp.arange(columns, dtype=jnp.int32)[None, :]).astype(jnp.float32)


def key_windows(padded, windows):
    span_count = KW // QW
    blocked = padded.reshape(padded.shape[0], windows + span_count - 1, QW, padded.shape[-1])
    return jnp.concatenate(
        [blocked[:, offset : offset + windows] for offset in range(span_count)], axis=2
    )


def from_windows(grad_win, windows):
    span_count = KW // QW
    lead = grad_win.shape[0]
    pieces = grad_win.reshape(lead, windows, span_count, QW, grad_win.shape[-1])
    summed = jnp.zeros((lead, windows + span_count - 1, QW, grad_win.shape[-1]), jnp.float32)
    for offset in range(span_count):
        summed = summed.at[:, offset : offset + windows].add(pieces[:, :, offset])
    return summed.reshape(lead, (windows + span_count - 1) * QW, grad_win.shape[-1])


def window_bias(table, query_hot, key_hot, windows):
    query_sel = query_hot.reshape(windows, QW, query_hot.shape[-1])
    key_sel = key_windows(key_hot[None], windows)[0]
    row_terms = jnp.einsum("wit,htu->whiu", query_sel, table, precision=FINEST)
    return (jnp.einsum("whiu,wju->whij", row_terms, key_sel, precision=FINEST), query_sel, key_sel)


def table_back(bias_grad, query_sel, key_sel):
    col_terms = jnp.einsum("whij,wju->whiu", bias_grad, key_sel, precision=FINEST)
    return jnp.einsum("wit,whiu->htu", query_sel, col_terms, precision=FINEST)


def window_mask(ranges, first_atom, windows):
    key_pos = (
        first_atom
        - RIM
        + QW * jnp.arange(windows, dtype=jnp.int32)[:, None]
        + jnp.arange(KW, dtype=jnp.int32)[None, :]
    )
    return (key_pos >= ranges[:, 0:1]) & (key_pos < ranges[:, 1:2])


def pair_front(tiles, pair_gain, pair_weight):
    z_hat, inv_std = layer_stats(tiles.astype(jnp.float32))
    pair_norm = (z_hat * pair_gain).astype(jnp.bfloat16)
    bias_rows = jnp.dot(
        pair_norm.reshape(-1, tiles.shape[-1]), pair_weight, preferred_element_type=jnp.float32
    )
    table = jnp.transpose(
        bias_rows.reshape(tiles.shape[0], tiles.shape[1], pair_weight.shape[1]), (2, 0, 1)
    )
    return (table, pair_norm, z_hat, inv_std)


def pair_back(pair_norm, z_hat, inv_std, grad_rows, pair_gain, pair_weight):
    channels = pair_norm.shape[-1]
    weight_part = jnp.dot(
        pair_norm.reshape(-1, channels).T, grad_rows, preferred_element_type=jnp.float32
    )
    norm_grad = jnp.dot(grad_rows, pair_weight.T, preferred_element_type=jnp.float32).astype(
        jnp.bfloat16
    )
    norm_wide = norm_grad.astype(jnp.float32).reshape(z_hat.shape)
    gain_part = jnp.sum(norm_wide * z_hat, axis=(0, 1))
    band_part = layer_back(norm_wide * pair_gain, z_hat, inv_std).astype(jnp.bfloat16)
    return (band_part, weight_part, gain_part)


def attend(query, gate, padded_kv, bias, allowed, cotangent, combine):
    samples, atom_count, inner_width = query.shape
    head_count = bias.shape[1]
    head_dim = inner_width // head_count
    windows = atom_count // QW
    score_scale = 1.0 / math.sqrt(head_dim)
    kv_win = key_windows(padded_kv, windows)
    key_win = kv_win[..., :inner_width].reshape(samples, windows, KW, head_count, head_dim)
    value_win = kv_win[..., inner_width:].reshape(samples, windows, KW, head_count, head_dim)
    query_win = query.reshape(samples, windows, QW, head_count, head_dim)
    scores = (
        jnp.einsum("swihd,swjhd->swhij", query_win, key_win, preferred_element_type=jnp.float32)
        * score_scale
        + bias[None]
    )
    scores = jnp.where(allowed[None, :, None, None, :], scores, NEG_FILL)
    exp_scores = jnp.exp(scores - jnp.max(scores, axis=-1, keepdims=True))
    weights = exp_scores / jnp.sum(exp_scores, axis=-1, keepdims=True)
    weights_low = weights.astype(jnp.bfloat16)
    mixture = jnp.einsum(
        "swhij,swjhd->swihd", weights_low, value_win, preferred_element_type=jnp.float32
    ).reshape(samples, atom_count, inner_width)
    sigmoid = jax.nn.sigmoid(gate.astype(jnp.float32))
    gated_out = (mixture * sigmoid).astype(jnp.bfloat16)
    out_rows = cotangent.reshape(-1, cotangent.shape[-1])
    gated_grad = jnp.dot(out_rows, combine.T, preferred_element_type=jnp.float32).astype(
        jnp.bfloat16
    )
    combine_part = jnp.dot(
        gated_out.reshape(-1, inner_width).T, out_rows, preferred_element_type=jnp.float32
    )
    gated_wide = gated_grad.astype(jnp.float32).reshape(samples, atom_count, inner_width)
    mixture_grad = (gated_wide * sigmoid).astype(jnp.bfloat16)
    gate_grad = (gated_wide * mixture * sigmoid * (1.0 - sigmoid)).astype(jnp.bfloat16)
    mixture_win = mixture_grad.reshape(samples, windows, QW, head_count, head_dim)
    weights_grad = jnp.einsum(
        "swihd,swjhd->swhij", mixture_win, value_win, preferred_element_type=jnp.float32
    )
    weights_grad = lax.optimization_barrier(weights_grad.astype(jnp.bfloat16)).astype(jnp.float32)
    value_grad = jnp.einsum(
        "swhij,swihd->swjhd", weights_low, mixture_win, preferred_element_type=jnp.float32
    )
    row_dot = jnp.sum(weights * weights_grad, axis=-1, keepdims=True)
    score_grad = weights * (weights_grad - row_dot)
    bias_grad = jnp.sum(score_grad, axis=0)
    score_low = (score_grad * score_scale).astype(jnp.bfloat16)
    query_grad = (
        jnp.einsum("swhij,swjhd->swihd", score_low, key_win, preferred_element_type=jnp.float32)
        .reshape(samples, atom_count, inner_width)
        .astype(jnp.bfloat16)
    )
    key_grad = jnp.einsum(
        "swhij,swihd->swjhd", score_low, query_win, preferred_element_type=jnp.float32
    )
    kv_grad = jnp.concatenate(
        [
            key_grad.reshape(samples, windows, KW, inner_width),
            value_grad.reshape(samples, windows, KW, inner_width),
        ],
        axis=-1,
    )
    return (query_grad, gate_grad, from_windows(kv_grad, windows), bias_grad, combine_part)


def shards(
    atoms,
    cotangent,
    project,
    combine,
    atom_gain,
    pair_band,
    pair_gain,
    pair_weight,
    atom_token,
    key_range,
):
    samples, atom_count, channels = atoms.shape
    inner_width = combine.shape[0]
    head_count = pair_weight.shape[1]
    col_count = lax.axis_size("col")
    band_width = pair_band.shape[1] * col_count
    device = lax.axis_index(("row", "col"))
    windows = atom_count // QW
    first_atom = device * atom_count
    x_hat, inv_std = layer_stats(atoms.astype(jnp.float32))
    normed = (x_hat * atom_gain).astype(jnp.bfloat16)
    flat_normed = normed.reshape(-1, channels)
    projected = (
        jnp.dot(flat_normed, project, preferred_element_type=jnp.float32)
        .astype(jnp.bfloat16)
        .reshape(samples, atom_count, 4 * inner_width)
    )
    query = projected[..., :inner_width]
    keyval = projected[..., inner_width : 3 * inner_width]
    gate = projected[..., 3 * inner_width :]
    padded_kv = padded_2(keyval, ((("row", "col"), 1),), RIM)
    padded_tokens = padded_2(atom_token, ((("row", "col"), 0),), RIM)
    tiles = lax.all_to_all(pair_band, "col", split_axis=0, concat_axis=1, tiled=True)
    table, pair_norm, z_hat, pair_std = pair_front(tiles, pair_gain, pair_weight)
    token_rows = table.shape[1]
    token_base = device * token_rows
    query_hot = one_hot(atom_token - token_base, token_rows)
    key_hot = one_hot(padded_tokens - token_base + token_rows, band_width)
    bias, query_sel, key_sel = window_bias(table, query_hot, key_hot, windows)
    allowed = window_mask(key_range, first_atom, windows)
    query_grad, gate_grad, pad_grad, bias_grad, combine_part = attend(
        query, gate, padded_kv, bias, allowed, cotangent, combine
    )
    table_grad = table_back(bias_grad, query_sel, key_sel).astype(jnp.bfloat16)
    grad_rows = jnp.transpose(table_grad, (1, 2, 0)).reshape(-1, head_count)
    local_band, weight_part, gain_part = pair_back(
        pair_norm, z_hat, pair_std, grad_rows, pair_gain, pair_weight
    )
    band_grad = lax.all_to_all(local_band, "col", split_axis=1, concat_axis=0, tiled=True)
    outgoing = jnp.concatenate([pad_grad[:, :RIM], pad_grad[:, RIM + atom_count :]], axis=1).astype(
        jnp.bfloat16
    )
    incoming = padded_2(outgoing, ((("row", "col"), 1),), RIM).astype(jnp.float32)
    kv_total = (
        pad_grad[:, RIM : RIM + atom_count]
        + jnp.pad(incoming[:, :RIM], ((0, 0), (0, atom_count - RIM), (0, 0)))
        + jnp.pad(incoming[:, -RIM:], ((0, 0), (atom_count - RIM, 0), (0, 0)))
    )
    projected_grad = jnp.concatenate(
        [query_grad, kv_total.astype(jnp.bfloat16), gate_grad], axis=-1
    ).reshape(-1, 4 * inner_width)
    project_part = jnp.dot(flat_normed.T, projected_grad, preferred_element_type=jnp.float32)
    normed_grad = jnp.dot(projected_grad, project.T, preferred_element_type=jnp.float32).astype(
        jnp.bfloat16
    )
    normed_wide = normed_grad.astype(jnp.float32).reshape(samples, atom_count, channels)
    scale_part = jnp.sum(normed_wide * x_hat, axis=(0, 1))
    atoms_grad = (
        cotangent.astype(jnp.float32) + layer_back(normed_wide * atom_gain, x_hat, inv_std)
    ).astype(jnp.bfloat16)
    summed = lax.psum(
        (project_part, combine_part, scale_part, weight_part, gain_part), ("row", "col")
    )
    return (
        atoms_grad,
        summed[0].astype(jnp.bfloat16),
        summed[1].astype(jnp.bfloat16),
        summed[2],
        band_grad,
        summed[3].astype(jnp.bfloat16),
        summed[4],
    )


def solution(mesh):
    in_specs = (
        P(None, ("row", "col"), None),
        P(None, ("row", "col"), None),
        P(),
        P(),
        P(),
        P("row", "col", None),
        P(),
        P(),
        P(("row", "col")),
        P(("row", "col"), None),
    )
    out_specs = (P(None, ("row", "col"), None), P(), P(), P(), P("row", "col", None), P(), P())
    return jax.shard_map(shards, mesh=mesh, in_specs=in_specs, out_specs=out_specs, check_vma=False)
```

profile of v0, /device:TPU:1, one launch (start us, length us, event | category | flops | bytes accessed | tf_op | source)
XLA Modules:
  0.0 262.6 jit_solution(2755263282093884315)
XLA Ops:
  1.5 3.9 %collective-permute-start.2 = (s32[48]{0:T(128)S(1)}, s32[48]{0:T(128)S(1)}, u32[]{:S(2)}, u32[]{:S(2)}) collective-permute-start(s32[48]{0:T(128)S(1)} %get-tuple-element.85), channel_id=1, source_target_pairs={{0,1},{1,2},{2,3},{3,4},{4,5},{5,6},{6,7},{7,8},{8,9},{9,10},{10,1... | collective-permute-start | bytes 584 | tf_op jit(solution)/shard_map/ppermute | solution.py:25
  5.5 7.8 %collective-permute-start.3 = (s32[48]{0:T(128)S(1)}, s32[48]{0:T(128)S(1)}, u32[]{:S(2)}, u32[]{:S(2)}) collective-permute-start(s32[48]{0:T(128)S(1)} %get-tuple-element.86), channel_id=1, source_target_pairs={{1,0},{2,1},{3,2},{4,3},{5,4},{6,5},{7,6},{8,7},{9,8},{10,9},{11,1... | collective-permute-start | bytes 584 | tf_op jit(solution)/shard_map/ppermute | solution.py:26
  13.3 1.8 copy.91
  15.1 4.1 %all-to-all-start = ((bf16[256,3,128]{2,1,0:T(4,128)(2,1)}), bf16[256,3,128]{2,1,0:T(4,128)(2,1)S(1)}, u32[]{:S(2)}, u32[]{:S(2)}) async-start(bf16[256,3,128]{2,1,0:T(4,128)(2,1)} %copy.91), calls=%async_computation | async-start | bytes 524288 | tf_op jit(solution)/shard_map/all_to_all | solution.py:211
  22.9 3.3 %collective-permute-start = (bf16[4,48,256]{2,1,0:T(8,128)(2,1)S(1)}, bf16[4,48,256]{2,1,0:T(8,128)(2,1)S(1)}, u32[]{:S(2)}, u32[]{:S(2)}) collective-permute-start(bf16[4,48,256]{2,1,0:T(8,128)(2,1)S(1)} %get-tuple-element.71), channel_id=1, source_target_pairs={{0,1},{1,2},{2,3},{3,4},{4,5},{5,6},{6,7},{7,8},{8,9},{9,10},{10,1... | collective-permute-start | bytes 294920 | tf_op jit(solution)/shard_map/ppermute | solution.py:25
  26.2 6.2 %collective-permute-start.1 = (bf16[4,48,256]{2,1,0:T(8,128)(2,1)S(1)}, bf16[4,48,256]{2,1,0:T(8,128)(2,1)S(1)}, u32[]{:S(2)}, u32[]{:S(2)}) collective-permute-start(bf16[4,48,256]{2,1,0:T(8,128)(2,1)S(1)} %get-tuple-element.72), channel_id=1, source_target_pairs={{1,0},{2,1},{3,2},{4,3},{5,4},{6,5},{7,6},{8,7},{9,8},{10,9},{11,1... | collective-permute-start | bytes 294920 | tf_op jit(solution)/shard_map/ppermute | solution.py:26
  40.3 2.3 copy.128
  42.6 2.6 pad_maximum_fusion
  52.1 4.7 %convolution_bitcast_fusion = f32[4,4,32,4,32]{2,4,3,1,0:T(8,128)} fusion(bf16[4,4,128,4,32]{2,4,3,1,0:T(8,128)(2,1)S(1)} %bitcast.169, f32[4,4,4,32]{3,2,1,0:T(4,128)S(1)} %get-tuple-element.87, f32[4,4,4,32,128]{4,3,2,1,0:T(8,128)S(1)} %fusion.7), kind=kOutput, calls=%fused_computation.12 | convolution fusion | flops 17565824 | bytes 1843200 | tf_op jit(solution)/shard_map/swhij,swjhd->swihd/dot_general | solution.py:133
  56.8 1.7 copy.106
  59.0 1.8 convolution_bitcast_fusion.6
  60.8 1.7 fusion.49
  64.4 5.4 %convolution_bitcast_fusion.1 = f32[4,4,128,4,32]{2,4,3,1,0:T(8,128)} fusion(bf16[4,4,32,4,32]{2,4,3,1,0:T(8,128)(2,1)S(1)} %copy.101, f32[4,4,4,32]{3,2,1,0:T(4,128)} %copy-done.26, f32[4,4,4,32,128]{4,3,2,1,0:T(8,128)S(1)} %fusion.7), kind=kOutput, calls=%fused_computation.13 | convolution fusion | flops 17565824 | bytes 2236416 | tf_op jit(solution)/shard_map/swhij,swihd->swjhd/dot_general | solution.py:153
  69.8 13.7 %fusion.9 = bf16[4,4,32,4,32]{2,4,3,1,0:T(8,128)(2,1)} fusion(bf16[4,4,128,4,32]{2,4,3,1,0:T(8,128)(2,1)S(1)} %bitcast.168, bf16[4,4,4,32,128]{4,3,2,1,0:T(8,128)(2,1)S(1)} %convolution_convert_fusion.1, f32[4,4,4,32,128]{4,3,2,1,0:T(8,128)} %get-tuple-element.88, f32[4,4,4,32]{3,2,1,0:T(4,128)S(1)} %copy-done.27), kind=kOutput, calls=%fused_computation.23 | convolution fusion | flops 19204224 | bytes 2236416 | tf_op jit(solution)/shard_map/swhij,swjhd->swihd/dot_general | solution.py:161
  83.5 11.9 %fusion.86 = f32[4,4,32,128]{3,2,1,0:T(8,128)S(1)} fusion(bf16[4,4,4,32,128]{4,3,2,1,0:T(8,128)(2,1)S(1)} %convolution_convert_fusion.1, f32[4,4,4,32,128]{4,3,2,1,0:T(8,128)S(1)} %copy-done.11, f32[4,4,4,32]{3,2,1,0:T(4,128)} %copy-done.26), kind=kOutput, calls=%fused_computation.150 | output fusion | flops 2033791 | bytes 1843200 | tf_op jit(solution)/shard_map/sub | solution.py:157
  95.4 13.7 %convolution_bitcast_fusion.2 = f32[4,4,128,4,32]{2,4,3,1,0:T(8,128)} fusion(bf16[4,4,32,4,32]{2,4,3,1,0:T(8,128)(2,1)S(1)} %copy-done.5, bf16[4,4,4,32,128]{4,3,2,1,0:T(8,128)(2,1)S(1)} %convolution_convert_fusion.1, f32[4,4,4,32,128]{4,3,2,1,0:T(8,128)} %get-tuple-element.88, f32[4,4,4,32]{3,2,1,0:T(4,128)S(1)} %copy-done.28), kind=kOutput, calls=%fused_computation.14 | convolution fusion | flops 19138688 | bytes 2760704 | tf_op jit(solution)/shard_map/swhij,swihd->swjhd/dot_general | solution.py:165
  114.0 7.6 %all-to-all-start.1 = ((bf16[16,48,128]{2,0,1:T(8,128)(2,1)}), bf16[16,48,128]{2,0,1:T(8,128)(2,1)S(1)}, u32[]{:S(2)}, u32[]{:S(2)}) async-start(bf16[16,48,128]{2,0,1:T(8,128)(2,1)} %fusion.34), calls=%async_computation.1 | async-start | bytes 393216 | tf_op jit(solution)/shard_map/all_to_all | solution.py:227
  121.6 4.3 %reshape.486 = f32[4,4,4,32,128]{3,2,4,1,0:T(4,128)} reshape(f32[4,4,128,4,32]{2,4,3,1,0:T(8,128)} %convolution_bitcast_fusion.2) | data formatting | bytes 2097152 | tf_op jit(solution)/shard_map/concatenate | solution.py:168
  126.0 3.5 %copy.123 = f32[4,4,4,32,128]{4,3,2,1,0:T(8,128)S(1)} copy(f32[4,4,4,32,128]{3,2,4,1,0:T(4,128)} %reshape.486) | data formatting | bytes 2097152 | tf_op jit(solution)/shard_map/concatenate | solution.py:168
  129.5 3.2 %reshape.487 = f32[4,4,4,32,128]{3,2,4,1,0:T(4,128)} reshape(f32[4,4,128,4,32]{2,4,3,1,0:T(8,128)S(1)} %copy-done.10) | data formatting | bytes 2097152 | tf_op jit(solution)/shard_map/concatenate | solution.py:168
  132.7 3.4 %copy.124 = f32[4,4,4,32,128]{4,3,2,1,0:T(8,128)S(1)} copy(f32[4,4,4,32,128]{3,2,4,1,0:T(4,128)} %reshape.487) | data formatting | bytes 2097152 | tf_op jit(solution)/shard_map/concatenate | solution.py:168
  136.8 3.4 %collective-permute-start.4 = (bf16[4,48,256]{2,1,0:T(8,128)(2,1)S(1)}, bf16[4,48,256]{2,1,0:T(8,128)(2,1)S(1)}, u32[]{:S(2)}, u32[]{:S(2)}) collective-permute-start(bf16[4,48,256]{2,1,0:T(8,128)(2,1)S(1)} %get-tuple-element.73), channel_id=1, source_target_pairs={{0,1},{1,2},{2,3},{3,4},{4,5},{5,6},{6,7},{7,8},{8,9},{9,10},{10,1... | collective-permute-start | bytes 294920 | tf_op jit(solution)/shard_map/ppermute | solution.py:25
  140.3 6.2 %collective-permute-start.5 = (bf16[4,48,256]{2,1,0:T(8,128)(2,1)S(1)}, bf16[4,48,256]{2,1,0:T(8,128)(2,1)S(1)}, u32[]{:S(2)}, u32[]{:S(2)}) collective-permute-start(bf16[4,48,256]{2,1,0:T(8,128)(2,1)S(1)} %get-tuple-element.74), channel_id=1, source_target_pairs={{1,0},{2,1},{3,2},{4,3},{5,4},{6,5},{7,6},{8,7},{9,8},{10,9},{11,1... | collective-permute-start | bytes 294920 | tf_op jit(solution)/shard_map/ppermute | solution.py:26
  149.5 111.4 %all-reduce.4 = (bf16[128,512]{1,0:T(8,128)(2,1)}, bf16[128,128]{1,0:T(8,128)(2,1)}, f32[128]{0:T(128)}, bf16[128,4]{0,1:T(4,128)(2,1)}, f32[128]{0:T(128)}) all-reduce(f32[128,512]{1,0:T(8,128)S(1)} %convolution_bitcast_fusion.3, f32[128,128]{1,0:T(8,128)S(1)} %copy-done.23, ...), channel_id=1, replica_groups=mesh['row'=32,'col'=16] {'row','col'}, use_global_device_ids=true, to_apply=%region_9.10 | all-reduce | flops 82688 | bytes 496640 | tf_op jit(solution)/shard_map/psum | solution.py:249
  (180 shorter events, 31.5 us)
Async XLA Ops:
  0.6 21.9 %copy-start = (bf16[128,512]{1,0:T(8,128)(2,1)S(1)}, bf16[128,512]{1,0:T(8,128)(2,1)}, u32[]{:S(2)}) copy-start(bf16[128,512]{1,0:T(8,128)(2,1)} %param.20) | copy-start | bytes 393220
  0.6 31.8 %copy-start.34 = (s32[128]{0:T(128)S(1)}, s32[128]{0:T(128)}, u32[]{:S(2)}) copy-start(s32[128]{0:T(128)} %param.26) | copy-start | bytes 1540
  0.7 31.8 %copy-start.40 = (s32[4,2]{0,1:T(2,128)S(1)}, s32[4,2]{0,1:T(2,128)}, u32[]{:S(2)}) copy-start(s32[4,2]{0,1:T(2,128)} %param.27) | copy-start | bytes 100
  0.7 31.9 %copy-start.18 = (bf16[4,128,128]{2,1,0:T(8,128)(2,1)S(1)}, bf16[4,128,128]{2,1,0:T(8,128)(2,1)}, u32[]{:S(2)}) copy-start(bf16[4,128,128]{2,1,0:T(8,128)(2,1)} %param.19) | copy-start | bytes 393220
  0.7 31.9 %copy-start.29 = (bf16[128,128]{1,0:T(8,128)(2,1)S(1)}, bf16[128,128]{1,0:T(8,128)(2,1)}, u32[]{:S(2)}) copy-start(bf16[128,128]{1,0:T(8,128)(2,1)} %param.21) | copy-start | bytes 98308
  1.5 34.4 %collective-permute-start.2 = (s32[48]{0:T(128)S(1)}, s32[48]{0:T(128)S(1)}, u32[]{:S(2)}, u32[]{:S(2)}) collective-permute-start(s32[48]{0:T(128)S(1)} %get-tuple-element.85), channel_id=1, source_target_pairs={{0,1},{1,2},{2,3},{3,4},{4,5},{5,6},{6,7},{7,8},{8,9},{9,10},{10,1... | collective-permute-start | bytes 584 | tf_op jit(solution)/shard_map/ppermute | solution.py:25
  5.5 30.4 %collective-permute-start.3 = (s32[48]{0:T(128)S(1)}, s32[48]{0:T(128)S(1)}, u32[]{:S(2)}, u32[]{:S(2)}) collective-permute-start(s32[48]{0:T(128)S(1)} %get-tuple-element.86), channel_id=1, source_target_pairs={{1,0},{2,1},{3,2},{4,3},{5,4},{6,5},{7,6},{8,7},{9,8},{10,9},{11,1... | collective-permute-start | bytes 584 | tf_op jit(solution)/shard_map/ppermute | solution.py:26
  15.1 30.2 %all-to-all-start = ((bf16[256,3,128]{2,1,0:T(4,128)(2,1)}), bf16[256,3,128]{2,1,0:T(4,128)(2,1)S(1)}, u32[]{:S(2)}, u32[]{:S(2)}) async-start(bf16[256,3,128]{2,1,0:T(4,128)(2,1)} %copy.91), calls=%async_computation | async-start | bytes 524288 | tf_op jit(solution)/shard_map/all_to_all | solution.py:211
  20.3 13.7 %copy-start.24 = (f32[4,128]{1,0:T(4,128)}, f32[4,128]{1,0:T(4,128)S(1)}, u32[]{:S(2)}) copy-start(f32[4,128]{1,0:T(4,128)S(1)} %broadcast_multiply_fusion.4) | copy-start | bytes 6148
  21.4 12.5 %copy-start.30 = (f32[4,128]{1,0:T(4,128)}, f32[4,128]{1,0:T(4,128)S(1)}, u32[]{:S(2)}) copy-start(f32[4,128]{1,0:T(4,128)S(1)} %add_rsqrt_fusion.1) | copy-start | bytes 6148
  22.9 14.0 %collective-permute-start = (bf16[4,48,256]{2,1,0:T(8,128)(2,1)S(1)}, bf16[4,48,256]{2,1,0:T(8,128)(2,1)S(1)}, u32[]{:S(2)}, u32[]{:S(2)}) collective-permute-start(bf16[4,48,256]{2,1,0:T(8,128)(2,1)S(1)} %get-tuple-element.71), channel_id=1, source_target_pairs={{0,1},{1,2},{2,3},{3,4},{4,5},{5,6},{6,7},{7,8},{8,9},{9,10},{10,1... | collective-permute-start | bytes 294920 | tf_op jit(solution)/shard_map/ppermute | solution.py:25
  26.2 10.8 %collective-permute-start.1 = (bf16[4,48,256]{2,1,0:T(8,128)(2,1)S(1)}, bf16[4,48,256]{2,1,0:T(8,128)(2,1)S(1)}, u32[]{:S(2)}, u32[]{:S(2)}) collective-permute-start(bf16[4,48,256]{2,1,0:T(8,128)(2,1)S(1)} %get-tuple-element.72), channel_id=1, source_target_pairs={{1,0},{2,1},{3,2},{4,3},{5,4},{6,5},{7,6},{8,7},{9,8},{10,9},{11,1... | collective-permute-start | bytes 294920 | tf_op jit(solution)/shard_map/ppermute | solution.py:26
  69.8 13.7 %copy-start.11 = (f32[4,4,4,32,128]{4,3,2,1,0:T(8,128)S(1)}, f32[4,4,4,32,128]{4,3,2,1,0:T(8,128)}, u32[]{:S(2)}) copy-start(f32[4,4,4,32,128]{4,3,2,1,0:T(8,128)} %get-tuple-element.88) | copy-start | bytes 3145732
  83.5 11.9 %copy-start.5 = (bf16[4,4,32,4,32]{2,4,3,1,0:T(8,128)(2,1)S(1)}, bf16[4,4,32,4,32]{2,4,3,1,0:T(8,128)(2,1)}, u32[]{:S(2)}) copy-start(bf16[4,4,32,4,32]{2,4,3,1,0:T(8,128)(2,1)} %copy.99) | copy-start | bytes 393220
  83.5 11.9 %copy-start.28 = (f32[4,4,4,32]{3,2,1,0:T(4,128)S(1)}, f32[4,4,4,32]{3,2,1,0:T(4,128)}, u32[]{:S(2)}) copy-start(f32[4,4,4,32]{3,2,1,0:T(4,128)} %copy-done.26) | copy-start | bytes 24580
  95.4 15.2 %copy-start.16 = (f32[16,16,3]{2,1,0:T(8,128)S(1)}, f32[16,16,3]{2,1,0:T(8,128)}, u32[]{:S(2)}) copy-start(f32[16,16,3]{2,1,0:T(8,128)} %copy.113) | copy-start | bytes 9220
  95.4 15.4 %copy-start.17 = (f32[16,16,3]{2,1,0:T(8,128)S(1)}, f32[16,16,3]{2,1,0:T(8,128)}, u32[]{:S(2)}) copy-start(f32[16,16,3]{2,1,0:T(8,128)} %copy.114) | copy-start | bytes 9220
  95.4 15.6 %copy-start.6 = (f32[16,16,3,128]{3,2,1,0:T(4,128)S(1)}, f32[16,16,3,128]{3,2,1,0:T(4,128)}, u32[]{:S(2)}) copy-start(f32[16,16,3,128]{3,2,1,0:T(4,128)} %copy.112) | copy-start | bytes 1179652
  114.0 147.9 %all-to-all-start.1 = ((bf16[16,48,128]{2,0,1:T(8,128)(2,1)}), bf16[16,48,128]{2,0,1:T(8,128)(2,1)S(1)}, u32[]{:S(2)}, u32[]{:S(2)}) async-start(bf16[16,48,128]{2,0,1:T(8,128)(2,1)} %fusion.34), calls=%async_computation.1 | async-start | bytes 393216 | tf_op jit(solution)/shard_map/all_to_all | solution.py:227
  136.8 11.6 %copy-start.21 = (bf16[4,128,128]{2,1,0:T(8,128)(2,1)S(1)}, bf16[4,128,128]{2,1,0:T(8,128)(2,1)}, u32[]{:S(2)}) copy-start(bf16[4,128,128]{2,1,0:T(8,128)(2,1)} %copy-done.20) | copy-start | bytes 393220
  136.8 11.6 %copy-start.22 = (bf16[4,128,128]{2,1,0:T(8,128)(2,1)S(1)}, bf16[4,128,128]{2,1,0:T(8,128)(2,1)}, u32[]{:S(2)}) copy-start(bf16[4,128,128]{2,1,0:T(8,128)(2,1)} %get-tuple-element.70) | copy-start | bytes 393220
  136.8 10.0 %collective-permute-start.4 = (bf16[4,48,256]{2,1,0:T(8,128)(2,1)S(1)}, bf16[4,48,256]{2,1,0:T(8,128)(2,1)S(1)}, u32[]{:S(2)}, u32[]{:S(2)}) collective-permute-start(bf16[4,48,256]{2,1,0:T(8,128)(2,1)S(1)} %get-tuple-element.73), channel_id=1, source_target_pairs={{0,1},{1,2},{2,3},{3,4},{4,5},{5,6},{6,7},{7,8},{8,9},{9,10},{10,1... | collective-permute-start | bytes 294920 | tf_op jit(solution)/shard_map/ppermute | solution.py:25
  140.3 7.8 %collective-permute-start.5 = (bf16[4,48,256]{2,1,0:T(8,128)(2,1)S(1)}, bf16[4,48,256]{2,1,0:T(8,128)(2,1)S(1)}, u32[]{:S(2)}, u32[]{:S(2)}) collective-permute-start(bf16[4,48,256]{2,1,0:T(8,128)(2,1)S(1)} %get-tuple-element.74), channel_id=1, source_target_pairs={{1,0},{2,1},{3,2},{4,3},{5,4},{6,5},{7,6},{8,7},{9,8},{10,9},{11,1... | collective-permute-start | bytes 294920 | tf_op jit(solution)/shard_map/ppermute | solution.py:26
  148.4 112.5 %copy-start.19 = (bf16[4,128,128]{2,1,0:T(8,128)(2,1)S(1)}, bf16[4,128,128]{2,1,0:T(8,128)(2,1)}, u32[]{:S(2)}) copy-start(bf16[4,128,128]{2,1,0:T(8,128)(2,1)} %param.19) | copy-start | bytes 393220
  (26 other events, 116.2 us)
where the time goes:
time: 264 us; the launch traced here: 263 us
  blocking collectives  111 us (42%)
  matrix products  46.1 us (17%)
  starting transfers between devices  42.6 us (16%)
  local copies, waits for them, and re-layouts  33.2 us (13%)
  other arithmetic  26.3 us (10%)
    psum x1, blocking collectives, shards(): lax.psum((project_part, combine_part, scale_part, weight_part, gain_part)...  111 us
    ppermute x3, starting transfers between devices, padded_2(): after = lax.ppermute(leading, axis, down)  20.2 us
    concatenate x4, local copies, waits for them, and re-layouts, attend(): jnp.concatenate([key_grad.reshape(samples, windows, KW, inner_width), val...  14.5 us
    dot_general x1, matrix products, attend(): jnp.einsum('swhij,swihd->swjhd', score_low, query_win, preferred_element_...  13.7 us
    dot_general x1, matrix products, attend(): jnp.einsum('swhij,swjhd->swihd', score_low, key_win, preferred_element_ty...  13.7 us
    sub x1, other arithmetic, attend(): score_grad = weights * (weights_grad - row_dot)  11.9 us
    ppermute x3, starting transfers between devices, padded_2(): before = lax.ppermute(last, axis, up)  10.6 us
    all_to_all x1, starting transfers between devices, shards(): lax.all_to_all(local_band, 'col', split_axis=1, concat_axis=0, tiled=True)  7.62 us
  transfers between devices with their start and end apart: 8, of which 2 were waited for; matrix products, arithmetic and copies ran while one was open for 14% of the time, Pallas kernels for 0%

commit v1 on v0

v1 whole, which is shorter than its diff:
```python
import math

import jax
import jax.numpy as jnp
from jax import lax
from jax.experimental import pallas as pl
from jax.experimental.pallas import tpu as pltpu
from jax.sharding import PartitionSpec as P

QW = 32
KW = 128
RIM = 48
EPSILON = 1e-05
NEG_FILL = -1e30
F32 = jnp.float32
BF = jnp.bfloat16


def nn(a, b):
    return lax.dot_general(a, b, (((1,), (0,)), ((), ())), preferred_element_type=F32)


def nt(a, b):
    return lax.dot_general(a, b, (((1,), (1,)), ((), ())), preferred_element_type=F32)


def tn(a, b):
    return lax.dot_general(a, b, (((0,), (0,)), ((), ())), preferred_element_type=F32)


def split2(x):
    high = x.astype(BF)
    return high, (x - high.astype(F32)).astype(BF)


def norm(v):
    mean = jnp.mean(v, axis=-1, keepdims=True)
    centred = v - mean
    inv = lax.rsqrt(jnp.mean(centred * centred, axis=-1, keepdims=True) + EPSILON)
    return centred * inv, inv


def norm_back(g, hat, inv):
    first = jnp.mean(g, axis=-1, keepdims=True)
    second = jnp.mean(g * hat, axis=-1, keepdims=True)
    return inv * (g - first - hat * second)


def iota(shape, dim):
    return lax.broadcasted_iota(jnp.int32, shape, dim)


def attention_kernel(
    ranges,
    atoms,
    cotangent,
    before,
    after,
    project,
    combine,
    atom_gain,
    band,
    pair_gain,
    weight_rows,
    query_tokens,
    key_tokens,
    grads,
    to_before,
    to_after,
    own_grad,
    local_band,
    bias,
    bias_grad,
    kv_grad,
    z_hat,
):
    samples, count, width = atoms.shape
    heads = 4
    windows = count // QW
    entries = band.shape[0]
    slots = entries // 16
    extent = count + 2 * RIM
    scale = 1.0 / math.sqrt(width // heads)
    gain = atom_gain[...]

    hat, pair_inv = norm(band[...].astype(F32))
    z_hat[...] = hat
    pair_norm = (hat * pair_gain[...]).astype(BF)
    bias_rows = nt(weight_rows[...], pair_norm)
    stacked = jnp.concatenate(
        [jnp.broadcast_to(bias_rows[h : h + 1], (16, entries)) for h in range(heads)], axis=0
    )
    own_token = (iota((64, entries), 0) & 15) == (iota((64, entries), 1) & 15)
    high, low = split2(jnp.where(own_token, stacked, 0.0))
    spread = (iota((entries, KW), 0) >> 4) == iota((entries, KW), 1)
    spread = jnp.where(spread, 1.0, 0.0).astype(BF)
    table = nn(jnp.concatenate([high, low], axis=0), spread).astype(BF)
    lane = iota((KW, KW), 1)
    line = iota((KW, KW), 0)

    def query_hot(w):
        tokens = query_tokens[w * QW : (w + 1) * QW, :]
        tokens = jnp.concatenate([tokens] * heads, axis=0)
        hit = (tokens == (lane & 15)) & ((line >> 5) == ((lane >> 4) & 3))
        return jnp.where(hit, 1.0, 0.0).astype(BF)

    def key_hot(w):
        return jnp.where(line == key_tokens[w : w + 1, :], 1.0, 0.0).astype(BF)

    for w in range(windows):
        by_key = nn(table, key_hot(w)).astype(BF)
        values = nn(query_hot(w), by_key)
        allowed = (lane >= ranges[w, 0]) & (lane < ranges[w, 1])
        bias[w] = jnp.where(allowed, values, NEG_FILL)
        bias_grad[w] = jnp.zeros((KW, KW), F32)
    grads[...] = jnp.zeros_like(grads)
    same_head = (line >> 5) == (lane >> 5)
    diag = jnp.where(same_head, 1.0, 0.0).astype(BF)
    head_of = iota((QW, width), 1) >> 5

    def spread_heads(x):
        return jnp.concatenate([x] * heads, axis=0) * diag

    def gather_heads(x):
        total = jnp.where(head_of == 0, x[:QW], 0.0)
        for h in range(1, heads):
            total = total + jnp.where(head_of == h, x[h * QW : (h + 1) * QW], 0.0)
        return total

    def sample(s, carry):
        project_sum, combine_sum, scale_sum = carry
        x = jnp.concatenate([before[s], atoms[s], after[s]], axis=0).astype(F32)
        x_hat, _ = norm(x)
        normed = (x_hat * gain).astype(BF)
        projected = nn(normed, project[...]).astype(BF)
        query = projected[RIM : RIM + count, :width]
        key = projected[:, width : 2 * width]
        value = projected[:, 2 * width : 3 * width]
        gate = projected[RIM : RIM + count, 3 * width :].astype(F32)
        out = cotangent[s]
        sigmoid = jax.nn.sigmoid(gate)
        gated_grad = nt(out, combine[...]).astype(BF).astype(F32)
        mixture_grad = (gated_grad * sigmoid).astype(BF)
        kv_grad[...] = jnp.zeros_like(kv_grad)
        mixtures = []
        query_grads = []
        for w in range(windows):
            own = slice(w * QW, (w + 1) * QW)
            near = slice(w * QW, w * QW + KW)
            q = spread_heads(query[own])
            k = key[near]
            v = value[near]
            scores = nt(q, k) * scale + bias[w]
            scores = jnp.exp(scores - jnp.max(scores, axis=-1, keepdims=True))
            weights = scores * (1.0 / jnp.sum(scores, axis=-1, keepdims=True))
            weights_low = weights.astype(BF)
            mixtures.append(gather_heads(nn(weights_low, v)))
            mg = spread_heads(mixture_grad[own])
            weights_grad = nt(mg, v).astype(BF).astype(F32)
            row_dot = jnp.sum(weights * weights_grad, axis=-1, keepdims=True)
            score_grad = weights * (weights_grad - row_dot)
            bias_grad[w] += score_grad
            score_low = (score_grad * scale).astype(BF)
            query_grads.append(gather_heads(nn(score_low, k)).astype(BF))
            kv_grad[near, :width] += tn(score_low, q)
            kv_grad[near, width:] += tn(weights_low, mg)
        mixture = jnp.concatenate(mixtures, axis=0)
        gated = (mixture * sigmoid).astype(BF)
        combine_sum = combine_sum + tn(gated, out)
        gate_grad = (gated_grad * mixture * sigmoid * (1.0 - sigmoid)).astype(BF)
        rim = jnp.zeros((RIM, width), BF)
        query_cols = jnp.concatenate([rim] + query_grads + [rim], axis=0)
        gate_cols = jnp.concatenate([rim, gate_grad, rim], axis=0)
        grad = jnp.concatenate([query_cols, kv_grad[...].astype(BF), gate_cols], axis=1)
        project_sum = project_sum + tn(normed, grad)
        normed_grad = nt(grad, project[...])
        scale_sum = scale_sum + jnp.sum(normed_grad * x_hat, axis=0, keepdims=True)
        to_before[s] = normed_grad[:RIM].astype(BF)
        to_after[s] = normed_grad[RIM + count :].astype(BF)
        own_grad[s] = normed_grad[RIM : RIM + count]
        return project_sum, combine_sum, scale_sum

    start = (
        jnp.zeros((width, 4 * width), F32),
        jnp.zeros((width, width), F32),
        jnp.zeros((1, width), F32),
    )
    project_sum, combine_sum, scale_sum = lax.fori_loop(0, samples, sample, start)
    for part in range(4):
        grads[part * width : (part + 1) * width, :] = project_sum[
            :, part * width : (part + 1) * width
        ].astype(BF)
    grads[4 * width : 5 * width, :] = combine_sum.astype(BF)

    table_grad = jnp.zeros((64, KW), F32)
    for w in range(windows):
        hot = key_hot(w)
        high, low = split2(bias_grad[w])
        by_slot = nt(high, hot) + nt(low, hot)
        high, low = split2(by_slot)
        rows = query_hot(w)
        table_grad = table_grad + (tn(rows, high) + tn(rows, low))[:64]
    table_grad = table_grad.astype(BF)
    entry_grad = jnp.where(own_token, nt(table_grad, spread), 0.0).astype(BF)
    weight_of = jnp.concatenate(
        [jnp.broadcast_to(weight_rows[h : h + 1, :], (16, width)) for h in range(heads)], axis=0
    )
    hat = z_hat[...]
    pair_norm = (hat * pair_gain[...]).astype(BF)
    norm_grad = tn(entry_grad, weight_of).astype(BF).astype(F32)
    weight_part = nn(entry_grad, pair_norm)
    tail = [
        jnp.sum(weight_part[h * 16 : (h + 1) * 16], axis=0, keepdims=True) for h in range(heads)
    ]
    tail = tail + [scale_sum, jnp.sum(norm_grad * hat, axis=0, keepdims=True)]
    tail = tail + [jnp.zeros((10, width), F32)]
    grads[5 * width : 5 * width + 16, :] = jnp.concatenate(tail, axis=0).astype(BF)
    local_band[...] = norm_back(norm_grad * pair_gain[...], hat, pair_inv).astype(BF)


def finish_kernel(atoms, cotangent, own_grad, from_before, from_after, atom_gain, result):
    samples, count, width = atoms.shape
    gain = atom_gain[...]
    for s in range(samples):
        x_hat, inv = norm(atoms[s].astype(F32))
        rim = jnp.zeros((count - RIM, width), F32)
        total = own_grad[s] + jnp.concatenate([from_before[s].astype(F32), rim], axis=0)
        total = total + jnp.concatenate([rim, from_after[s].astype(F32)], axis=0)
        g = total.astype(BF).astype(F32) * gain
        result[s] = (cotangent[s].astype(F32) + norm_back(g, x_hat, inv)).astype(BF)


def vmem(n):
    return [pl.BlockSpec(memory_space=pltpu.VMEM)] * n


def shards(
    atoms,
    cotangent,
    project,
    combine,
    atom_gain,
    pair_band,
    pair_gain,
    pair_weight,
    atom_token,
    key_range,
):
    samples, count, width = atoms.shape
    heads = pair_weight.shape[1]
    rows, cols = lax.axis_size("row"), lax.axis_size("col")
    peers = rows * cols
    device = lax.axis_index(("row", "col"))
    windows = count // QW
    block = pair_band.shape[0] // cols
    keys = pair_band.shape[1]
    up = [(i, i + 1) for i in range(peers - 1)]
    down = [(i + 1, i) for i in range(peers - 1)]

    tiles = jnp.transpose(pair_band.reshape(cols, block, keys, width), (0, 2, 1, 3))
    tiles = lax.all_to_all(tiles, "col", 0, 0, tiled=True).reshape(cols * keys * block, width)

    local = atom_token - device * block

    def packed(part, tokens):
        line = jnp.pad(tokens.astype(BF), (0, width - RIM))
        return jnp.concatenate([part, jnp.broadcast_to(line, (1, RIM, width))], axis=0)

    before = lax.ppermute(packed(atoms[:, count - RIM :], local[count - RIM :]), ("row", "col"), up)
    after = lax.ppermute(packed(atoms[:, :RIM], local[:RIM]), ("row", "col"), down)
    extended = jnp.concatenate(
        [
            before[samples, 0, :RIM].astype(jnp.int32),
            local + block,
            after[samples, 0, :RIM].astype(jnp.int32) + 2 * block,
        ]
    )
    key_tokens = jnp.stack([extended[w * QW : w * QW + KW] for w in range(windows)])
    key_tokens = jnp.pad(key_tokens, ((0, 8 - windows), (0, 0)))
    query_tokens = jnp.broadcast_to(local[:, None], (count, KW))
    first_slot = device * count - RIM + QW * jnp.arange(windows, dtype=jnp.int32)
    ranges = key_range - first_slot[:, None]
    weight_rows = jnp.pad(pair_weight.T, ((0, 16 - heads), (0, 0)))
    gain = atom_gain.reshape(1, width)
    entries = tiles.shape[0]
    shape = jax.ShapeDtypeStruct
    grads, to_before, to_after, own_grad, local_band = pl.pallas_call(
        attention_kernel,
        out_shape=(
            shape((768, width), BF),
            shape((samples, RIM, width), BF),
            shape((samples, RIM, width), BF),
            shape((samples, count, width), F32),
            shape((entries, width), BF),
        ),
        in_specs=[pl.BlockSpec(memory_space=pltpu.SMEM)] + vmem(12),
        out_specs=tuple(vmem(5)),
        scratch_shapes=[
            pltpu.VMEM((windows, KW, KW), F32),
            pltpu.VMEM((windows, KW, KW), F32),
            pltpu.VMEM((count + 2 * RIM, 2 * width), F32),
            pltpu.VMEM((entries, width), F32),
        ],
        compiler_params=pltpu.CompilerParams(vmem_limit_bytes=32 * 1024 * 1024),
        name="attention",
    )(
        ranges,
        atoms,
        cotangent,
        before,
        after,
        project,
        combine,
        gain,
        tiles,
        pair_gain.reshape(1, width),
        weight_rows,
        query_tokens,
        key_tokens,
    )

    from_before = lax.ppermute(to_after, ("row", "col"), up)
    from_after = lax.ppermute(to_before, ("row", "col"), down)

    chunk = grads.shape[0] // cols
    pair = lax.ppermute(grads, "row", [(i, i ^ 1) for i in range(rows)])
    summed = (grads.astype(F32) + pair.astype(F32)).astype(BF).reshape(cols, chunk, width)
    part = lax.all_to_all(summed, "col", 0, 0, tiled=True)
    part = jnp.sum(part.astype(F32), axis=0).astype(BF)
    groups = [list(range(first, rows, 2)) for first in range(2)]
    part = jnp.broadcast_to(part, (rows // 2, chunk, width))
    part = lax.all_to_all(part, "row", 0, 0, axis_index_groups=groups, tiled=True)
    part = jnp.sum(part.astype(F32), axis=0).astype(BF)
    part = jnp.broadcast_to(part, (cols, chunk, width))
    total = lax.all_to_all(part, "col", 0, 0, tiled=True).reshape(cols * chunk, width)

    band_grad = local_band.reshape(cols, keys, block, width)
    band_grad = lax.all_to_all(band_grad, "col", 0, 0, tiled=True)
    band_grad = jnp.transpose(band_grad, (0, 2, 1, 3)).reshape(pair_band.shape)

    atoms_grad = pl.pallas_call(
        finish_kernel,
        out_shape=shape(atoms.shape, BF),
        in_specs=vmem(6),
        out_specs=pl.BlockSpec(memory_space=pltpu.VMEM),
        name="finish",
    )(atoms, cotangent, own_grad, from_before, from_after, gain)

    project_grad = jnp.transpose(total[: 4 * width].reshape(4, width, width), (1, 0, 2))
    tail = total[5 * width :]
    return (
        atoms_grad,
        project_grad.reshape(width, 4 * width),
        total[4 * width : 5 * width],
        tail[heads].astype(F32),
        band_grad,
        tail[:heads].T,
        tail[heads + 1].astype(F32),
    )


def solution(mesh):
    in_specs = (
        P(None, ("row", "col"), None),
        P(None, ("row", "col"), None),
        P(),
        P(),
        P(),
        P("row", "col", None),
        P(),
        P(),
        P(("row", "col")),
        P(("row", "col"), None),
    )
    out_specs = (P(None, ("row", "col"), None), P(), P(), P(), P("row", "col", None), P(), P())
    return jax.shard_map(shards, mesh=mesh, in_specs=in_specs, out_specs=out_specs, check_vma=False)
```

time: 264 us -> 131 us (0.50)
  blocking collectives: 111 us -> 45.4 us
  matrix products: 46.1 us -> 0 us
  other arithmetic: 26.3 us -> 0.86 us
  local copies, waits for them, and re-layouts: 33.2 us -> 8.47 us
  Pallas kernels: 0 us -> 17.9 us
  waiting for transfers between devices: 1.42 us -> 18.4 us
  starting transfers between devices: 42.6 us -> 38.8 us
    psum x1 -> x0, blocking collectives: 111 us -> none  [shards(): lax.psum((project_part, combine_part, scale_part, weight_part, gain_part)...]
    dot_general x18 -> x0, matrix products: 46.1 us -> none  [the longest x1 13.7 us: attend(): jnp.einsum('swhij,swihd->swjhd', score_low, query_win, preferred_element_...]
    all_to_all x0 -> x2, blocking collectives: none -> 45.4 us  [the longest x1 33.5 us: shards(): lax.all_to_all(part, 'row', 0, 0, axis_index_groups=groups, tiled=True)]
    pallas_call x0 -> x2, Pallas kernels: none -> 17.9 us  [the longest x1 15.7 us: shards(): pl.pallas_call(attention_kernel, out_shape=(shape((768, width), BF), shap...]
    all_to_all x2 -> x3, waiting for transfers between devices: 0.01 us -> 16.2 us  [the longest x1 8.36 us: shards(): band_grad = lax.all_to_all(band_grad, 'col', 0, 0, tiled=True)]
    concatenate x4 -> x0, local copies, waits for them, and re-layouts: 14.5 us -> none  [attend(): jnp.concatenate([key_grad.reshape(samples, windows, KW, inner_width), val...]
    sub x3 -> x1, other arithmetic: 13.2 us -> 0.07 us  [shards(): ranges = key_range - first_slot[:, None]]
    convert_element_type x9 -> x3, other arithmetic: 5.48 us -> 0.58 us  [the longest x1 0.52 us: shards(): tail[heads + 1].astype(F32)]
  transfers between devices with their start and end apart: 8 -> 8, of which waited for: 2 -> 4; matrix products, arithmetic and copies ran while one was open for 14% -> 1% of each run, Pallas kernels for 0% -> 2%
where the time goes in v1:
time: 131 us
  blocking collectives  45.4 us (35%)
  starting transfers between devices  38.8 us (30%)
  waiting for transfers between devices  18.4 us (14%)
  Pallas kernels  17.9 us (14%)
  local copies, waits for them, and re-layouts  8.47 us (6%)
    all_to_all x1, blocking collectives, shards(): lax.all_to_all(part, 'row', 0, 0, axis_index_groups=groups, tiled=True)  33.5 us
    pallas_call x1, Pallas kernels, shards(): pl.pallas_call(attention_kernel, out_shape=(shape((768, width), BF), shap...  15.7 us
    all_to_all x1, blocking collectives, shards(): part = lax.all_to_all(summed, 'col', 0, 0, tiled=True)  11.8 us
    ppermute x1, starting transfers between devices, shards(): from_after = lax.ppermute(to_before, ('row', 'col'), down)  9.61 us
    all_to_all x1, waiting for transfers between devices, shards(): band_grad = lax.all_to_all(band_grad, 'col', 0, 0, tiled=True)  8.36 us
    all_to_all x1, waiting for transfers between devices, shards(): lax.all_to_all(tiles, 'col', 0, 0, tiled=True)  7.86 us
    ppermute x1, starting transfers between devices, shards(): lax.ppermute(packed(atoms[:, :RIM], local[:RIM]), ('row', 'col'), down)  7.81 us
    all_to_all x1, starting transfers between devices, shards(): lax.all_to_all(tiles, 'col', 0, 0, tiled=True)  4.27 us
  transfers between devices with their start and end apart: 8, of which 4 were waited for; matrix products, arithmetic and copies ran while one was open for 1% of the time, Pallas kernels for 2%

profile of v1, /device:TPU:1, one launch (start us, length us, event | category | flops | bytes accessed | tf_op | source)
XLA Modules:
  0.0 130.7 jit_solution(12553969570625065879)
XLA Ops:
  0.6 0.6 copy-done.12
  1.4 0.9 fusion.5
  2.3 3.9 %collective-permute-start = (bf16[5,48,128]{2,1,0:T(8,128)(2,1)S(1)}, bf16[5,48,128]{2,1,0:T(8,128)(2,1)S(1)}, u32[]{:S(2)}, u32[]{:S(2)}) collective-permute-start(bf16[5,48,128]{2,1,0:T(8,128)(2,1)S(1)} %pad_maximum_fusion), channel_id=1, source_target_pairs={{0,1},{1,2},{2,3},{3,4},{4,5},{5,6},{6,7},{7,8},{8,9},{9,10},{10,1... | collective-permute-start | bytes 184328 | tf_op jit(solution)/shard_map/ppermute | solution.py:269
  6.3 7.8 %collective-permute-start.1 = (bf16[5,48,128]{2,1,0:T(8,128)(2,1)S(1)}, bf16[5,48,128]{2,1,0:T(8,128)(2,1)S(1)}, u32[]{:S(2)}, u32[]{:S(2)}) collective-permute-start(bf16[5,48,128]{2,1,0:T(8,128)(2,1)S(1)} %pad_maximum_fusion.1), channel_id=1, source_target_pairs={{1,0},{2,1},{3,2},{4,3},{5,4},{6,5},{7,6},{8,7},{9,8},{10,9},{11,1... | collective-permute-start | bytes 184328 | tf_op jit(solution)/shard_map/ppermute | solution.py:270
  14.1 0.7 copy.28
  14.8 4.3 %all-to-all-start = ((bf16[16,3,16,128]{3,2,1,0:T(8,128)(2,1)}), bf16[16,3,16,128]{3,2,1,0:T(8,128)(2,1)S(1)}, u32[]{:S(2)}, u32[]{:S(2)}) async-start(bf16[16,3,16,128]{3,2,1,0:T(8,128)(2,1)} %bitcast.45), calls=%async_computation | async-start | bytes 393216 | tf_op jit(solution)/shard_map/all_to_all | solution.py:261
  19.1 0.7 copy-done.10
  20.0 0.7 copy-done.11
  20.9 7.9 %all-to-all-done = bf16[16,3,16,128]{3,2,1,0:T(8,128)(2,1)S(1)} async-done(((bf16[16,3,16,128]{3,2,1,0:T(8,128)(2,1)}), bf16[16,3,16,128]{3,2,1,0:T(8,128)(2,1)S(1)}, u32[]{:S(2)}, u32[]{:S(2)}) %all-to-all-start) | async-done | bytes 196640 | tf_op jit(solution)/shard_map/all_to_all | solution.py:261
  29.5 15.7 %attention.1 = (bf16[768,128]{1,0:T(8,128)(2,1)S(1)}, bf16[4,48,128]{2,1,0:T(8,128)(2,1)S(1)}, bf16[4,48,128]{2,1,0:T(8,128)(2,1)S(1)}, f32[4,128,128]{2,1,0:T(8,128)S(1)}, bf16[768,128]{1,0:T(8,128)(2,1)}) custom-call(s32[4,2]{1,0:T(4,128)S(1)} %broadcast_subtract_fusion.ranges, bf16[4,128,128]{2,1,0:T(8,128)(2,1)S(1)} %copy-done, ...), custom_call_target="tpu_custom_call" | custom-call | tf_op jit(solution)/shard_map/attention/pallas_call | solution.py:287
  45.2 2.9 %collective-permute-start.4 = (bf16[768,128]{1,0:T(8,128)(2,1)S(1)}, bf16[768,128]{1,0:T(8,128)(2,1)S(1)}, u32[]{:S(2)}, u32[]{:S(2)}) collective-permute-start(bf16[768,128]{1,0:T(8,128)(2,1)S(1)} %get-tuple-element.15), channel_id=1, source_target_pairs={{0,16},{16,0},{32,48},{48,32},{64,80},{80,64},{96,112},{112,96},{1... | collective-permute-start | bytes 589832 | tf_op jit(solution)/shard_map/ppermute | solution.py:326
  48.0 1.0 collective-permute-done.4
  49.1 11.8 %all_to_all.25 = bf16[16,48,128]{2,1,0:T(8,128)(2,1)S(1)} all-to-all(bf16[16,48,128]{2,1,0:T(8,128)(2,1)S(1)} %bitcast.52), channel_id=1, replica_groups=mesh['row'=32,'col'=16] {'col'}, dimensions={0} | all-to-all | bytes 393216 | tf_op jit(solution)/shard_map/all_to_all | solution.py:328
  61.1 33.5 %all_to_all.26 = bf16[16,48,128]{2,1,0:T(8,128)(2,1)S(1)} all-to-all(bf16[16,48,128]{2,1,0:T(8,128)(2,1)S(1)} %broadcast_in_dim.22), channel_id=1, replica_groups={{0,32,64,96,128,160,192,224,256,288,320,352,384,416,448,480},{16,48,80,..., dimensions={0} | all-to-all | bytes 393216 | tf_op jit(solution)/shard_map/all_to_all | solution.py:332
  94.6 3.6 %all-to-all-start.4 = ((bf16[16,3,16,128]{3,2,1,0:T(8,128)(2,1)}), bf16[16,3,16,128]{3,2,1,0:T(8,128)(2,1)S(1)}, u32[]{:S(2)}, u32[]{:S(2)}) async-start(bf16[16,3,16,128]{3,2,1,0:T(8,128)(2,1)} %bitcast.17), calls=%async_computation.4 | async-start | bytes 393216 | tf_op jit(solution)/shard_map/all_to_all | solution.py:338
  98.3 8.4 %all-to-all-done.4 = bf16[16,3,16,128]{3,2,1,0:T(8,128)(2,1)S(1)} async-done(((bf16[16,3,16,128]{3,2,1,0:T(8,128)(2,1)}), bf16[16,3,16,128]{3,2,1,0:T(8,128)(2,1)S(1)}, u32[]{:S(2)}, u32[]{:S(2)}) %all-to-all-start.4) | async-done | bytes 196640 | tf_op jit(solution)/shard_map/all_to_all | solution.py:338
  106.7 0.7 broadcast_in_dim.23
  107.4 3.5 %all-to-all-start.3 = ((bf16[16,48,128]{2,1,0:T(8,128)(2,1)}), bf16[16,48,128]{2,1,0:T(8,128)(2,1)S(1)}, u32[]{:S(2)}, u32[]{:S(2)}) async-start(bf16[16,48,128]{2,1,0:T(8,128)(2,1)} %broadcast_in_dim.23), calls=%async_computation.3 | async-start | bytes 393216 | tf_op jit(solution)/shard_map/all_to_all | solution.py:335
  110.9 3.1 %collective-permute-start.2 = (bf16[4,48,128]{2,1,0:T(8,128)(2,1)S(1)}, bf16[4,48,128]{2,1,0:T(8,128)(2,1)S(1)}, u32[]{:S(2)}, u32[]{:S(2)}) collective-permute-start(bf16[4,48,128]{2,1,0:T(8,128)(2,1)S(1)} %get-tuple-element.13), channel_id=1, source_target_pairs={{0,1},{1,2},{2,3},{3,4},{4,5},{5,6},{6,7},{7,8},{8,9},{9,10},{10,1... | collective-permute-start | bytes 147464 | tf_op jit(solution)/shard_map/ppermute | solution.py:322
  114.0 9.6 %collective-permute-start.3 = (bf16[4,48,128]{2,1,0:T(8,128)(2,1)S(1)}, bf16[4,48,128]{2,1,0:T(8,128)(2,1)S(1)}, u32[]{:S(2)}, u32[]{:S(2)}) collective-permute-start(bf16[4,48,128]{2,1,0:T(8,128)(2,1)S(1)} %get-tuple-element.14), channel_id=1, source_target_pairs={{1,0},{2,1},{3,2},{4,3},{5,4},{6,5},{7,6},{8,7},{9,8},{10,9},{11,1... | collective-permute-start | bytes 147464 | tf_op jit(solution)/shard_map/ppermute | solution.py:323
  123.7 1.1 collective-permute-done.3.from_after
  125.4 2.2 %finish.1 = bf16[4,128,128]{2,1,0:T(8,128)(2,1)} custom-call(bf16[4,128,128]{2,1,0:T(8,128)(2,1)} %atoms.3, bf16[4,128,128]{2,1,0:T(8,128)(2,1)} %cotangent.3, f32[4,128,128]{2,1,0:T(8,128)} %copy-done.2, bf16[4,48,128]{2,1,0:T(8,128)(2,1)} %copy-done.8, bf16[4,48,128]{2,1,0:T(8,128)(2,1)} %copy-done.9, f32[1,128]{1,0:T(1,128)} %bitcast.48), custom_call_target="tpu_custom_call" | custom-call | tf_op jit(solution)/shard_map/finish/pallas_call | solution.py:341
  127.6 0.7 copy.24
  130.0 0.7 copy.29
  (57 shorter events, 3.7 us)
Async XLA Ops:
  0.6 0.7 copy-start.12
  1.4 12.8 %copy-start.7 = (bf16[256,3,128]{2,0,1:T(8,128)(2,1)S(1)}, bf16[256,3,128]{2,0,1:T(8,128)(2,1)}, u32[]{:S(2)}) copy-start(bf16[256,3,128]{2,0,1:T(8,128)(2,1)} %param.15) | copy-start | bytes 589828
  2.3 4.0 %copy-start.13 = (pred[128]{0:T(512)(128)(4,1)S(1)}, pred[128]{0:T(512)(128)(4,1)}, u32[]{:S(2)}) copy-start(pred[128]{0:T(512)(128)(4,1)} %constant.27.clone.1) | copy-start | bytes 388
  2.3 18.4 %collective-permute-start = (bf16[5,48,128]{2,1,0:T(8,128)(2,1)S(1)}, bf16[5,48,128]{2,1,0:T(8,128)(2,1)S(1)}, u32[]{:S(2)}, u32[]{:S(2)}) collective-permute-start(bf16[5,48,128]{2,1,0:T(8,128)(2,1)S(1)} %pad_maximum_fusion), channel_id=1, source_target_pairs={{0,1},{1,2},{2,3},{3,4},{4,5},{5,6},{6,7},{7,8},{8,9},{9,10},{10,1... | collective-permute-start | bytes 184328 | tf_op jit(solution)/shard_map/ppermute | solution.py:269
  6.3 14.4 %collective-permute-start.1 = (bf16[5,48,128]{2,1,0:T(8,128)(2,1)S(1)}, bf16[5,48,128]{2,1,0:T(8,128)(2,1)S(1)}, u32[]{:S(2)}, u32[]{:S(2)}) collective-permute-start(bf16[5,48,128]{2,1,0:T(8,128)(2,1)S(1)} %pad_maximum_fusion.1), channel_id=1, source_target_pairs={{1,0},{2,1},{3,2},{4,3},{5,4},{6,5},{7,6},{8,7},{9,8},{10,9},{11,1... | collective-permute-start | bytes 184328 | tf_op jit(solution)/shard_map/ppermute | solution.py:270
  14.8 14.0 %copy-start = (bf16[4,128,128]{2,1,0:T(8,128)(2,1)S(1)}, bf16[4,128,128]{2,1,0:T(8,128)(2,1)}, u32[]{:S(2)}) copy-start(bf16[4,128,128]{2,1,0:T(8,128)(2,1)} %atoms.3) | copy-start | bytes 393220
  14.8 14.0 %copy-start.1 = (bf16[4,128,128]{2,1,0:T(8,128)(2,1)S(1)}, bf16[4,128,128]{2,1,0:T(8,128)(2,1)}, u32[]{:S(2)}) copy-start(bf16[4,128,128]{2,1,0:T(8,128)(2,1)} %cotangent.3) | copy-start | bytes 393220
  14.8 14.0 %copy-start.3 = (bf16[128,512]{1,0:T(8,128)(2,1)S(1)}, bf16[128,512]{1,0:T(8,128)(2,1)}, u32[]{:S(2)}) copy-start(bf16[128,512]{1,0:T(8,128)(2,1)} %project.1) | copy-start | bytes 393220
  14.8 13.9 %all-to-all-start = ((bf16[16,3,16,128]{3,2,1,0:T(8,128)(2,1)}), bf16[16,3,16,128]{3,2,1,0:T(8,128)(2,1)S(1)}, u32[]{:S(2)}, u32[]{:S(2)}) async-start(bf16[16,3,16,128]{3,2,1,0:T(8,128)(2,1)} %bitcast.45), calls=%async_computation | async-start | bytes 393216 | tf_op jit(solution)/shard_map/all_to_all | solution.py:261
  19.1 0.7 copy-start.10
  20.0 0.7 copy-start.11
  28.7 0.8 copy-start.4
  28.8 0.7 copy-start.5
  28.8 0.7 copy-start.6
  45.1 4.0 %copy-start.2 = (f32[4,128,128]{2,1,0:T(8,128)}, f32[4,128,128]{2,1,0:T(8,128)S(1)}, u32[]{:S(2)}) copy-start(f32[4,128,128]{2,1,0:T(8,128)S(1)} %get-tuple-element.12.own_grad) | copy-start | bytes 786436
  45.2 3.9 %collective-permute-start.4 = (bf16[768,128]{1,0:T(8,128)(2,1)S(1)}, bf16[768,128]{1,0:T(8,128)(2,1)S(1)}, u32[]{:S(2)}, u32[]{:S(2)}) collective-permute-start(bf16[768,128]{1,0:T(8,128)(2,1)S(1)} %get-tuple-element.15), channel_id=1, source_target_pairs={{0,16},{16,0},{32,48},{48,32},{64,80},{80,64},{96,112},{112,96},{1... | collective-permute-start | bytes 589832 | tf_op jit(solution)/shard_map/ppermute | solution.py:326
  94.6 12.1 %all-to-all-start.4 = ((bf16[16,3,16,128]{3,2,1,0:T(8,128)(2,1)}), bf16[16,3,16,128]{3,2,1,0:T(8,128)(2,1)S(1)}, u32[]{:S(2)}, u32[]{:S(2)}) async-start(bf16[16,3,16,128]{3,2,1,0:T(8,128)(2,1)} %bitcast.17), calls=%async_computation.4 | async-start | bytes 393216 | tf_op jit(solution)/shard_map/all_to_all | solution.py:338
  107.4 21.0 %all-to-all-start.3 = ((bf16[16,48,128]{2,1,0:T(8,128)(2,1)}), bf16[16,48,128]{2,1,0:T(8,128)(2,1)S(1)}, u32[]{:S(2)}, u32[]{:S(2)}) async-start(bf16[16,48,128]{2,1,0:T(8,128)(2,1)} %broadcast_in_dim.23), calls=%async_computation.3 | async-start | bytes 393216 | tf_op jit(solution)/shard_map/all_to_all | solution.py:335
  110.9 12.8 %collective-permute-start.2 = (bf16[4,48,128]{2,1,0:T(8,128)(2,1)S(1)}, bf16[4,48,128]{2,1,0:T(8,128)(2,1)S(1)}, u32[]{:S(2)}, u32[]{:S(2)}) collective-permute-start(bf16[4,48,128]{2,1,0:T(8,128)(2,1)S(1)} %get-tuple-element.13), channel_id=1, source_target_pairs={{0,1},{1,2},{2,3},{3,4},{4,5},{5,6},{6,7},{7,8},{8,9},{9,10},{10,1... | collective-permute-start | bytes 147464 | tf_op jit(solution)/shard_map/ppermute | solution.py:322
  114.0 10.8 %collective-permute-start.3 = (bf16[4,48,128]{2,1,0:T(8,128)(2,1)S(1)}, bf16[4,48,128]{2,1,0:T(8,128)(2,1)S(1)}, u32[]{:S(2)}, u32[]{:S(2)}) collective-permute-start(bf16[4,48,128]{2,1,0:T(8,128)(2,1)S(1)} %get-tuple-element.14), channel_id=1, source_target_pairs={{1,0},{2,1},{3,2},{4,3},{5,4},{6,5},{7,6},{8,7},{9,8},{10,9},{11,1... | collective-permute-start | bytes 147464 | tf_op jit(solution)/shard_map/ppermute | solution.py:323
  123.7 1.1 copy-start.8
  124.8 0.6 copy-start.9

commit v2 on v1

--- a/solution.py
+++ b/solution.py
@@ -68,7 +68,7 @@
     to_before,
     to_after,
     own_grad,
-    local_band,
+    outgoing,
     bias,
     bias_grad,
     kv_grad,
@@ -215,7 +215,9 @@
     tail = tail + [scale_sum, jnp.sum(norm_grad * hat, axis=0, keepdims=True)]
     tail = tail + [jnp.zeros((10, width), F32)]
     grads[5 * width : 5 * width + 16, :] = jnp.concatenate(tail, axis=0).astype(BF)
-    local_band[...] = norm_back(norm_grad * pair_gain[...], hat, pair_inv).astype(BF)
+    band_part = norm_back(norm_grad * pair_gain[...], hat, pair_inv).astype(BF)
+    for c in range(16):
+        outgoing[c, : entries // 16, :] = band_part[c * (entries // 16) : (c + 1) * (entries // 16)]
 
 
 def finish_kernel(atoms, cotangent, own_grad, from_before, from_after, atom_gain, result):
@@ -284,14 +286,14 @@
     gain = atom_gain.reshape(1, width)
     entries = tiles.shape[0]
     shape = jax.ShapeDtypeStruct
-    grads, to_before, to_after, own_grad, local_band = pl.pallas_call(
+    grads, to_before, to_after, own_grad, outgoing = pl.pallas_call(
         attention_kernel,
         out_shape=(
             shape((768, width), BF),
             shape((samples, RIM, width), BF),
             shape((samples, RIM, width), BF),
             shape((samples, count, width), F32),
-            shape((entries, width), BF),
+            shape((cols, 2 * RIM - 24, width), BF),
         ),
         in_specs=[pl.BlockSpec(memory_space=pltpu.SMEM)] + vmem(12),
         out_specs=tuple(vmem(5)),
@@ -319,25 +321,30 @@
         key_tokens,
     )
 
-    from_before = lax.ppermute(to_after, ("row", "col"), up)
-    from_after = lax.ppermute(to_before, ("row", "col"), down)
-
-    chunk = grads.shape[0] // cols
-    pair = lax.ppermute(grads, "row", [(i, i ^ 1) for i in range(rows)])
-    summed = (grads.astype(F32) + pair.astype(F32)).astype(BF).reshape(cols, chunk, width)
-    part = lax.all_to_all(summed, "col", 0, 0, tiled=True)
-    part = jnp.sum(part.astype(F32), axis=0).astype(BF)
+    core = lax.axis_index("row") % 2
+    swap = [(i, i ^ 1) for i in range(rows)]
+    grads = grads.reshape(2, grads.shape[0] // 2, width)
+    chunk = grads.shape[1] // cols
+    line = keys * block
+    theirs = lax.ppermute(lax.dynamic_index_in_dim(grads, 1 - core, 0, False), "row", swap)
+    mine = lax.dynamic_index_in_dim(grads, core, 0, False)
+    half = (mine.astype(F32) + theirs.astype(F32)).astype(BF).reshape(cols, chunk, width)
+    outgoing = lax.dynamic_update_slice(outgoing, half, (0, line, 0))
+    scattered = lax.all_to_all(outgoing, "col", 0, 0, tiled=True)
+    band_grad = scattered[:, :line].reshape(cols, keys, block, width)
+    band_grad = jnp.transpose(band_grad, (0, 2, 1, 3)).reshape(pair_band.shape)
+    part = jnp.sum(scattered[:, line:].astype(F32), axis=0).astype(BF)
+
+    part, to_before, to_after = lax.optimization_barrier((part, to_before, to_after))
     groups = [list(range(first, rows, 2)) for first in range(2)]
     part = jnp.broadcast_to(part, (rows // 2, chunk, width))
     part = lax.all_to_all(part, "row", 0, 0, axis_index_groups=groups, tiled=True)
+    from_before = lax.ppermute(to_after, ("row", "col"), up)
+    from_after = lax.ppermute(to_before, ("row", "col"), down)
     part = jnp.sum(part.astype(F32), axis=0).astype(BF)
+    part, from_before, from_after = lax.optimization_barrier((part, from_before, from_after))
     part = jnp.broadcast_to(part, (cols, chunk, width))
-    total = lax.all_to_all(part, "col", 0, 0, tiled=True).reshape(cols * chunk, width)
-
-    band_grad = local_band.reshape(cols, keys, block, width)
-    band_grad = lax.all_to_all(band_grad, "col", 0, 0, tiled=True)
-    band_grad = jnp.transpose(band_grad, (0, 2, 1, 3)).reshape(pair_band.shape)
-
+    half = lax.all_to_all(part, "col", 0, 0, tiled=True).reshape(cols * chunk, width)
     atoms_grad = pl.pallas_call(
         finish_kernel,
         out_shape=shape(atoms.shape, BF),
@@ -345,6 +352,13 @@
         out_specs=pl.BlockSpec(memory_space=pltpu.VMEM),
         name="finish",
     )(atoms, cotangent, own_grad, from_before, from_after, gain)
+    half, atoms_grad, band_grad = lax.optimization_barrier((half, atoms_grad, band_grad))
+    other = lax.ppermute(half, "row", swap)
+    total = jnp.where(
+        core == 0,
+        jnp.concatenate([half, other], axis=0),
+        jnp.concatenate([other, half], axis=0),
+    )
 
     project_grad = jnp.transpose(total[: 4 * width].reshape(4, width, width), (1, 0, 2))
     tail = total[5 * width :]

time: 131 us -> 116 us (0.89)
  blocking collectives: 45.4 us -> 13.4 us
  starting transfers between devices: 38.8 us -> 53.9 us
  waiting for transfers between devices: 18.4 us -> 21.1 us
    all_to_all x2 -> x1, blocking collectives: 45.4 us -> 13.4 us  [shards(): scattered = lax.all_to_all(outgoing, 'col', 0, 0, tiled=True)]
    all_to_all x1, starting transfers between devices: 3.64 us -> 15.4 us  [shards(): lax.all_to_all(part, 'row', 0, 0, axis_index_groups=groups, tiled=True)]
    all_to_all x1, waiting for transfers between devices: 0.01 us -> 5.15 us  [shards(): lax.all_to_all(part, 'col', 0, 0, tiled=True).reshape(cols * chunk, width)]
    all_to_all x1, starting transfers between devices: 3.52 us -> 7.32 us  [shards(): lax.all_to_all(part, 'col', 0, 0, tiled=True).reshape(cols * chunk, width)]
    all_to_all x1, waiting for transfers between devices: 8.36 us -> 4.95 us  [shards(): lax.all_to_all(part, 'row', 0, 0, axis_index_groups=groups, tiled=True)]
    ppermute x1 -> x2, starting transfers between devices: 2.87 us -> 5.68 us  [the longest x1 2.87 us: shards(): lax.ppermute(lax.dynamic_index_in_dim(grads, 1 - core, 0, False), 'row',...]
    ppermute x1, starting transfers between devices: 9.61 us -> 7.28 us  [shards(): from_after = lax.ppermute(to_before, ('row', 'col'), down)]
    all_to_all x1, waiting for transfers between devices: 7.86 us -> 9.17 us  [shards(): lax.all_to_all(tiles, 'col', 0, 0, tiled=True)]
  transfers between devices with their start and end apart: 8 -> 9, of which waited for: 4 -> 5; matrix products, arithmetic and copies ran while one was open for 1% -> 2% of each run, Pallas kernels for 2% -> 2%
where the time goes in v2:
time: 116 us; the launch traced here: 115 us
  starting transfers between devices  53.9 us (46%)
  waiting for transfers between devices  21.1 us (18%)
  Pallas kernels  17.2 us (15%)
  blocking collectives  13.4 us (12%)
  local copies, waits for them, and re-layouts  7.84 us (7%)
    all_to_all x1, starting transfers between devices, shards(): lax.all_to_all(part, 'row', 0, 0, axis_index_groups=groups, tiled=True)  15.4 us
    pallas_call x1, Pallas kernels, shards(): pl.pallas_call(attention_kernel, out_shape=(shape((768, width), BF), shap...  15 us
    all_to_all x1, blocking collectives, shards(): scattered = lax.all_to_all(outgoing, 'col', 0, 0, tiled=True)  13.4 us
    all_to_all x1, waiting for transfers between devices, shards(): lax.all_to_all(tiles, 'col', 0, 0, tiled=True)  9.17 us
    ppermute x1, starting transfers between devices, shards(): lax.ppermute(packed(atoms[:, :RIM], local[:RIM]), ('row', 'col'), down)  7.81 us
    all_to_all x1, starting transfers between devices, shards(): lax.all_to_all(part, 'col', 0, 0, tiled=True).reshape(cols * chunk, width)  7.32 us
    ppermute x1, starting transfers between devices, shards(): from_after = lax.ppermute(to_before, ('row', 'col'), down)  7.28 us
    all_to_all x1, waiting for transfers between devices, shards(): lax.all_to_all(part, 'col', 0, 0, tiled=True).reshape(cols * chunk, width)  5.15 us
  transfers between devices with their start and end apart: 9, of which 5 were waited for; matrix products, arithmetic and copies ran while one was open for 2% of the time, Pallas kernels for 2%

profile of v2, /device:TPU:1, one launch (start us, length us, event | category | flops | bytes accessed | tf_op | source)
XLA Modules:
  0.0 115.4 jit_solution(1059065337582222708)
XLA Ops:
  1.4 0.9 fusion.6
  2.3 3.9 %collective-permute-start = (bf16[5,48,128]{2,1,0:T(8,128)(2,1)S(1)}, bf16[5,48,128]{2,1,0:T(8,128)(2,1)S(1)}, u32[]{:S(2)}, u32[]{:S(2)}) collective-permute-start(bf16[5,48,128]{2,1,0:T(8,128)(2,1)S(1)} %pad_maximum_fusion), channel_id=1, source_target_pairs={{0,1},{1,2},{2,3},{3,4},{4,5},{5,6},{6,7},{7,8},{8,9},{9,10},{10,1... | collective-permute-start | bytes 184328 | tf_op jit(solution)/shard_map/ppermute | solution.py:271
  6.3 7.8 %collective-permute-start.1 = (bf16[5,48,128]{2,1,0:T(8,128)(2,1)S(1)}, bf16[5,48,128]{2,1,0:T(8,128)(2,1)S(1)}, u32[]{:S(2)}, u32[]{:S(2)}) collective-permute-start(bf16[5,48,128]{2,1,0:T(8,128)(2,1)S(1)} %pad_maximum_fusion.1), channel_id=1, source_target_pairs={{1,0},{2,1},{3,2},{4,3},{5,4},{6,5},{7,6},{8,7},{9,8},{10,9},{11,1... | collective-permute-start | bytes 184328 | tf_op jit(solution)/shard_map/ppermute | solution.py:272
  14.1 0.7 copy.28
  14.9 4.3 %all-to-all-start = ((bf16[16,3,16,128]{3,2,1,0:T(8,128)(2,1)}), bf16[16,3,16,128]{3,2,1,0:T(8,128)(2,1)S(1)}, u32[]{:S(2)}, u32[]{:S(2)}) async-start(bf16[16,3,16,128]{3,2,1,0:T(8,128)(2,1)} %bitcast.52), calls=%async_computation | async-start | bytes 393216 | tf_op jit(solution)/shard_map/all_to_all | solution.py:263
  19.6 9.2 %all-to-all-done = bf16[16,3,16,128]{3,2,1,0:T(8,128)(2,1)S(1)} async-done(((bf16[16,3,16,128]{3,2,1,0:T(8,128)(2,1)}), bf16[16,3,16,128]{3,2,1,0:T(8,128)(2,1)S(1)}, u32[]{:S(2)}, u32[]{:S(2)}) %all-to-all-start) | async-done | bytes 196640 | tf_op jit(solution)/shard_map/all_to_all | solution.py:263
  29.5 15.0 %attention.1 = (bf16[768,128]{1,0:T(8,128)(2,1)S(1)}, bf16[4,48,128]{2,1,0:T(8,128)(2,1)S(1)}, bf16[4,48,128]{2,1,0:T(8,128)(2,1)S(1)}, f32[4,128,128]{2,1,0:T(8,128)S(1)}, bf16[16,72,128]{2,1,0:T(8,128)(2,1)S(1)}) custom-call(s32[4,2]{1,0:T(4,128)S(1)} %broadcast_subtract_fusion.ranges, bf16[4,128,128]{2,1,0:T(8,128)(2,1)S(1)} %copy-done, ...), custom_call_target="tpu_custom_call" | custom-call | tf_op jit(solution)/shard_map/attention/pallas_call | solution.py:289
  44.5 0.7 copy-done.2
  45.2 2.9 %collective-permute-start.2 = (bf16[384,128]{1,0:T(8,128)(2,1)S(1)}, bf16[384,128]{1,0:T(8,128)(2,1)S(1)}, u32[]{:S(2)}, u32[]{:S(2)}) collective-permute-start(bf16[384,128]{1,0:T(8,128)(2,1)S(1)} %dynamic-slice_bitcast_fusion), channel_id=1, source_target_pairs={{0,16},{16,0},{32,48},{48,32},{64,80},{80,64},{96,112},{112,96},{1... | collective-permute-start | bytes 294920 | tf_op jit(solution)/shard_map/ppermute | solution.py:329
  48.1 0.9 collective-permute-done.2
  49.1 13.4 %all_to_all.20 = bf16[16,72,128]{2,1,0:T(8,128)(2,1)S(1)} all-to-all(bf16[16,72,128]{2,1,0:T(8,128)(2,1)S(1)} %constant_dynamic-update-slice_fusion), channel_id=1, replica_groups=mesh['row'=32,'col'=16] {'col'}, dimensions={0} | all-to-all | bytes 589824 | tf_op jit(solution)/shard_map/all_to_all | solution.py:333
  62.5 0.7 broadcast_in_dim.22
  63.2 15.4 %all-to-all-start.2 = ((bf16[16,24,128]{2,1,0:T(8,128)(2,1)}), bf16[16,24,128]{2,1,0:T(8,128)(2,1)S(1)}, u32[]{:S(2)}, u32[]{:S(2)}) async-start(bf16[16,24,128]{2,1,0:T(8,128)(2,1)} %broadcast_in_dim.22), calls=%async_computation.2 | async-start | bytes 196608 | tf_op jit(solution)/shard_map/all_to_all | solution.py:341
  78.6 2.2 %collective-permute-start.3 = (bf16[4,48,128]{2,1,0:T(8,128)(2,1)S(1)}, bf16[4,48,128]{2,1,0:T(8,128)(2,1)S(1)}, u32[]{:S(2)}, u32[]{:S(2)}) collective-permute-start(bf16[4,48,128]{2,1,0:T(8,128)(2,1)S(1)} %get-tuple-element.26), channel_id=1, source_target_pairs={{0,1},{1,2},{2,3},{3,4},{4,5},{5,6},{6,7},{7,8},{8,9},{9,10},{10,1... | collective-permute-start | bytes 147464 | tf_op jit(solution)/shard_map/ppermute | solution.py:342
  80.8 7.3 %collective-permute-start.4 = (bf16[4,48,128]{2,1,0:T(8,128)(2,1)S(1)}, bf16[4,48,128]{2,1,0:T(8,128)(2,1)S(1)}, u32[]{:S(2)}, u32[]{:S(2)}) collective-permute-start(bf16[4,48,128]{2,1,0:T(8,128)(2,1)S(1)} %get-tuple-element.27), channel_id=1, source_target_pairs={{1,0},{2,1},{3,2},{4,3},{5,4},{6,5},{7,6},{8,7},{9,8},{10,9},{11,1... | collective-permute-start | bytes 147464 | tf_op jit(solution)/shard_map/ppermute | solution.py:343
  88.1 5.0 %all-to-all-done.2 = bf16[16,24,128]{2,1,0:T(8,128)(2,1)S(1)} async-done(((bf16[16,24,128]{2,1,0:T(8,128)(2,1)}), bf16[16,24,128]{2,1,0:T(8,128)(2,1)S(1)}, u32[]{:S(2)}, u32[]{:S(2)}) %all-to-all-start.2) | async-done | bytes 98336 | tf_op jit(solution)/shard_map/all_to_all | solution.py:341
  93.1 0.7 broadcast_in_dim.23
  93.8 7.3 %all-to-all-start.3 = ((bf16[16,24,128]{2,1,0:T(8,128)(2,1)}), bf16[16,24,128]{2,1,0:T(8,128)(2,1)S(1)}, u32[]{:S(2)}, u32[]{:S(2)}) async-start(bf16[16,24,128]{2,1,0:T(8,128)(2,1)} %broadcast_in_dim.23), calls=%async_computation.3 | async-start | bytes 196608 | tf_op jit(solution)/shard_map/all_to_all | solution.py:347
  101.1 0.7 copy.23
  101.8 2.2 %finish.1 = bf16[4,128,128]{2,1,0:T(8,128)(2,1)} custom-call(bf16[4,128,128]{2,1,0:T(8,128)(2,1)} %atoms.3, bf16[4,128,128]{2,1,0:T(8,128)(2,1)} %cotangent.3, f32[4,128,128]{2,1,0:T(8,128)} %copy-done.2, bf16[4,48,128]{2,1,0:T(8,128)(2,1)} %copy-done.8, bf16[4,48,128]{2,1,0:T(8,128)(2,1)} %copy-done.9, f32[1,128]{1,0:T(1,128)} %bitcast.57), custom_call_target="tpu_custom_call" | custom-call | tf_op jit(solution)/shard_map/finish/pallas_call | solution.py:348
  104.0 5.2 %all-to-all-done.3 = bf16[16,24,128]{2,1,0:T(8,128)(2,1)S(1)} async-done(((bf16[16,24,128]{2,1,0:T(8,128)(2,1)}), bf16[16,24,128]{2,1,0:T(8,128)(2,1)S(1)}, u32[]{:S(2)}, u32[]{:S(2)}) %all-to-all-start.3) | async-done | bytes 98336 | tf_op jit(solution)/shard_map/all_to_all | solution.py:347
  109.2 2.8 %collective-permute-start.5 = (bf16[384,128]{1,0:T(8,128)(2,1)S(1)}, bf16[384,128]{1,0:T(8,128)(2,1)S(1)}, u32[]{:S(2)}, u32[]{:S(2)}) collective-permute-start(bf16[384,128]{1,0:T(8,128)(2,1)S(1)} %bitcast.62), channel_id=1, source_target_pairs={{0,16},{16,0},{32,48},{48,32},{64,80},{80,64},{96,112},{112,96},{1... | collective-permute-start | bytes 294920 | tf_op jit(solution)/shard_map/ppermute | solution.py:356
  112.0 0.9 collective-permute-done.5
  114.7 0.7 copy.29
  (62 shorter events, 3.8 us)
Async XLA Ops:
  0.6 0.7 copy-start.12
  1.4 12.8 %copy-start.7 = (bf16[256,3,128]{2,0,1:T(8,128)(2,1)S(1)}, bf16[256,3,128]{2,0,1:T(8,128)(2,1)}, u32[]{:S(2)}) copy-start(bf16[256,3,128]{2,0,1:T(8,128)(2,1)} %param.15) | copy-start | bytes 589828
  2.3 4.0 %copy-start.13 = (pred[128]{0:T(512)(128)(4,1)S(1)}, pred[128]{0:T(512)(128)(4,1)}, u32[]{:S(2)}) copy-start(pred[128]{0:T(512)(128)(4,1)} %constant.45.clone.1) | copy-start | bytes 388
  2.3 17.1 %collective-permute-start = (bf16[5,48,128]{2,1,0:T(8,128)(2,1)S(1)}, bf16[5,48,128]{2,1,0:T(8,128)(2,1)S(1)}, u32[]{:S(2)}, u32[]{:S(2)}) collective-permute-start(bf16[5,48,128]{2,1,0:T(8,128)(2,1)S(1)} %pad_maximum_fusion), channel_id=1, source_target_pairs={{0,1},{1,2},{2,3},{3,4},{4,5},{5,6},{6,7},{7,8},{8,9},{9,10},{10,1... | collective-permute-start | bytes 184328 | tf_op jit(solution)/shard_map/ppermute | solution.py:271
  6.3 13.1 %collective-permute-start.1 = (bf16[5,48,128]{2,1,0:T(8,128)(2,1)S(1)}, bf16[5,48,128]{2,1,0:T(8,128)(2,1)S(1)}, u32[]{:S(2)}, u32[]{:S(2)}) collective-permute-start(bf16[5,48,128]{2,1,0:T(8,128)(2,1)S(1)} %pad_maximum_fusion.1), channel_id=1, source_target_pairs={{1,0},{2,1},{3,2},{4,3},{5,4},{6,5},{7,6},{8,7},{9,8},{10,9},{11,1... | collective-permute-start | bytes 184328 | tf_op jit(solution)/shard_map/ppermute | solution.py:272
  14.8 4.3 %copy-start.10 = (s32[4,2]{0,1:T(2,128)S(1)}, s32[4,2]{0,1:T(2,128)}, u32[]{:S(2)}) copy-start(s32[4,2]{0,1:T(2,128)} %param.19) | copy-start | bytes 100
  14.8 4.5 %copy-start.11 = (bf16[128,4]{0,1:T(4,128)(2,1)S(1)}, bf16[128,4]{0,1:T(4,128)(2,1)}, u32[]{:S(2)}) copy-start(bf16[128,4]{0,1:T(4,128)(2,1)} %param.17) | copy-start | bytes 3076
  14.8 14.0 %copy-start.1 = (bf16[4,128,128]{2,1,0:T(8,128)(2,1)S(1)}, bf16[4,128,128]{2,1,0:T(8,128)(2,1)}, u32[]{:S(2)}) copy-start(bf16[4,128,128]{2,1,0:T(8,128)(2,1)} %cotangent.3) | copy-start | bytes 393220
  14.8 14.0 %copy-start.3 = (bf16[128,512]{1,0:T(8,128)(2,1)S(1)}, bf16[128,512]{1,0:T(8,128)(2,1)}, u32[]{:S(2)}) copy-start(bf16[128,512]{1,0:T(8,128)(2,1)} %project.1) | copy-start | bytes 393220
  14.8 14.0 %copy-start.4 = (bf16[128,128]{1,0:T(8,128)(2,1)S(1)}, bf16[128,128]{1,0:T(8,128)(2,1)}, u32[]{:S(2)}) copy-start(bf16[128,128]{1,0:T(8,128)(2,1)} %combine.1) | copy-start | bytes 98308
  14.9 13.9 %all-to-all-start = ((bf16[16,3,16,128]{3,2,1,0:T(8,128)(2,1)}), bf16[16,3,16,128]{3,2,1,0:T(8,128)(2,1)S(1)}, u32[]{:S(2)}, u32[]{:S(2)}) async-start(bf16[16,3,16,128]{3,2,1,0:T(8,128)(2,1)} %bitcast.52), calls=%async_computation | async-start | bytes 393216 | tf_op jit(solution)/shard_map/all_to_all | solution.py:263
  19.2 9.7 %copy-start = (bf16[4,128,128]{2,1,0:T(8,128)(2,1)S(1)}, bf16[4,128,128]{2,1,0:T(8,128)(2,1)}, u32[]{:S(2)}) copy-start(bf16[4,128,128]{2,1,0:T(8,128)(2,1)} %atoms.3) | copy-start | bytes 393220
  28.8 0.7 copy-start.5
  28.8 0.7 copy-start.6
  44.5 0.7 copy-start.2
  45.2 3.8 %collective-permute-start.2 = (bf16[384,128]{1,0:T(8,128)(2,1)S(1)}, bf16[384,128]{1,0:T(8,128)(2,1)S(1)}, u32[]{:S(2)}, u32[]{:S(2)}) collective-permute-start(bf16[384,128]{1,0:T(8,128)(2,1)S(1)} %dynamic-slice_bitcast_fusion), channel_id=1, source_target_pairs={{0,16},{16,0},{32,48},{48,32},{64,80},{80,64},{96,112},{112,96},{1... | collective-permute-start | bytes 294920 | tf_op jit(solution)/shard_map/ppermute | solution.py:329
  63.2 29.8 %all-to-all-start.2 = ((bf16[16,24,128]{2,1,0:T(8,128)(2,1)}), bf16[16,24,128]{2,1,0:T(8,128)(2,1)S(1)}, u32[]{:S(2)}, u32[]{:S(2)}) async-start(bf16[16,24,128]{2,1,0:T(8,128)(2,1)} %broadcast_in_dim.22), calls=%async_computation.2 | async-start | bytes 196608 | tf_op jit(solution)/shard_map/all_to_all | solution.py:341
  78.6 14.5 %collective-permute-start.3 = (bf16[4,48,128]{2,1,0:T(8,128)(2,1)S(1)}, bf16[4,48,128]{2,1,0:T(8,128)(2,1)S(1)}, u32[]{:S(2)}, u32[]{:S(2)}) collective-permute-start(bf16[4,48,128]{2,1,0:T(8,128)(2,1)S(1)} %get-tuple-element.26), channel_id=1, source_target_pairs={{0,1},{1,2},{2,3},{3,4},{4,5},{5,6},{6,7},{7,8},{8,9},{9,10},{10,1... | collective-permute-start | bytes 147464 | tf_op jit(solution)/shard_map/ppermute | solution.py:342
  80.8 12.3 %collective-permute-start.4 = (bf16[4,48,128]{2,1,0:T(8,128)(2,1)S(1)}, bf16[4,48,128]{2,1,0:T(8,128)(2,1)S(1)}, u32[]{:S(2)}, u32[]{:S(2)}) collective-permute-start(bf16[4,48,128]{2,1,0:T(8,128)(2,1)S(1)} %get-tuple-element.27), channel_id=1, source_target_pairs={{1,0},{2,1},{3,2},{4,3},{5,4},{6,5},{7,6},{8,7},{9,8},{10,9},{11,1... | collective-permute-start | bytes 147464 | tf_op jit(solution)/shard_map/ppermute | solution.py:343
  93.1 0.7 copy-start.8
  93.1 0.7 copy-start.9
  93.8 15.4 %all-to-all-start.3 = ((bf16[16,24,128]{2,1,0:T(8,128)(2,1)}), bf16[16,24,128]{2,1,0:T(8,128)(2,1)S(1)}, u32[]{:S(2)}, u32[]{:S(2)}) async-start(bf16[16,24,128]{2,1,0:T(8,128)(2,1)} %broadcast_in_dim.23), calls=%async_computation.3 | async-start | bytes 196608 | tf_op jit(solution)/shard_map/all_to_all | solution.py:347
  109.2 3.7 %collective-permute-start.5 = (bf16[384,128]{1,0:T(8,128)(2,1)S(1)}, bf16[384,128]{1,0:T(8,128)(2,1)S(1)}, u32[]{:S(2)}, u32[]{:S(2)}) collective-permute-start(bf16[384,128]{1,0:T(8,128)(2,1)S(1)} %bitcast.62), channel_id=1, source_target_pairs={{0,16},{16,0},{32,48},{48,32},{64,80},{80,64},{96,112},{112,96},{1... | collective-permute-start | bytes 294920 | tf_op jit(solution)/shard_map/ppermute | solution.py:356

commit v3 on v2

v3 whole, which is shorter than its diff:
```python
import math

import jax
import jax.numpy as jnp
from jax import lax
from jax.experimental import pallas as pl
from jax.experimental.pallas import tpu as pltpu
from jax.sharding import PartitionSpec as P

QW = 32
KW = 128
RIM = 48
EPSILON = 1e-05
NEG_FILL = -1e30
F32 = jnp.float32
BF = jnp.bfloat16


def nn(a, b):
    return lax.dot_general(a, b, (((1,), (0,)), ((), ())), preferred_element_type=F32)


def nt(a, b):
    return lax.dot_general(a, b, (((1,), (1,)), ((), ())), preferred_element_type=F32)


def tn(a, b):
    return lax.dot_general(a, b, (((0,), (0,)), ((), ())), preferred_element_type=F32)


def split2(x):
    high = x.astype(BF)
    return high, (x - high.astype(F32)).astype(BF)


def norm(v):
    mean = jnp.mean(v, axis=-1, keepdims=True)
    centred = v - mean
    inv = lax.rsqrt(jnp.mean(centred * centred, axis=-1, keepdims=True) + EPSILON)
    return centred * inv, inv


def norm_back(g, hat, inv):
    first = jnp.mean(g, axis=-1, keepdims=True)
    second = jnp.mean(g * hat, axis=-1, keepdims=True)
    return inv * (g - first - hat * second)


def iota(shape, dim):
    return lax.broadcasted_iota(jnp.int32, shape, dim)


def pack_kernel(atoms, tokens, to_before, to_after):
    samples, count, width = atoms.shape
    to_before[:samples] = atoms[:, :RIM]
    to_after[:samples] = atoms[:, count - RIM :]
    line = tokens[...].astype(F32)
    to_before[samples] = jnp.broadcast_to(line, (RIM, width)).astype(BF)
    to_after[samples] = jnp.broadcast_to(line, (RIM, width)).astype(BF)


def pair_kernel(band, pair_gain, weight_rows, table, z_hat, pair_inv):
    heads = 4
    entries = band.shape[0]
    hat, inv = norm(band[...].astype(F32))
    z_hat[...] = hat
    pair_inv[...] = inv
    pair_norm = (hat * pair_gain[...]).astype(BF)
    bias_rows = nt(weight_rows[...], pair_norm)
    stacked = jnp.concatenate(
        [jnp.broadcast_to(bias_rows[h : h + 1], (16, entries)) for h in range(heads)], axis=0
    )
    own_token = (iota((64, entries), 0) & 15) == (iota((64, entries), 1) & 15)
    high, low = split2(jnp.where(own_token, stacked, 0.0))
    spread = (iota((entries, KW), 0) >> 4) == iota((entries, KW), 1)
    spread = jnp.where(spread, 1.0, 0.0).astype(BF)
    table[...] = nn(jnp.concatenate([high, low], axis=0), spread).astype(BF)


def attention_kernel(
    key_range,
    device,
    atoms,
    cotangent,
    before,
    after,
    project,
    combine,
    atom_gain,
    table,
    z_hat,
    pair_inv,
    pair_gain,
    weight_rows,
    tokens,
    outgoing,
    to_before,
    to_after,
    own_grad,
    bias,
    bias_grad,
):
    samples, count, width = atoms.shape
    heads = 4
    windows = count // QW
    entries = z_hat.shape[0]
    scale = 1.0 / math.sqrt(width // heads)
    gain = atom_gain[...]

    lane = iota((KW, KW), 1)
    line = iota((KW, KW), 0)

    own = jnp.broadcast_to(tokens[...].astype(F32), (8, KW))
    left = before[samples][:16].astype(F32)[:8] - 16.0
    right = after[samples][:16].astype(F32)[:8] + 16.0
    row_lane = iota((8, KW), 1)
    turned = [own] + [pltpu.roll(own, h * QW, 1) for h in range(1, heads)]

    def query_row(w):
        row = turned[(-w) % heads]
        for h in range(1, heads):
            row = jnp.where((row_lane >> 5) == h, turned[(h - w) % heads], row)
        return row.astype(jnp.int32)[:1]

    def key_row(w):
        shift = RIM - w * QW
        first, second = (left, own) if shift > 0 else (own, right)
        shift = shift % KW
        row = jnp.where(row_lane < shift, pltpu.roll(first, shift, 1), pltpu.roll(second, shift, 1))
        return row.astype(jnp.int32)[:1] + 16

    def query_hot(w):
        hit = ((line & 15) == query_row(w)) & (((line >> 4) & 3) == (lane >> 5))
        return jnp.where(hit, 1.0, 0.0).astype(BF)

    def key_hot(w):
        return jnp.where(line == key_row(w), 1.0, 0.0).astype(BF)

    for w in range(windows):
        by_key = nn(table[...], key_hot(w)).astype(BF)
        values = tn(by_key, query_hot(w))
        first = device[0] * count - RIM + w * QW
        allowed = (line >= key_range[w, 0] - first) & (line < key_range[w, 1] - first)
        bias[w] = jnp.where(allowed, values, NEG_FILL)
        bias_grad[w] = jnp.zeros((KW, KW), F32)
    diag = jnp.where((line >> 5) == (lane >> 5), 1.0, 0.0).astype(BF)
    head_of = iota((QW, width), 1) >> 5

    def spread_heads(x):
        return jnp.concatenate([x] * heads, axis=0) * diag

    def gather_heads(x):
        total = x[:QW]
        for h in range(1, heads):
            total = jnp.where(head_of == h, x[h * QW : (h + 1) * QW], total)
        return total

    def overlap(parts):
        sums = []
        for m in range(windows + KW // QW - 1):
            total = None
            for w in range(windows):
                if 0 <= m - w < KW // QW:
                    term = parts[w][(m - w) * QW : (m - w + 1) * QW]
                    total = term if total is None else total + term
            sums.append(total)
        return jnp.concatenate(sums, axis=0).astype(BF)

    def sample(s, carry):
        project_sum, combine_sum, scale_sum = carry
        x = jnp.concatenate([before[s], atoms[s], after[s]], axis=0).astype(F32)
        x_hat, _ = norm(x)
        normed = (x_hat * gain).astype(BF)
        projected = nn(normed, project[...]).astype(BF)
        query = projected[RIM : RIM + count, :width]
        key = projected[:, width : 2 * width]
        value = projected[:, 2 * width : 3 * width]
        gate = projected[RIM : RIM + count, 3 * width :].astype(F32)
        out = cotangent[s]
        sigmoid = jax.nn.sigmoid(gate)
        gated_grad = nt(out, combine[...]).astype(BF).astype(F32)
        mixture_grad = (gated_grad * sigmoid).astype(BF)
        span = range(windows)
        q = [spread_heads(query[w * QW : (w + 1) * QW]) for w in span]
        g = [spread_heads(mixture_grad[w * QW : (w + 1) * QW]) for w in span]
        k = [key[w * QW : w * QW + KW] for w in span]
        v = [value[w * QW : w * QW + KW] for w in span]
        scores = [nt(k[w], q[w]) * scale + bias[w] for w in span]
        weights_grad = [nt(v[w], g[w]).astype(BF).astype(F32) for w in span]
        scores = [jnp.exp(x - jnp.max(x, axis=0, keepdims=True)) for x in scores]
        weights = [x * (1.0 / jnp.sum(x, axis=0, keepdims=True)) for x in scores]
        low = [x.astype(BF) for x in weights]
        mixture = jnp.concatenate([gather_heads(tn(low[w], v[w])) for w in span], axis=0)
        row_dot = [jnp.sum(weights[w] * weights_grad[w], axis=0, keepdims=True) for w in span]
        score_grad = [weights[w] * (weights_grad[w] - row_dot[w]) for w in span]
        for w in span:
            bias_grad[w] += score_grad[w]
        score_low = [(x * scale).astype(BF) for x in score_grad]
        query_grads = [gather_heads(tn(score_low[w], k[w])).astype(BF) for w in span]
        key_grad = overlap([nn(score_low[w], q[w]) for w in span])
        value_grad = overlap([nn(low[w], g[w]) for w in span])
        gated = (mixture * sigmoid).astype(BF)
        combine_sum = combine_sum + tn(gated, out)
        gate_grad = (gated_grad * mixture * sigmoid * (1.0 - sigmoid)).astype(BF)
        rim = jnp.zeros((RIM, width), BF)
        query_cols = jnp.concatenate([rim] + query_grads + [rim], axis=0)
        gate_cols = jnp.concatenate([rim, gate_grad, rim], axis=0)
        grad = jnp.concatenate([query_cols, key_grad, value_grad, gate_cols], axis=1)
        project_sum = project_sum + tn(normed, grad)
        normed_grad = nt(grad, project[...])
        scale_sum = scale_sum + jnp.sum(normed_grad * x_hat, axis=0, keepdims=True)
        to_before[s] = normed_grad[:RIM].astype(BF)
        to_after[s] = normed_grad[RIM + count :].astype(BF)
        own_grad[s] = normed_grad[RIM : RIM + count]
        return project_sum, combine_sum, scale_sum

    start = (
        jnp.zeros((width, 4 * width), F32),
        jnp.zeros((width, width), F32),
        jnp.zeros((1, width), F32),
    )
    project_sum, combine_sum, scale_sum = lax.fori_loop(0, samples, sample, start, unroll=True)

    table_grad = jnp.zeros((KW, KW), F32)
    for w in range(windows):
        high, low = split2(bias_grad[w])
        hot = key_hot(w)
        by_slot = nn(hot, high) + nn(hot, low)
        high, low = split2(by_slot)
        rows = query_hot(w)
        table_grad = table_grad + nt(high, rows) + nt(low, rows)
    spread = (iota((entries, KW), 0) >> 4) == iota((entries, KW), 1)
    spread = jnp.where(spread, 1.0, 0.0).astype(BF)
    entry_grad = nn(spread, table_grad.astype(BF))
    shown = (iota((entries, KW), 0) & 15) == (iota((entries, KW), 1) & 15)
    shown = shown & (iota((entries, KW), 1) < 64)
    entry_grad = jnp.where(shown, entry_grad, 0.0).astype(BF)
    weight_of = jnp.concatenate(
        [jnp.broadcast_to(weight_rows[h : h + 1, :], (16, width)) for h in range(heads)] * 2, axis=0
    )
    hat = z_hat[...]
    pair_norm = (hat * pair_gain[...]).astype(BF)
    norm_grad = nn(entry_grad, weight_of).astype(BF).astype(F32)
    weight_part = tn(entry_grad, pair_norm)
    tail = [
        jnp.sum(weight_part[h * 16 : (h + 1) * 16], axis=0, keepdims=True) for h in range(heads)
    ]
    tail = tail + [scale_sum, jnp.sum(norm_grad * hat, axis=0, keepdims=True)]
    tail = tail + [jnp.zeros((10, width), F32)]
    band_part = norm_back(norm_grad * pair_gain[...], hat, pair_inv[...]).astype(BF)
    sums = jnp.concatenate(
        [project_sum[:, part * width : (part + 1) * width] for part in range(4)]
        + [combine_sum]
        + tail
        + [jnp.zeros((entries - 5 * width - 16, width), F32)],
        axis=0,
    ).astype(BF)
    part = entries // 16
    for c in range(16):
        outgoing[c, :part, :] = band_part[c * part : (c + 1) * part]
        outgoing[c, part:, :] = sums[c * part : (c + 1) * part]


def last_kernel(parts, project_grad, combine_grad, weight_grad, scale_grad, gain_grad):
    rows = jnp.concatenate([parts[c] for c in range(parts.shape[0])], axis=0)
    width = rows.shape[1]
    for part in range(4):
        project_grad[:, part * width : (part + 1) * width] = rows[part * width : (part + 1) * width]
    combine_grad[...] = rows[4 * width : 5 * width]
    tail = rows[5 * width : 5 * width + 16].astype(F32)
    weight_grad[...] = tail[:4].astype(BF)
    scale_grad[...] = tail[4:5]
    gain_grad[...] = tail[5:6]


def finish_kernel(atoms, cotangent, own_grad, from_before, from_after, atom_gain, result):
    samples, count, width = atoms.shape
    gain = atom_gain[...]
    for s in range(samples):
        x_hat, inv = norm(atoms[s].astype(F32))
        rim = jnp.zeros((count - RIM, width), F32)
        total = own_grad[s] + jnp.concatenate([from_before[s].astype(F32), rim], axis=0)
        total = total + jnp.concatenate([rim, from_after[s].astype(F32)], axis=0)
        g = total.astype(BF).astype(F32) * gain
        result[s] = (cotangent[s].astype(F32) + norm_back(g, x_hat, inv)).astype(BF)


def vmem(n):
    return [pl.BlockSpec(memory_space=pltpu.VMEM)] * n


def shards(
    atoms,
    cotangent,
    project,
    combine,
    atom_gain,
    pair_band,
    pair_gain,
    pair_weight,
    atom_token,
    key_range,
):
    samples, count, width = atoms.shape
    heads = pair_weight.shape[1]
    rows, cols = lax.axis_size("row"), lax.axis_size("col")
    peers = rows * cols
    device = lax.axis_index(("row", "col"))
    windows = count // QW
    block = pair_band.shape[0] // cols
    keys = pair_band.shape[1]
    up = [(i, i + 1) for i in range(peers - 1)]
    down = [(i + 1, i) for i in range(peers - 1)]

    shape = jax.ShapeDtypeStruct

    tiles = jnp.transpose(pair_band.reshape(cols, block, keys, width), (0, 2, 1, 3))
    tiles = lax.all_to_all(tiles, "col", 0, 0, tiled=True).reshape(cols * keys * block, width)

    local = atom_token - device * block
    to_before, to_after = pl.pallas_call(
        pack_kernel,
        out_shape=(shape((samples + 1, RIM, width), BF),) * 2,
        in_specs=vmem(2),
        out_specs=tuple(vmem(2)),
        name="pack",
    )(atoms, local.reshape(1, count))
    before = lax.ppermute(to_after, ("row", "col"), up)
    after = lax.ppermute(to_before, ("row", "col"), down)
    weight_rows = jnp.pad(pair_weight.T, ((0, 16 - heads), (0, 0)))
    gain = atom_gain.reshape(1, width)
    entries = tiles.shape[0]
    table, z_hat, pair_inv = pl.pallas_call(
        pair_kernel,
        out_shape=(
            shape((KW, KW), BF),
            shape((entries, width), F32),
            shape((entries, 1), F32),
        ),
        in_specs=vmem(3),
        out_specs=tuple(vmem(3)),
        cost_estimate=pl.CostEstimate(flops=10**9, bytes_accessed=10**7, transcendentals=0),
        name="pair",
    )(tiles, pair_gain.reshape(1, width), weight_rows)
    outgoing, to_before, to_after, own_grad = pl.pallas_call(
        attention_kernel,
        out_shape=(
            shape((cols, 2 * keys * block, width), BF),
            shape((samples, RIM, width), BF),
            shape((samples, RIM, width), BF),
            shape((samples, count, width), F32),
        ),
        in_specs=[pl.BlockSpec(memory_space=pltpu.SMEM)] * 2 + vmem(13),
        out_specs=tuple(vmem(4)),
        scratch_shapes=[
            pltpu.VMEM((windows, KW, KW), F32),
            pltpu.VMEM((windows, KW, KW), F32),
        ],
        compiler_params=pltpu.CompilerParams(vmem_limit_bytes=32 * 1024 * 1024),
        name="attention",
    )(
        key_range,
        device.astype(jnp.int32).reshape(1),
        atoms,
        cotangent,
        before,
        after,
        project,
        combine,
        gain,
        table,
        z_hat,
        pair_inv,
        pair_gain.reshape(1, width),
        weight_rows,
        local.reshape(1, count),
    )

    line = keys * block
    chunk = outgoing.shape[1] - line
    scattered = lax.all_to_all(outgoing, "col", 0, 0, tiled=True)
    band_grad = scattered[:, :line].reshape(cols, keys, block, width)
    band_grad = jnp.transpose(band_grad, (0, 2, 1, 3)).reshape(pair_band.shape)
    part = jnp.sum(scattered[:, line:].astype(F32), axis=0).astype(BF)

    def summed(x, groups):
        x = jnp.broadcast_to(x, (len(groups[0]), chunk, width))
        x = lax.all_to_all(x, "row", 0, 0, axis_index_groups=groups, tiled=True)
        return jnp.sum(x.astype(F32), axis=0).astype(BF)

    near = [
        [y * 8 + z * 2 + core for y in range(rows // 8) for core in range(2)] for z in range(4)
    ]
    far = [
        [y * 8 + z * 2 + core for z in range(4)] for y in range(rows // 8) for core in range(2)
    ]
    part = summed(part, near)

    part, to_before, to_after = lax.optimization_barrier((part, to_before, to_after))
    part = summed(part, far)
    from_before = lax.ppermute(to_after, ("row", "col"), up)
    from_after = lax.ppermute(to_before, ("row", "col"), down)
    part, from_before, from_after = lax.optimization_barrier((part, from_before, from_after))
    part = jnp.broadcast_to(part, (cols, chunk, width))
    part = lax.all_to_all(part, "col", 0, 0, tiled=True)
    atoms_grad = pl.pallas_call(
        finish_kernel,
        out_shape=shape(atoms.shape, BF),
        in_specs=vmem(6),
        out_specs=pl.BlockSpec(memory_space=pltpu.VMEM),
        name="finish",
    )(atoms, cotangent, own_grad, from_before, from_after, gain)
    part, atoms_grad, band_grad = lax.optimization_barrier((part, atoms_grad, band_grad))
    project_grad, combine_grad, weight_grad, scale_grad, gain_grad = pl.pallas_call(
        last_kernel,
        out_shape=(
            shape(project.shape, BF),
            shape(combine.shape, BF),
            shape((heads, width), BF),
            shape((1, width), F32),
            shape((1, width), F32),
        ),
        in_specs=vmem(1),
        out_specs=tuple(vmem(5)),
        name="last",
    )(part)
    return (
        atoms_grad,
        project_grad,
        combine_grad,
        scale_grad.reshape(width),
        band_grad,
        weight_grad.T,
        gain_grad.reshape(width),
    )


def solution(mesh):
    in_specs = (
        P(None, ("row", "col"), None),
        P(None, ("row", "col"), None),
        P(),
        P(),
        P(),
        P("row", "col", None),
        P(),
        P(),
        P(("row", "col")),
        P(("row", "col"), None),
    )
    out_specs = (P(None, ("row", "col"), None), P(), P(), P(), P("row", "col", None), P(), P())
    return jax.shard_map(shards, mesh=mesh, in_specs=in_specs, out_specs=out_specs, check_vma=False)
```

time: 116 us -> 110 us (0.948)
  blocking collectives: 13.4 us -> 29.5 us
  waiting for transfers between devices: 21.1 us -> 7.54 us
  starting transfers between devices: 53.9 us -> 47.1 us
  Pallas kernels: 17.2 us -> 12.8 us
  local copies, waits for them, and re-layouts: 7.84 us -> 10.4 us
    all_to_all x0 -> x1, blocking collectives: none -> 10.6 us  [summed(): x = lax.all_to_all(x, 'row', 0, 0, axis_index_groups=groups, tiled=True)]
    all_to_all x1, waiting for transfers between devices: 9.17 us -> 0.01 us  [shards(): lax.all_to_all(tiles, 'col', 0, 0, tiled=True)]
    ppermute x4 -> x2, starting transfers between devices: 17.4 us -> 10.7 us  [the longest x1 7.36 us: shards(): after = lax.ppermute(to_before, ('row', 'col'), down)]
    all_to_all x1, blocking collectives: 13.4 us -> 18.9 us  [shards(): scattered = lax.all_to_all(outgoing, 'col', 0, 0, tiled=True)]
    all_to_all x2, starting transfers between devices: 22.7 us -> 17.9 us  [the longest x1 9.38 us: shards(): part = lax.all_to_all(part, 'col', 0, 0, tiled=True)]
    all_to_all x1, starting transfers between devices: 4.29 us -> 9.01 us  [shards(): lax.all_to_all(tiles, 'col', 0, 0, tiled=True)]
    pallas_call x1 -> x4, Pallas kernels: 15 us -> 10.6 us  [the longest x1 5.24 us: shards(): pl.pallas_call(attention_kernel, out_shape=(shape((cols, 2 * keys * block...]
    unnamed x29 -> x39, local copies, waits for them, and re-layouts: 2.11 us -> 6.18 us
  transfers between devices with their start and end apart: 9 -> 7, of which waited for: 5 -> 2; matrix products, arithmetic and copies ran while one was open for 2% -> 2% of each run, Pallas kernels for 2% -> 5%
where the time goes in v3:
time: 110 us; the launch traced here: 109 us
  starting transfers between devices  47.1 us (43%)
  blocking collectives  29.5 us (27%)
  Pallas kernels  12.8 us (12%)
  local copies, waits for them, and re-layouts  10.4 us (9%)
  waiting for transfers between devices  7.54 us (7%)
    all_to_all x1, blocking collectives, shards(): scattered = lax.all_to_all(outgoing, 'col', 0, 0, tiled=True)  18.9 us
    all_to_all x1, blocking collectives, summed(): x = lax.all_to_all(x, 'row', 0, 0, axis_index_groups=groups, tiled=True)  10.6 us
    all_to_all x1, starting transfers between devices, shards(): part = lax.all_to_all(part, 'col', 0, 0, tiled=True)  9.38 us
    all_to_all x1, starting transfers between devices, shards(): lax.all_to_all(tiles, 'col', 0, 0, tiled=True)  9.01 us
    all_to_all x1, starting transfers between devices, summed(): x = lax.all_to_all(x, 'row', 0, 0, axis_index_groups=groups, tiled=True)  8.52 us
    ppermute x1, starting transfers between devices, shards(): from_after = lax.ppermute(to_before, ('row', 'col'), down)  7.5 us
    ppermute x1, starting transfers between devices, shards(): after = lax.ppermute(to_before, ('row', 'col'), down)  7.36 us
    unnamed x39, local copies, waits for them, and re-layouts  6.18 us
  transfers between devices with their start and end apart: 7, of which 2 were waited for; matrix products, arithmetic and copies ran while one was open for 2% of the time, Pallas kernels for 5%

profile of v3, /device:TPU:1, one launch (start us, length us, event | category | flops | bytes accessed | tf_op | source)
XLA Modules:
  0.0 108.9 jit_solution(17162971993160231328)
XLA Ops:
  0.6 1.6 %copy.24 = bf16[16,16,3,128]{3,1,2,0:T(8,128)(2,1)} copy(bf16[16,16,3,128]{3,1,0,2:T(8,128)(2,1)} %bitcast.23) | data formatting | bytes 393216 | tf_op jit(solution)/shard_map/reshape | solution.py:317
  2.2 9.0 %all-to-all-start = ((bf16[16,3,16,128]{3,2,1,0:T(8,128)(2,1)}), bf16[16,3,16,128]{3,2,1,0:T(8,128)(2,1)S(1)}, u32[]{:S(2)}, u32[]{:S(2)}) async-start(bf16[16,3,16,128]{3,2,1,0:T(8,128)(2,1)} %bitcast.17), calls=%async_computation | async-start | bytes 393216 | tf_op jit(solution)/shard_map/all_to_all | solution.py:318
  12.4 1.6 %pack.1 = (bf16[5,48,128]{2,1,0:T(8,128)(2,1)}, bf16[5,48,128]{2,1,0:T(8,128)(2,1)}) custom-call(bf16[4,128,128]{2,1,0:T(8,128)(2,1)} %atoms.5, s32[1,128]{1,0:T(1,128)} %subtract_bitcast_fusion.tokens), custom_call_target="tpu_custom_call" | custom-call | tf_op jit(solution)/shard_map/pack/pallas_call | solution.py:321
  14.0 3.4 %collective-permute-start = (bf16[5,48,128]{2,1,0:T(8,128)(2,1)}, bf16[5,48,128]{2,1,0:T(8,128)(2,1)S(1)}, u32[]{:S(2)}, u32[]{:S(2)}) collective-permute-start(bf16[5,48,128]{2,1,0:T(8,128)(2,1)} %get-tuple-element.30), channel_id=1, source_target_pairs={{0,1},{1,2},{2,3},{3,4},{4,5},{5,6},{6,7},{7,8},{8,9},{9,10},{10,1... | collective-permute-start | bytes 184328 | tf_op jit(solution)/shard_map/ppermute | solution.py:328
  17.4 7.4 %collective-permute-start.1 = (bf16[5,48,128]{2,1,0:T(8,128)(2,1)}, bf16[5,48,128]{2,1,0:T(8,128)(2,1)S(1)}, u32[]{:S(2)}, u32[]{:S(2)}) collective-permute-start(bf16[5,48,128]{2,1,0:T(8,128)(2,1)} %get-tuple-element.31), channel_id=1, source_target_pairs={{1,0},{2,1},{3,2},{4,3},{5,4},{6,5},{7,6},{8,7},{9,8},{10,9},{11,1... | collective-permute-start | bytes 184328 | tf_op jit(solution)/shard_map/ppermute | solution.py:329
  24.9 0.7 copy-done.17
  26.1 0.7 copy-done.13
  26.8 2.2 %pair.1 = (bf16[128,128]{1,0:T(8,128)(2,1)}, f32[768,128]{1,0:T(8,128)}, f32[768,1]{1,0:T(8,128)}) custom-call(bf16[768,128]{1,0:T(8,128)(2,1)} %bitcast.24, f32[1,128]{1,0:T(1,128)} %bitcast.20, bf16[16,128]{1,0:T(8,128)(2,1)} %pad.4.weight_rows), custom_call_target="tpu_custom_call" | custom-call | flops 1000000000 | bytes 10000000 | tf_op jit(solution)/shard_map/pair/pallas_call | solution.py:333
  29.7 1.0 copy-done.2
  30.7 1.0 copy-done.3
  31.7 0.8 copy-done.7
  32.5 5.2 %attention.1 = (bf16[16,96,128]{2,1,0:T(8,128)(2,1)S(1)}, bf16[4,48,128]{2,1,0:T(8,128)(2,1)S(1)}, bf16[4,48,128]{2,1,0:T(8,128)(2,1)S(1)}, f32[4,128,128]{2,1,0:T(8,128)S(1)}) custom-call(s32[4,2]{1,0:T(4,128)S(1)} %copy.21.key_range, s32[1]{0:T(128)} %bitcast.device, bf16[4,128,128]{2,1,0:T(8,128)(2,1)S(1)} %copy-done, bf16[4,128,128]{2,1,0:T(8,128)(2,1)S(1)} %copy-done.1, ...), custom_call_target="tpu_custom_call" | custom-call | tf_op jit(solution)/shard_map/attention/pallas_call | solution.py:345
  37.7 18.9 %all_to_all.25 = bf16[16,96,128]{2,1,0:T(8,128)(2,1)S(1)} all-to-all(bf16[16,96,128]{2,1,0:T(8,128)(2,1)S(1)} %get-tuple-element.35), channel_id=1, replica_groups=mesh['row'=32,'col'=16] {'col'}, dimensions={0} | all-to-all | bytes 786432 | tf_op jit(solution)/shard_map/all_to_all | solution.py:381
  56.7 10.6 %all_to_all.26 = bf16[8,48,128]{2,1,0:T(8,128)(2,1)S(1)} all-to-all(bf16[8,48,128]{2,1,0:T(8,128)(2,1)S(1)} %broadcast_in_dim.9), channel_id=1, replica_groups={{0,16,128,144,256,272,384,400},{32,48,160,176,288,304,416,432},{64,80,1..., dimensions={0} | all-to-all | bytes 196608 | tf_op jit(solution)/shard_map/all_to_all | solution.py:388
  68.0 8.5 %all-to-all-start.3 = ((bf16[4,48,128]{2,1,0:T(8,128)(2,1)}), bf16[4,48,128]{2,1,0:T(8,128)(2,1)S(1)}, u32[]{:S(2)}, u32[]{:S(2)}) async-start(bf16[4,48,128]{2,1,0:T(8,128)(2,1)} %broadcast_in_dim.10), calls=%async_computation.3 | async-start | bytes 98304 | tf_op jit(solution)/shard_map/all_to_all | solution.py:388
  76.5 2.0 %collective-permute-start.2 = (bf16[4,48,128]{2,1,0:T(8,128)(2,1)S(1)}, bf16[4,48,128]{2,1,0:T(8,128)(2,1)S(1)}, u32[]{:S(2)}, u32[]{:S(2)}) collective-permute-start(bf16[4,48,128]{2,1,0:T(8,128)(2,1)S(1)} %get-tuple-element.39), channel_id=1, source_target_pairs={{0,1},{1,2},{2,3},{3,4},{4,5},{5,6},{6,7},{7,8},{8,9},{9,10},{10,1... | collective-permute-start | bytes 147464 | tf_op jit(solution)/shard_map/ppermute | solution.py:401
  78.5 7.5 %collective-permute-start.3 = (bf16[4,48,128]{2,1,0:T(8,128)(2,1)S(1)}, bf16[4,48,128]{2,1,0:T(8,128)(2,1)S(1)}, u32[]{:S(2)}, u32[]{:S(2)}) collective-permute-start(bf16[4,48,128]{2,1,0:T(8,128)(2,1)S(1)} %get-tuple-element.40), channel_id=1, source_target_pairs={{1,0},{2,1},{3,2},{4,3},{5,4},{6,5},{7,6},{8,7},{9,8},{10,9},{11,1... | collective-permute-start | bytes 147464 | tf_op jit(solution)/shard_map/ppermute | solution.py:402
  86.0 2.1 %all-to-all-done.3 = bf16[4,48,128]{2,1,0:T(8,128)(2,1)S(1)} async-done(((bf16[4,48,128]{2,1,0:T(8,128)(2,1)}), bf16[4,48,128]{2,1,0:T(8,128)(2,1)S(1)}, u32[]{:S(2)}, u32[]{:S(2)}) %all-to-all-start.3) | async-done | bytes 49184 | tf_op jit(solution)/shard_map/all_to_all | solution.py:388
  88.2 0.7 broadcast_in_dim.11
  88.9 9.4 %all-to-all-start.4 = ((bf16[16,48,128]{2,1,0:T(8,128)(2,1)}), bf16[16,48,128]{2,1,0:T(8,128)(2,1)S(1)}, u32[]{:S(2)}, u32[]{:S(2)}) async-start(bf16[16,48,128]{2,1,0:T(8,128)(2,1)} %broadcast_in_dim.11), calls=%async_computation.4 | async-start | bytes 393216 | tf_op jit(solution)/shard_map/all_to_all | solution.py:405
  98.3 0.7 copy.22
  99.0 2.2 %finish.1 = bf16[4,128,128]{2,1,0:T(8,128)(2,1)} custom-call(bf16[4,128,128]{2,1,0:T(8,128)(2,1)} %atoms.5, bf16[4,128,128]{2,1,0:T(8,128)(2,1)} %cotangent.3, f32[4,128,128]{2,1,0:T(8,128)} %copy-done.4, bf16[4,48,128]{2,1,0:T(8,128)(2,1)} %copy-done.14, bf16[4,48,128]{2,1,0:T(8,128)(2,1)} %copy-done.15, f32[1,128]{1,0:T(1,128)} %bitcast.18), custom_call_target="tpu_custom_call" | custom-call | tf_op jit(solution)/shard_map/finish/pallas_call | solution.py:406
  101.2 5.4 %all-to-all-done.4.parts = bf16[16,48,128]{2,1,0:T(8,128)(2,1)S(1)} async-done(((bf16[16,48,128]{2,1,0:T(8,128)(2,1)}), bf16[16,48,128]{2,1,0:T(8,128)(2,1)S(1)}, u32[]{:S(2)}, u32[]{:S(2)}) %all-to-all-start.4) | async-done | bytes 196640 | tf_op jit(solution)/shard_map/all_to_all | solution.py:405
  107.3 1.6 %last.1 = (bf16[128,512]{1,0:T(8,128)(2,1)}, bf16[128,128]{1,0:T(8,128)(2,1)}, bf16[4,128]{1,0:T(4,128)(2,1)}, f32[1,128]{1,0:T(1,128)}, f32[1,128]{1,0:T(1,128)}) custom-call(bf16[16,48,128]{2,1,0:T(8,128)(2,1)} %copy-done.12), custom_call_target="tpu_custom_call" | custom-call | tf_op jit(solution)/shard_map/last/pallas_call | solution.py:414
  (46 shorter events, 3.9 us)
Async XLA Ops:
  2.2 23.9 %all-to-all-start = ((bf16[16,3,16,128]{3,2,1,0:T(8,128)(2,1)}), bf16[16,3,16,128]{3,2,1,0:T(8,128)(2,1)S(1)}, u32[]{:S(2)}, u32[]{:S(2)}) async-start(bf16[16,3,16,128]{3,2,1,0:T(8,128)(2,1)} %bitcast.17), calls=%async_computation | async-start | bytes 393216 | tf_op jit(solution)/shard_map/all_to_all | solution.py:318
  14.0 10.8 %copy-start.16 = (s32[4,2]{0,1:T(2,128)S(1)}, s32[4,2]{0,1:T(2,128)}, u32[]{:S(2)}) copy-start(s32[4,2]{0,1:T(2,128)} %param.19) | copy-start | bytes 100
  14.0 15.0 %collective-permute-start = (bf16[5,48,128]{2,1,0:T(8,128)(2,1)}, bf16[5,48,128]{2,1,0:T(8,128)(2,1)S(1)}, u32[]{:S(2)}, u32[]{:S(2)}) collective-permute-start(bf16[5,48,128]{2,1,0:T(8,128)(2,1)} %get-tuple-element.30), channel_id=1, source_target_pairs={{0,1},{1,2},{2,3},{3,4},{4,5},{5,6},{6,7},{7,8},{8,9},{9,10},{10,1... | collective-permute-start | bytes 184328 | tf_op jit(solution)/shard_map/ppermute | solution.py:328
  17.4 11.6 %collective-permute-start.1 = (bf16[5,48,128]{2,1,0:T(8,128)(2,1)}, bf16[5,48,128]{2,1,0:T(8,128)(2,1)S(1)}, u32[]{:S(2)}, u32[]{:S(2)}) collective-permute-start(bf16[5,48,128]{2,1,0:T(8,128)(2,1)} %get-tuple-element.31), channel_id=1, source_target_pairs={{1,0},{2,1},{3,2},{4,3},{5,4},{6,5},{7,6},{8,7},{9,8},{10,9},{11,1... | collective-permute-start | bytes 184328 | tf_op jit(solution)/shard_map/ppermute | solution.py:329
  24.9 0.7 copy-start.17
  26.1 0.7 copy-start.13
  26.8 2.3 %copy-start = (bf16[4,128,128]{2,1,0:T(8,128)(2,1)S(1)}, bf16[4,128,128]{2,1,0:T(8,128)(2,1)}, u32[]{:S(2)}) copy-start(bf16[4,128,128]{2,1,0:T(8,128)(2,1)} %atoms.5) | copy-start | bytes 393220
  26.8 2.3 %copy-start.1 = (bf16[4,128,128]{2,1,0:T(8,128)(2,1)S(1)}, bf16[4,128,128]{2,1,0:T(8,128)(2,1)}, u32[]{:S(2)}) copy-start(bf16[4,128,128]{2,1,0:T(8,128)(2,1)} %cotangent.3) | copy-start | bytes 393220
  26.8 2.3 %copy-start.5 = (bf16[128,512]{1,0:T(8,128)(2,1)S(1)}, bf16[128,512]{1,0:T(8,128)(2,1)}, u32[]{:S(2)}) copy-start(bf16[128,512]{1,0:T(8,128)(2,1)} %project.1) | copy-start | bytes 393220
  26.8 2.3 %copy-start.6 = (bf16[128,128]{1,0:T(8,128)(2,1)S(1)}, bf16[128,128]{1,0:T(8,128)(2,1)}, u32[]{:S(2)}) copy-start(bf16[128,128]{1,0:T(8,128)(2,1)} %combine.1) | copy-start | bytes 98308
  29.0 0.7 copy-start.8
  29.0 0.7 copy-start.9
  29.1 0.7 copy-start.11
  29.7 1.0 copy-start.2
  30.7 1.0 copy-start.3
  31.7 0.8 copy-start.7
  37.7 18.9 %copy-start.4 = (f32[4,128,128]{2,1,0:T(8,128)}, f32[4,128,128]{2,1,0:T(8,128)S(1)}, u32[]{:S(2)}) copy-start(f32[4,128,128]{2,1,0:T(8,128)S(1)} %get-tuple-element.42.own_grad) | copy-start | bytes 786436
  68.0 20.1 %all-to-all-start.3 = ((bf16[4,48,128]{2,1,0:T(8,128)(2,1)}), bf16[4,48,128]{2,1,0:T(8,128)(2,1)S(1)}, u32[]{:S(2)}, u32[]{:S(2)}) async-start(bf16[4,48,128]{2,1,0:T(8,128)(2,1)} %broadcast_in_dim.10), calls=%async_computation.3 | async-start | bytes 98304 | tf_op jit(solution)/shard_map/all_to_all | solution.py:388
  76.5 11.6 %collective-permute-start.2 = (bf16[4,48,128]{2,1,0:T(8,128)(2,1)S(1)}, bf16[4,48,128]{2,1,0:T(8,128)(2,1)S(1)}, u32[]{:S(2)}, u32[]{:S(2)}) collective-permute-start(bf16[4,48,128]{2,1,0:T(8,128)(2,1)S(1)} %get-tuple-element.39), channel_id=1, source_target_pairs={{0,1},{1,2},{2,3},{3,4},{4,5},{5,6},{6,7},{7,8},{8,9},{9,10},{10,1... | collective-permute-start | bytes 147464 | tf_op jit(solution)/shard_map/ppermute | solution.py:401
  78.5 9.7 %collective-permute-start.3 = (bf16[4,48,128]{2,1,0:T(8,128)(2,1)S(1)}, bf16[4,48,128]{2,1,0:T(8,128)(2,1)S(1)}, u32[]{:S(2)}, u32[]{:S(2)}) collective-permute-start(bf16[4,48,128]{2,1,0:T(8,128)(2,1)S(1)} %get-tuple-element.40), channel_id=1, source_target_pairs={{1,0},{2,1},{3,2},{4,3},{5,4},{6,5},{7,6},{8,7},{9,8},{10,9},{11,1... | collective-permute-start | bytes 147464 | tf_op jit(solution)/shard_map/ppermute | solution.py:402
  88.1 0.7 copy-start.14
  88.2 0.7 copy-start.15
  88.9 17.7 %all-to-all-start.4 = ((bf16[16,48,128]{2,1,0:T(8,128)(2,1)}), bf16[16,48,128]{2,1,0:T(8,128)(2,1)S(1)}, u32[]{:S(2)}, u32[]{:S(2)}) async-start(bf16[16,48,128]{2,1,0:T(8,128)(2,1)} %broadcast_in_dim.11), calls=%async_computation.4 | async-start | bytes 393216 | tf_op jit(solution)/shard_map/all_to_all | solution.py:405
  106.6 0.7 copy-start.12
  (2 other events, 1.3 us)

commit v4 on v3

--- a/solution.py
+++ b/solution.py
@@ -16,6 +16,9 @@
 BF = jnp.bfloat16
 
 
+LIMIT = pltpu.CompilerParams(vmem_limit_bytes=16 * 1024 * 1024)
+
+
 def nn(a, b):
     return lax.dot_general(a, b, (((1,), (0,)), ((), ())), preferred_element_type=F32)
 
@@ -50,67 +53,131 @@
     return lax.broadcasted_iota(jnp.int32, shape, dim)
 
 
-def pack_kernel(atoms, tokens, to_before, to_after):
+def fetch(pairs, sems):
+    copies = [pltpu.make_async_copy(src, dst, sems.at[n]) for n, (src, dst) in enumerate(pairs)]
+    for copy in copies:
+        copy.start()
+    return copies
+
+
+def pack_kernel(device, atoms, tokens, to_before, to_after, line, sems):
     samples, count, width = atoms.shape
-    to_before[:samples] = atoms[:, :RIM]
-    to_after[:samples] = atoms[:, count - RIM :]
-    line = tokens[...].astype(F32)
-    to_before[samples] = jnp.broadcast_to(line, (RIM, width)).astype(BF)
-    to_after[samples] = jnp.broadcast_to(line, (RIM, width)).astype(BF)
-
-
-def pair_kernel(band, pair_gain, weight_rows, table, z_hat, pair_inv):
+    copies = fetch(
+        [
+            (tokens, line),
+            (atoms.at[:, :RIM], to_before.at[:samples]),
+            (atoms.at[:, count - RIM :], to_after.at[:samples]),
+        ],
+        sems,
+    )
+    copies[0].wait()
+    local = jnp.broadcast_to((line[...] - device[0] * 16).astype(F32), (RIM, width)).astype(BF)
+    to_before[samples] = local
+    to_after[samples] = local
+    copies[1].wait()
+    copies[2].wait()
+
+
+def weight_lines(weights):
+    rows = weights[...].astype(F32)
+    return jnp.concatenate([rows, jnp.zeros((16 - rows.shape[0], rows.shape[1]), F32)], axis=0)
+
+
+def weight_spread(weights):
+    rows = weights[...].astype(F32)
+    rows = [jnp.broadcast_to(rows[h : h + 1], (16, rows.shape[1])) for h in range(4)]
+    return jnp.concatenate(rows * 2, axis=0).astype(BF)
+
+
+def spread_slots(entries):
+    hit = (iota((entries, KW), 0) >> 4) == iota((entries, KW), 1)
+    return jnp.where(hit, 1.0, 0.0).astype(BF)
+
+
+def entry_grads(table_grad, entries):
+    grad = nn(spread_slots(entries), table_grad)
+    column = iota((entries, KW), 1)
+    shown = ((iota((entries, KW), 0) & 15) == (column & 15)) & (column < 64)
+    return jnp.where(shown, grad, 0.0).astype(BF)
+
+
+def pair_kernel(band, gain_hbm, weight_hbm, table, pair_norm, gain, weights, sems):
     heads = 4
     entries = band.shape[0]
-    hat, inv = norm(band[...].astype(F32))
-    z_hat[...] = hat
-    pair_inv[...] = inv
-    pair_norm = (hat * pair_gain[...]).astype(BF)
-    bias_rows = nt(weight_rows[...], pair_norm)
+    copies = fetch([(gain_hbm, gain), (weight_hbm, weights)], sems)
+    hat, _ = norm(band[...].astype(F32))
+    for copy in copies:
+        copy.wait()
+    normed = (hat * gain[...]).astype(BF)
+    pair_norm[...] = normed
+    bias_rows = nt(weight_lines(weights).astype(BF), normed)
     stacked = jnp.concatenate(
         [jnp.broadcast_to(bias_rows[h : h + 1], (16, entries)) for h in range(heads)], axis=0
     )
     own_token = (iota((64, entries), 0) & 15) == (iota((64, entries), 1) & 15)
     high, low = split2(jnp.where(own_token, stacked, 0.0))
-    spread = (iota((entries, KW), 0) >> 4) == iota((entries, KW), 1)
-    spread = jnp.where(spread, 1.0, 0.0).astype(BF)
-    table[...] = nn(jnp.concatenate([high, low], axis=0), spread).astype(BF)
+    both = jnp.concatenate([high, low], axis=0)
+    table[...] = nn(both, spread_slots(entries)).astype(BF)
+
+
+def band_kernel(band, scattered, pair_gain, weights, band_grad):
+    entries = band.shape[0]
+    width = band.shape[1]
+    rows = [scattered[c].astype(F32)[40:43] for c in range(scattered.shape[0])]
+    rows = jnp.concatenate(rows + [jnp.zeros((KW - 3 * len(rows), width), F32)], axis=0).astype(BF)
+    hat, inv = norm(band[...].astype(F32))
+    norm_grad = nn(entry_grads(rows, entries), weight_spread(weights)).astype(BF).astype(F32)
+    band_grad[...] = norm_back(norm_grad * pair_gain[...], hat, inv).astype(BF)
 
 
 def attention_kernel(
     key_range,
     device,
-    atoms,
-    cotangent,
+    atoms_hbm,
+    cotangent_hbm,
+    project_hbm,
+    combine_hbm,
+    gain_hbm,
+    tokens_hbm,
     before,
     after,
-    project,
-    combine,
-    atom_gain,
     table,
-    z_hat,
-    pair_inv,
-    pair_gain,
-    weight_rows,
-    tokens,
+    pair_norm,
     outgoing,
     to_before,
     to_after,
     own_grad,
     bias,
     bias_grad,
+    atoms,
+    cotangent,
+    project,
+    combine,
+    atom_gain,
+    tokens,
+    sems,
 ):
     samples, count, width = atoms.shape
     heads = 4
     windows = count // QW
-    entries = z_hat.shape[0]
+    entries = pair_norm.shape[0]
     scale = 1.0 / math.sqrt(width // heads)
-    gain = atom_gain[...]
-
+    copies = fetch(
+        [
+            (tokens_hbm, tokens),
+            (gain_hbm, atom_gain),
+            (atoms_hbm, atoms),
+            (project_hbm, project),
+            (cotangent_hbm, cotangent),
+            (combine_hbm, combine),
+        ],
+        sems,
+    )
+    copies[0].wait()
     lane = iota((KW, KW), 1)
     line = iota((KW, KW), 0)
 
-    own = jnp.broadcast_to(tokens[...].astype(F32), (8, KW))
+    own = jnp.broadcast_to((tokens[...] - device[0] * 16).astype(F32), (8, KW))
     left = before[samples][:16].astype(F32)[:8] - 16.0
     right = after[samples][:16].astype(F32)[:8] + 16.0
     row_lane = iota((8, KW), 1)
@@ -143,6 +210,9 @@
         allowed = (line >= key_range[w, 0] - first) & (line < key_range[w, 1] - first)
         bias[w] = jnp.where(allowed, values, NEG_FILL)
         bias_grad[w] = jnp.zeros((KW, KW), F32)
+    for copy in copies[1:]:
+        copy.wait()
+    gain = atom_gain[...]
     diag = jnp.where((line >> 5) == (lane >> 5), 1.0, 0.0).astype(BF)
     head_of = iota((QW, width), 1) >> 5
 
@@ -167,7 +237,7 @@
         return jnp.concatenate(sums, axis=0).astype(BF)
 
     def sample(s, carry):
-        project_sum, combine_sum, scale_sum = carry
+        project_sum, combine_sum = carry
         x = jnp.concatenate([before[s], atoms[s], after[s]], axis=0).astype(F32)
         x_hat, _ = norm(x)
         normed = (x_hat * gain).astype(BF)
@@ -208,18 +278,16 @@
         grad = jnp.concatenate([query_cols, key_grad, value_grad, gate_cols], axis=1)
         project_sum = project_sum + tn(normed, grad)
         normed_grad = nt(grad, project[...])
-        scale_sum = scale_sum + jnp.sum(normed_grad * x_hat, axis=0, keepdims=True)
         to_before[s] = normed_grad[:RIM].astype(BF)
         to_after[s] = normed_grad[RIM + count :].astype(BF)
         own_grad[s] = normed_grad[RIM : RIM + count]
-        return project_sum, combine_sum, scale_sum
+        return project_sum, combine_sum
 
     start = (
         jnp.zeros((width, 4 * width), F32),
         jnp.zeros((width, width), F32),
-        jnp.zeros((1, width), F32),
-    )
-    project_sum, combine_sum, scale_sum = lax.fori_loop(0, samples, sample, start, unroll=True)
+    )
+    project_sum, combine_sum = lax.fori_loop(0, samples, sample, start, unroll=True)
 
     table_grad = jnp.zeros((KW, KW), F32)
     for w in range(windows):
@@ -229,48 +297,68 @@
         high, low = split2(by_slot)
         rows = query_hot(w)
         table_grad = table_grad + nt(high, rows) + nt(low, rows)
-    spread = (iota((entries, KW), 0) >> 4) == iota((entries, KW), 1)
-    spread = jnp.where(spread, 1.0, 0.0).astype(BF)
-    entry_grad = nn(spread, table_grad.astype(BF))
-    shown = (iota((entries, KW), 0) & 15) == (iota((entries, KW), 1) & 15)
-    shown = shown & (iota((entries, KW), 1) < 64)
-    entry_grad = jnp.where(shown, entry_grad, 0.0).astype(BF)
-    weight_of = jnp.concatenate(
-        [jnp.broadcast_to(weight_rows[h : h + 1, :], (16, width)) for h in range(heads)] * 2, axis=0
-    )
-    hat = z_hat[...]
-    pair_norm = (hat * pair_gain[...]).astype(BF)
-    norm_grad = nn(entry_grad, weight_of).astype(BF).astype(F32)
-    weight_part = tn(entry_grad, pair_norm)
-    tail = [
-        jnp.sum(weight_part[h * 16 : (h + 1) * 16], axis=0, keepdims=True) for h in range(heads)
-    ]
-    tail = tail + [scale_sum, jnp.sum(norm_grad * hat, axis=0, keepdims=True)]
-    tail = tail + [jnp.zeros((10, width), F32)]
-    band_part = norm_back(norm_grad * pair_gain[...], hat, pair_inv[...]).astype(BF)
+    entry_grad = entry_grads(table_grad.astype(BF), entries)
+    weight_part = tn(entry_grad, pair_norm[...])
     sums = jnp.concatenate(
-        [project_sum[:, part * width : (part + 1) * width] for part in range(4)]
-        + [combine_sum]
-        + tail
-        + [jnp.zeros((entries - 5 * width - 16, width), F32)],
+        [project_sum[:, part * width : (part + 1) * width] for part in range(4)] + [combine_sum],
         axis=0,
-    ).astype(BF)
-    part = entries // 16
-    for c in range(16):
-        outgoing[c, :part, :] = band_part[c * part : (c + 1) * part]
-        outgoing[c, part:, :] = sums[c * part : (c + 1) * part]
-
-
-def last_kernel(parts, project_grad, combine_grad, weight_grad, scale_grad, gain_grad):
-    rows = jnp.concatenate([parts[c] for c in range(parts.shape[0])], axis=0)
+    )
+    peers = outgoing.shape[0]
+    for c in range(peers):
+        weight_row = jnp.zeros((1, width), F32)
+        if c < heads:
+            weight_row = jnp.sum(weight_part[c * 16 : (c + 1) * 16], axis=0, keepdims=True)
+        parts = [sums[c * 40 : (c + 1) * 40], table_grad[3 * c : 3 * c + 3], weight_row]
+        parts = parts + [jnp.zeros((4, width), F32)]
+        outgoing[c] = jnp.concatenate(parts, axis=0).astype(BF)
+
+
+def last_kernel(
+    parts_hbm,
+    project_hbm,
+    atom_gain_hbm,
+    pair_gain_hbm,
+    weight_hbm,
+    project_grad,
+    combine_grad,
+    weight_grad,
+    scale_grad,
+    gain_grad,
+    parts,
+    project,
+    atom_gain,
+    pair_gain,
+    weights,
+    sems,
+):
+    copies = fetch(
+        [
+            (parts_hbm, parts),
+            (project_hbm, project),
+            (atom_gain_hbm, atom_gain),
+            (pair_gain_hbm, pair_gain),
+            (weight_hbm, weights),
+        ],
+        sems,
+    )
+    for copy in copies:
+        copy.wait()
+    chunks = [parts[c].astype(F32) for c in range(parts.shape[0])]
+    rows = jnp.concatenate([x[:40] for x in chunks], axis=0)
     width = rows.shape[1]
+    dots = jnp.zeros((width, 1), F32)
     for part in range(4):
-        project_grad[:, part * width : (part + 1) * width] = rows[part * width : (part + 1) * width]
-    combine_grad[...] = rows[4 * width : 5 * width]
-    tail = rows[5 * width : 5 * width + 16].astype(F32)
-    weight_grad[...] = tail[:4].astype(BF)
-    scale_grad[...] = tail[4:5]
-    gain_grad[...] = tail[5:6]
+        columns = slice(part * width, (part + 1) * width)
+        block = rows[part * width : (part + 1) * width]
+        project_grad[:, columns] = block.astype(BF)
+        dots = dots + jnp.sum(block * project[:, columns].astype(F32), axis=1, keepdims=True)
+    combine_grad[...] = rows[4 * width :].astype(BF)
+    dots = jnp.transpose(jnp.broadcast_to(dots, (width, width)))[:1]
+    scale_grad[...] = dots / atom_gain[...]
+    tail = jnp.concatenate([x[43:44] for x in chunks[:4]], axis=0)
+    weight_grad[...] = tail.astype(BF)
+    dots = jnp.sum(tail * weights[...].astype(F32), axis=0, keepdims=True)
+    gain_grad[...] = dots / pair_gain[...]
 
 
 def finish_kernel(atoms, cotangent, own_grad, from_before, from_after, atom_gain, result):
@@ -287,6 +375,20 @@
 
 def vmem(n):
     return [pl.BlockSpec(memory_space=pltpu.VMEM)] * n
+
+
+def smem(n):
+    return [pl.BlockSpec(memory_space=pltpu.SMEM)] * n
+
+
+def anywhere(n):
+    return [pl.BlockSpec(memory_space=pl.ANY)] * n
+
+
+def copied(arrays):
+    return [pltpu.VMEM(x.shape, x.dtype) for x in arrays] + [
+        pltpu.SemaphoreType.DMA((len(arrays),))
+    ]
 
 
 def shards(
@@ -302,7 +404,6 @@
     key_range,
 ):
     samples, count, width = atoms.shape
-    heads = pair_weight.shape[1]
     rows, cols = lax.axis_size("row"), lax.axis_size("col")
     peers = rows * cols
     device = lax.axis_index(("row", "col"))
@@ -314,74 +415,63 @@
 
     shape = jax.ShapeDtypeStruct
 
+    shape = jax.ShapeDtypeStruct
+    device = device.astype(jnp.int32).reshape(1)
+    tokens = atom_token.reshape(1, count)
+    weights = pair_weight.T
+    gain = atom_gain.reshape(1, width)
+    band_gain = pair_gain.reshape(1, width)
+
+    entries = cols * keys * block
     tiles = jnp.transpose(pair_band.reshape(cols, block, keys, width), (0, 2, 1, 3))
-    tiles = lax.all_to_all(tiles, "col", 0, 0, tiled=True).reshape(cols * keys * block, width)
-
-    local = atom_token - device * block
+    band = lax.all_to_all(tiles, "col", 0, 0, tiled=True).reshape(entries, width)
+
     to_before, to_after = pl.pallas_call(
         pack_kernel,
         out_shape=(shape((samples + 1, RIM, width), BF),) * 2,
-        in_specs=vmem(2),
+        in_specs=smem(1) + anywhere(2),
         out_specs=tuple(vmem(2)),
+        scratch_shapes=[pltpu.VMEM((1, count), jnp.int32), pltpu.SemaphoreType.DMA((3,))],
+        compiler_params=LIMIT,
         name="pack",
-    )(atoms, local.reshape(1, count))
+    )(device, atoms, tokens)
     before = lax.ppermute(to_after, ("row", "col"), up)
     after = lax.ppermute(to_before, ("row", "col"), down)
-    weight_rows = jnp.pad(pair_weight.T, ((0, 16 - heads), (0, 0)))
-    gain = atom_gain.reshape(1, width)
-    entries = tiles.shape[0]
-    table, z_hat, pair_inv = pl.pallas_call(
+
+    fetched = [band_gain, weights]
+    table, pair_norm = pl.pallas_call(
         pair_kernel,
-        out_shape=(
-            shape((KW, KW), BF),
-            shape((entries, width), F32),
-            shape((entries, 1), F32),
-        ),
-        in_specs=vmem(3),
-        out_specs=tuple(vmem(3)),
+        out_shape=(shape((KW, KW), BF), shape((entries, width), BF)),
+        in_specs=vmem(1) + anywhere(2),
+        out_specs=tuple(vmem(2)),
+        scratch_shapes=copied(fetched),
         cost_estimate=pl.CostEstimate(flops=10**9, bytes_accessed=10**7, transcendentals=0),
+        compiler_params=LIMIT,
         name="pair",
-    )(tiles, pair_gain.reshape(1, width), weight_rows)
+    )(band, *fetched)
+    fetched = [atoms, cotangent, project, combine, gain, tokens]
     outgoing, to_before, to_after, own_grad = pl.pallas_call(
         attention_kernel,
         out_shape=(
-            shape((cols, 2 * keys * block, width), BF),
+            shape((cols, RIM, width), BF),
             shape((samples, RIM, width), BF),
             shape((samples, RIM, width), BF),
             shape((samples, count, width), F32),
         ),
-        in_specs=[pl.BlockSpec(memory_space=pltpu.SMEM)] * 2 + vmem(13),
+        in_specs=smem(2) + anywhere(len(fetched)) + vmem(4),
         out_specs=tuple(vmem(4)),
         scratch_shapes=[
             pltpu.VMEM((windows, KW, KW), F32),
             pltpu.VMEM((windows, KW, KW), F32),
-        ],
-        compiler_params=pltpu.CompilerParams(vmem_limit_bytes=32 * 1024 * 1024),
+        ]
+        + copied(fetched),
+        compiler_params=LIMIT,
         name="attention",
-    )(
-        key_range,
-        device.astype(jnp.int32).reshape(1),
-        atoms,
-        cotangent,
-        before,
-        after,
-        project,
-        combine,
-        gain,
-        table,
-        z_hat,
-        pair_inv,
-        pair_gain.reshape(1, width),
-        weight_rows,
-        local.reshape(1, count),
-    )
-
-    line = keys * block
-    chunk = outgoing.shape[1] - line
+    )(key_range, device, *fetched, before, after, table, pair_norm)
+
+    chunk = outgoing.shape[1]
     scattered = lax.all_to_all(outgoing, "col", 0, 0, tiled=True)
-    band_grad = scattered[:, :line].reshape(cols, keys, block, width)
-    band_grad = jnp.transpose(band_grad, (0, 2, 1, 3)).reshape(pair_band.shape)
-    part = jnp.sum(scattered[:, line:].astype(F32), axis=0).astype(BF)
+    part = jnp.sum(scattered.astype(F32), axis=0).astype(BF)
 
     def summed(x, groups):
         x = jnp.broadcast_to(x, (len(groups[0]), chunk, width))
@@ -395,6 +485,17 @@
         [y * 8 + z * 2 + core for z in range(4)] for y in range(rows // 8) for core in range(2)
     ]
     part = summed(part, near)
+    band_grad = pl.pallas_call(
+        band_kernel,
+        out_shape=shape((entries, width), BF),
+        in_specs=vmem(4),
+        out_specs=pl.BlockSpec(memory_space=pltpu.VMEM),
+        compiler_params=LIMIT,
+        name="band",
+    )(tiles.reshape(entries, width), scattered, band_gain, weights)
+    part, band_grad = lax.optimization_barrier((part, band_grad))
+    band_grad = jnp.transpose(band_grad.reshape(cols, keys, block, width), (0, 2, 1, 3))
+    band_grad = band_grad.reshape(pair_band.shape)
 
     part, to_before, to_after = lax.optimization_barrier((part, to_before, to_after))
     part = summed(part, far)
@@ -408,22 +509,26 @@
         out_shape=shape(atoms.shape, BF),
         in_specs=vmem(6),
         out_specs=pl.BlockSpec(memory_space=pltpu.VMEM),
+        compiler_params=LIMIT,
         name="finish",
     )(atoms, cotangent, own_grad, from_before, from_after, gain)
     part, atoms_grad, band_grad = lax.optimization_barrier((part, atoms_grad, band_grad))
+    fetched = [part, project, gain, band_gain, weights]
     project_grad, combine_grad, weight_grad, scale_grad, gain_grad = pl.pallas_call(
         last_kernel,
         out_shape=(
             shape(project.shape, BF),
             shape(combine.shape, BF),
-            shape((heads, width), BF),
+            shape(weights.shape, BF),
             shape((1, width), F32),
             shape((1, width), F32),
         ),
-        in_specs=vmem(1),
+        in_specs=anywhere(5),
         out_specs=tuple(vmem(5)),
+        scratch_shapes=copied(fetched),
+        compiler_params=LIMIT,
         name="last",
-    )(part)
+    )(*fetched)
     return (
         atoms_grad,
         project_grad,

time: 110 us -> 103 us (0.936)
  blocking collectives: 29.5 us -> 18.2 us
  starting transfers between devices: 47.1 us -> 53.6 us
  waiting for transfers between devices: 7.54 us -> 12.2 us
  local copies, waits for them, and re-layouts: 10.4 us -> 6.41 us
  Pallas kernels: 12.8 us -> 10.6 us
    all_to_all x1 -> x0, blocking collectives: 10.6 us -> none  [summed(): x = lax.all_to_all(x, 'row', 0, 0, axis_index_groups=groups, tiled=True)]
    all_to_all x1 -> x2, starting transfers between devices: 8.52 us -> 15 us  [summed(): x = lax.all_to_all(x, 'row', 0, 0, axis_index_groups=groups, tiled=True)]
    unnamed x39 -> x19, local copies, waits for them, and re-layouts: 6.18 us -> 2.11 us
    all_to_all x1 -> x2, waiting for transfers between devices: 2.12 us -> 5.65 us  [summed(): x = lax.all_to_all(x, 'row', 0, 0, axis_index_groups=groups, tiled=True)]
    pallas_call x1 -> x2, Pallas kernels: 5.24 us -> 7.56 us  [the longest x1 6.1 us: shards(): pl.pallas_call(attention_kernel, out_shape=(shape((cols, RIM, width), BF)...]
    pallas_call x1, Pallas kernels: 2.19 us -> 0.67 us  [shards(): pl.pallas_call(pair_kernel, out_shape=(shape((KW, KW), BF), shape((entrie...]
    pallas_call x1, Pallas kernels: 1.56 us -> 0.06 us  [shards(): pl.pallas_call(pack_kernel, out_shape=(shape((samples + 1, RIM, width), B...]
  transfers between devices with their start and end apart: 7 -> 8, of which waited for: 2 -> 3; matrix products, arithmetic and copies ran while one was open for 2% -> 1% of each run, Pallas kernels for 5% -> 3%
where the time goes in v4:
time: 103 us; the launch traced here: 102 us
  starting transfers between devices  53.6 us (52%)
  blocking collectives  18.2 us (18%)
  waiting for transfers between devices  12.2 us (12%)
  Pallas kernels  10.6 us (10%)
  local copies, waits for them, and re-layouts  6.41 us (6%)
    all_to_all x1, blocking collectives, shards(): scattered = lax.all_to_all(outgoing, 'col', 0, 0, tiled=True)  18.2 us
    all_to_all x2, starting transfers between devices, summed(): x = lax.all_to_all(x, 'row', 0, 0, axis_index_groups=groups, tiled=True)  15 us
    all_to_all x1, starting transfers between devices, shards(): part = lax.all_to_all(part, 'col', 0, 0, tiled=True)  9.4 us
    all_to_all x1, starting transfers between devices, shards(): lax.all_to_all(tiles, 'col', 0, 0, tiled=True).reshape(entries, width)  9.15 us
    ppermute x1, starting transfers between devices, shards(): after = lax.ppermute(to_before, ('row', 'col'), down)  7.36 us
    ppermute x1, starting transfers between devices, shards(): from_after = lax.ppermute(to_before, ('row', 'col'), down)  7.28 us
    all_to_all x1, waiting for transfers between devices, shards(): part = lax.all_to_all(part, 'col', 0, 0, tiled=True)  6.5 us
    pallas_call x1, Pallas kernels, shards(): pl.pallas_call(attention_kernel, out_shape=(shape((cols, RIM, width), BF)...  6.1 us
  transfers between devices with their start and end apart: 8, of which 3 were waited for; matrix products, arithmetic and copies ran while one was open for 1% of the time, Pallas kernels for 3%

profile of v4, /device:TPU:1, one launch (start us, length us, event | category | flops | bytes accessed | tf_op | source)
XLA Modules:
  0.0 101.9 jit_solution(4069418272542429972)
XLA Ops:
  0.6 1.6 %copy.25 = bf16[16,16,3,128]{3,1,2,0:T(8,128)(2,1)} copy(bf16[16,16,3,128]{3,1,0,2:T(8,128)(2,1)} %bitcast.31) | data formatting | bytes 393216 | tf_op jit(solution)/shard_map/reshape | solution.py:426
  2.3 9.1 %all-to-all-start = ((bf16[16,3,16,128]{3,2,1,0:T(8,128)(2,1)}), bf16[16,3,16,128]{3,2,1,0:T(8,128)(2,1)S(1)}, u32[]{:S(2)}, u32[]{:S(2)}) async-start(bf16[16,3,16,128]{3,2,1,0:T(8,128)(2,1)} %bitcast.17.clone.2), calls=%async_computation | async-start | bytes 393216 | tf_op jit(solution)/shard_map/all_to_all | solution.py:427
  11.4 0.6 copy-done.6
  12.2 3.3 %collective-permute-start = (bf16[5,48,128]{2,1,0:T(8,128)(2,1)S(1)}, bf16[5,48,128]{2,1,0:T(8,128)(2,1)S(1)}, u32[]{:S(2)}, u32[]{:S(2)}) collective-permute-start(bf16[5,48,128]{2,1,0:T(8,128)(2,1)S(1)} %get-tuple-element.31), channel_id=1, source_target_pairs={{0,1},{1,2},{2,3},{3,4},{4,5},{5,6},{6,7},{7,8},{8,9},{9,10},{10,1... | collective-permute-start | bytes 184328 | tf_op jit(solution)/shard_map/ppermute | solution.py:438
  15.4 7.4 %collective-permute-start.1 = (bf16[5,48,128]{2,1,0:T(8,128)(2,1)S(1)}, bf16[5,48,128]{2,1,0:T(8,128)(2,1)S(1)}, u32[]{:S(2)}, u32[]{:S(2)}) collective-permute-start(bf16[5,48,128]{2,1,0:T(8,128)(2,1)S(1)} %get-tuple-element.32), channel_id=1, source_target_pairs={{1,0},{2,1},{3,2},{4,3},{5,4},{6,5},{7,6},{8,7},{9,8},{10,9},{11,1... | collective-permute-start | bytes 184328 | tf_op jit(solution)/shard_map/ppermute | solution.py:439
  22.9 0.7 copy-done.5
  23.6 0.7 pair.1
  25.0 6.1 %attention.1 = (bf16[16,48,128]{2,1,0:T(8,128)(2,1)S(1)}, bf16[4,48,128]{2,1,0:T(8,128)(2,1)S(1)}, bf16[4,48,128]{2,1,0:T(8,128)(2,1)S(1)}, f32[4,128,128]{2,1,0:T(8,128)S(1)}) custom-call(s32[4,2]{1,0:T(4,128)S(1)} %copy.21.key_range, s32[1]{0:T(128)} %bitcast.device, bf16[4,128,128]{2,1,0:T(8,128)(2,1)S(1)} %copy-done, bf16[4,128,128]{2,1,0:T(8,128)(2,1)S(1)} %copy-done.1, ...), custom_call_target="tpu_custom_call" | custom-call | tf_op jit(solution)/shard_map/attention/pallas_call | solution.py:453
  31.1 18.2 %all_to_all.25.scattered = bf16[16,48,128]{2,1,0:T(8,128)(2,1)S(1)} all-to-all(bf16[16,48,128]{2,1,0:T(8,128)(2,1)S(1)} %get-tuple-element.35), channel_id=1, replica_groups=mesh['row'=32,'col'=16] {'col'}, dimensions={0} | all-to-all | bytes 393216 | tf_op jit(solution)/shard_map/all_to_all | solution.py:473
  49.4 0.7 broadcast_in_dim.9
  50.0 4.6 %all-to-all-start.2 = ((bf16[8,48,128]{2,1,0:T(8,128)(2,1)}), bf16[8,48,128]{2,1,0:T(8,128)(2,1)S(1)}, u32[]{:S(2)}, u32[]{:S(2)}) async-start(bf16[8,48,128]{2,1,0:T(8,128)(2,1)} %broadcast_in_dim.9), calls=%async_computation.2 | async-start | bytes 196608 | tf_op jit(solution)/shard_map/all_to_all | solution.py:478
  54.6 1.5 %band.1 = bf16[768,128]{1,0:T(8,128)(2,1)S(1)} custom-call(bf16[768,128]{1,0:T(8,128)(2,1)} %bitcast.8.band, bf16[16,48,128]{2,1,0:T(8,128)(2,1)S(1)} %all_to_all.25.scattered, f32[1,128]{1,0:T(1,128)S(1)} %bitcast.29, bf16[4,128]{1,0:T(4,128)(2,1)S(1)} %bitcast.24), custom_call_target="tpu_custom_call" | custom-call | tf_op jit(solution)/shard_map/band/pallas_call | solution.py:488
  56.1 3.5 %all-to-all-done.2 = bf16[8,48,128]{2,1,0:T(8,128)(2,1)S(1)} async-done(((bf16[8,48,128]{2,1,0:T(8,128)(2,1)}), bf16[8,48,128]{2,1,0:T(8,128)(2,1)S(1)}, u32[]{:S(2)}, u32[]{:S(2)}) %all-to-all-start.2) | async-done | bytes 98336 | tf_op jit(solution)/shard_map/all_to_all | solution.py:478
  59.6 0.6 broadcast_in_dim.10
  60.2 10.4 %all-to-all-start.3 = ((bf16[4,48,128]{2,1,0:T(8,128)(2,1)}), bf16[4,48,128]{2,1,0:T(8,128)(2,1)S(1)}, u32[]{:S(2)}, u32[]{:S(2)}) async-start(bf16[4,48,128]{2,1,0:T(8,128)(2,1)} %broadcast_in_dim.10), calls=%async_computation.3 | async-start | bytes 98304 | tf_op jit(solution)/shard_map/all_to_all | solution.py:478
  70.6 2.2 %collective-permute-start.2 = (bf16[4,48,128]{2,1,0:T(8,128)(2,1)S(1)}, bf16[4,48,128]{2,1,0:T(8,128)(2,1)S(1)}, u32[]{:S(2)}, u32[]{:S(2)}) collective-permute-start(bf16[4,48,128]{2,1,0:T(8,128)(2,1)S(1)} %get-tuple-element.40), channel_id=1, source_target_pairs={{0,1},{1,2},{2,3},{3,4},{4,5},{5,6},{6,7},{7,8},{8,9},{9,10},{10,1... | collective-permute-start | bytes 147464 | tf_op jit(solution)/shard_map/ppermute | solution.py:502
  72.8 7.3 %collective-permute-start.3 = (bf16[4,48,128]{2,1,0:T(8,128)(2,1)S(1)}, bf16[4,48,128]{2,1,0:T(8,128)(2,1)S(1)}, u32[]{:S(2)}, u32[]{:S(2)}) collective-permute-start(bf16[4,48,128]{2,1,0:T(8,128)(2,1)S(1)} %get-tuple-element.41), channel_id=1, source_target_pairs={{1,0},{2,1},{3,2},{4,3},{5,4},{6,5},{7,6},{8,7},{9,8},{10,9},{11,1... | collective-permute-start | bytes 147464 | tf_op jit(solution)/shard_map/ppermute | solution.py:503
  80.1 2.1 %all-to-all-done.3 = bf16[4,48,128]{2,1,0:T(8,128)(2,1)S(1)} async-done(((bf16[4,48,128]{2,1,0:T(8,128)(2,1)}), bf16[4,48,128]{2,1,0:T(8,128)(2,1)S(1)}, u32[]{:S(2)}, u32[]{:S(2)}) %all-to-all-start.3) | async-done | bytes 49184 | tf_op jit(solution)/shard_map/all_to_all | solution.py:478
  82.3 0.7 broadcast_in_dim.11
  83.0 9.4 %all-to-all-start.4 = ((bf16[16,48,128]{2,1,0:T(8,128)(2,1)}), bf16[16,48,128]{2,1,0:T(8,128)(2,1)S(1)}, u32[]{:S(2)}, u32[]{:S(2)}) async-start(bf16[16,48,128]{2,1,0:T(8,128)(2,1)} %broadcast_in_dim.11), calls=%async_computation.4 | async-start | bytes 393216 | tf_op jit(solution)/shard_map/all_to_all | solution.py:506
  92.4 0.7 copy.22
  93.1 1.1 %finish.1 = bf16[4,128,128]{2,1,0:T(8,128)(2,1)} custom-call(bf16[4,128,128]{2,1,0:T(8,128)(2,1)S(1)} %copy-done, bf16[4,128,128]{2,1,0:T(8,128)(2,1)S(1)} %copy-done.1, f32[4,128,128]{2,1,0:T(8,128)S(1)} %get-tuple-element.43.own_grad, bf16[4,48,128]{2,1,0:T(8,128)(2,1)S(1)} %collective-permute-done.2.from_before, ...), custom_call_target="tpu_custom_call" | custom-call | tf_op jit(solution)/shard_map/finish/pallas_call | solution.py:507
  94.2 6.5 %all-to-all-done.4.parts_hbm = bf16[16,48,128]{2,1,0:T(8,128)(2,1)S(1)} async-done(((bf16[16,48,128]{2,1,0:T(8,128)(2,1)}), bf16[16,48,128]{2,1,0:T(8,128)(2,1)S(1)}, u32[]{:S(2)}, u32[]{:S(2)}) %all-to-all-start.4) | async-done | bytes 196640 | tf_op jit(solution)/shard_map/all_to_all | solution.py:506
  100.7 1.2 %last.1 = (bf16[128,512]{1,0:T(8,128)(2,1)}, bf16[128,128]{1,0:T(8,128)(2,1)}, bf16[4,128]{1,0:T(4,128)(2,1)}, f32[1,128]{1,0:T(1,128)}, f32[1,128]{1,0:T(1,128)}) custom-call(bf16[16,48,128]{2,1,0:T(8,128)(2,1)S(1)} %all-to-all-done.4.parts_hbm, bf16[128,512]{1,0:T(8,128)(2,1)S(1)} %copy-done.2, f32[1,128]{1,0:T(1,128)S(1)} %bitcast.22, ...), custom_call_target="tpu_custom_call" | custom-call | tf_op jit(solution)/shard_map/last/pallas_call | solution.py:517
  (26 shorter events, 0.9 us)
Async XLA Ops:
  2.2 9.2 %copy-start = (bf16[4,128,128]{2,1,0:T(8,128)(2,1)S(1)}, bf16[4,128,128]{2,1,0:T(8,128)(2,1)}, u32[]{:S(2)}) copy-start(bf16[4,128,128]{2,1,0:T(8,128)(2,1)} %atoms.3) | copy-start | bytes 393220
  2.3 20.6 %all-to-all-start = ((bf16[16,3,16,128]{3,2,1,0:T(8,128)(2,1)}), bf16[16,3,16,128]{3,2,1,0:T(8,128)(2,1)S(1)}, u32[]{:S(2)}, u32[]{:S(2)}) async-start(bf16[16,3,16,128]{3,2,1,0:T(8,128)(2,1)} %bitcast.17.clone.2), calls=%async_computation | async-start | bytes 393216 | tf_op jit(solution)/shard_map/all_to_all | solution.py:427
  11.4 0.7 copy-start.6
  12.1 10.7 %copy-start.8 = (s32[4,2]{0,1:T(2,128)S(1)}, s32[4,2]{0,1:T(2,128)}, u32[]{:S(2)}) copy-start(s32[4,2]{0,1:T(2,128)} %param.19) | copy-start | bytes 100
  12.2 12.1 %collective-permute-start = (bf16[5,48,128]{2,1,0:T(8,128)(2,1)S(1)}, bf16[5,48,128]{2,1,0:T(8,128)(2,1)S(1)}, u32[]{:S(2)}, u32[]{:S(2)}) collective-permute-start(bf16[5,48,128]{2,1,0:T(8,128)(2,1)S(1)} %get-tuple-element.31), channel_id=1, source_target_pairs={{0,1},{1,2},{2,3},{3,4},{4,5},{5,6},{6,7},{7,8},{8,9},{9,10},{10,1... | collective-permute-start | bytes 184328 | tf_op jit(solution)/shard_map/ppermute | solution.py:438
  15.4 8.9 %collective-permute-start.1 = (bf16[5,48,128]{2,1,0:T(8,128)(2,1)S(1)}, bf16[5,48,128]{2,1,0:T(8,128)(2,1)S(1)}, u32[]{:S(2)}, u32[]{:S(2)}) collective-permute-start(bf16[5,48,128]{2,1,0:T(8,128)(2,1)S(1)} %get-tuple-element.32), channel_id=1, source_target_pairs={{1,0},{2,1},{3,2},{4,3},{5,4},{6,5},{7,6},{8,7},{9,8},{10,9},{11,1... | collective-permute-start | bytes 184328 | tf_op jit(solution)/shard_map/ppermute | solution.py:439
  22.9 0.7 copy-start.5
  22.9 0.7 copy-start.7
  23.6 0.9 copy-start.1
  23.6 1.0 copy-start.2
  23.6 1.0 copy-start.3
  24.3 0.7 copy-start.4
  50.0 9.6 %all-to-all-start.2 = ((bf16[8,48,128]{2,1,0:T(8,128)(2,1)}), bf16[8,48,128]{2,1,0:T(8,128)(2,1)S(1)}, u32[]{:S(2)}, u32[]{:S(2)}) async-start(bf16[8,48,128]{2,1,0:T(8,128)(2,1)} %broadcast_in_dim.9), calls=%async_computation.2 | async-start | bytes 196608 | tf_op jit(solution)/shard_map/all_to_all | solution.py:478
  60.2 22.0 %all-to-all-start.3 = ((bf16[4,48,128]{2,1,0:T(8,128)(2,1)}), bf16[4,48,128]{2,1,0:T(8,128)(2,1)S(1)}, u32[]{:S(2)}, u32[]{:S(2)}) async-start(bf16[4,48,128]{2,1,0:T(8,128)(2,1)} %broadcast_in_dim.10), calls=%async_computation.3 | async-start | bytes 98304 | tf_op jit(solution)/shard_map/all_to_all | solution.py:478
  70.6 11.6 %collective-permute-start.2 = (bf16[4,48,128]{2,1,0:T(8,128)(2,1)S(1)}, bf16[4,48,128]{2,1,0:T(8,128)(2,1)S(1)}, u32[]{:S(2)}, u32[]{:S(2)}) collective-permute-start(bf16[4,48,128]{2,1,0:T(8,128)(2,1)S(1)} %get-tuple-element.40), channel_id=1, source_target_pairs={{0,1},{1,2},{2,3},{3,4},{4,5},{5,6},{6,7},{7,8},{8,9},{9,10},{10,1... | collective-permute-start | bytes 147464 | tf_op jit(solution)/shard_map/ppermute | solution.py:502
  72.8 9.4 %collective-permute-start.3 = (bf16[4,48,128]{2,1,0:T(8,128)(2,1)S(1)}, bf16[4,48,128]{2,1,0:T(8,128)(2,1)S(1)}, u32[]{:S(2)}, u32[]{:S(2)}) collective-permute-start(bf16[4,48,128]{2,1,0:T(8,128)(2,1)S(1)} %get-tuple-element.41), channel_id=1, source_target_pairs={{1,0},{2,1},{3,2},{4,3},{5,4},{6,5},{7,6},{8,7},{9,8},{10,9},{11,1... | collective-permute-start | bytes 147464 | tf_op jit(solution)/shard_map/ppermute | solution.py:503
  83.0 17.7 %all-to-all-start.4 = ((bf16[16,48,128]{2,1,0:T(8,128)(2,1)}), bf16[16,48,128]{2,1,0:T(8,128)(2,1)S(1)}, u32[]{:S(2)}, u32[]{:S(2)}) async-start(bf16[16,48,128]{2,1,0:T(8,128)(2,1)} %broadcast_in_dim.11), calls=%async_computation.4 | async-start | bytes 393216 | tf_op jit(solution)/shard_map/all_to_all | solution.py:506

commit v5 on v4

--- a/solution.py
+++ b/solution.py
@@ -60,20 +60,23 @@
     return copies
 
 
-def pack_kernel(device, atoms, tokens, to_before, to_after, line, sems):
+def pack_kernel(device, atoms, tokens, first, second, line, sems):
     samples, count, width = atoms.shape
+    odd = device[0] & 1
+    low = pl.multiple_of((1 - odd) * (count - RIM), 16)
+    high = pl.multiple_of(odd * (count - RIM), 16)
     copies = fetch(
         [
             (tokens, line),
-            (atoms.at[:, :RIM], to_before.at[:samples]),
-            (atoms.at[:, count - RIM :], to_after.at[:samples]),
+            (atoms.at[:, pl.ds(low, RIM)], first.at[:samples]),
+            (atoms.at[:, pl.ds(high, RIM)], second.at[:samples]),
         ],
         sems,
     )
     copies[0].wait()
     local = jnp.broadcast_to((line[...] - device[0] * 16).astype(F32), (RIM, width)).astype(BF)
-    to_before[samples] = local
-    to_after[samples] = local
+    first[samples] = local
+    second[samples] = local
     copies[1].wait()
     copies[2].wait()
 
@@ -120,10 +123,12 @@
     table[...] = nn(both, spread_slots(entries)).astype(BF)
 
 
-def band_kernel(band, scattered, pair_gain, weights, band_grad):
+def band_kernel(device, band, scattered, pair_gain, weights, band_grad):
     entries = band.shape[0]
     width = band.shape[1]
-    rows = [scattered[c].astype(F32)[40:43] for c in range(scattered.shape[0])]
+    peers = scattered.shape[0] // 2
+    core = (device[0] // peers) & 1
+    rows = [scattered[core * peers + c].astype(F32)[20:23] for c in range(peers)]
     rows = jnp.concatenate(rows + [jnp.zeros((KW - 3 * len(rows), width), F32)], axis=0).astype(BF)
     hat, inv = norm(band[...].astype(F32))
     norm_grad = nn(entry_grads(rows, entries), weight_spread(weights)).astype(BF).astype(F32)
@@ -139,13 +144,13 @@
     combine_hbm,
     gain_hbm,
     tokens_hbm,
-    before,
-    after,
+    first,
+    second,
     table,
     pair_norm,
     outgoing,
-    to_before,
-    to_after,
+    to_first,
+    to_second,
     own_grad,
     bias,
     bias_grad,
@@ -178,8 +183,14 @@
     line = iota((KW, KW), 0)
 
     own = jnp.broadcast_to((tokens[...] - device[0] * 16).astype(F32), (8, KW))
-    left = before[samples][:16].astype(F32)[:8] - 16.0
-    right = after[samples][:16].astype(F32)[:8] + 16.0
+    odd = (device[0] & 1) == 1
+
+    def sides(x, y):
+        return jnp.where(odd, x, y), jnp.where(odd, y, x)
+
+    left, right = sides(first[samples].astype(F32), second[samples].astype(F32))
+    left = left[:8] - 16.0
+    right = right[:8] + 16.0
     row_lane = iota((8, KW), 1)
     turned = [own] + [pltpu.roll(own, h * QW, 1) for h in range(1, heads)]
 
@@ -191,9 +202,9 @@
 
     def key_row(w):
         shift = RIM - w * QW
-        first, second = (left, own) if shift > 0 else (own, right)
+        one, two = (left, own) if shift > 0 else (own, right)
         shift = shift % KW
-        row = jnp.where(row_lane < shift, pltpu.roll(first, shift, 1), pltpu.roll(second, shift, 1))
+        row = jnp.where(row_lane < shift, pltpu.roll(one, shift, 1), pltpu.roll(two, shift, 1))
         return row.astype(jnp.int32)[:1] + 16
 
     def query_hot(w):
@@ -206,8 +217,8 @@
     for w in range(windows):
         by_key = nn(table[...], key_hot(w)).astype(BF)
         values = tn(by_key, query_hot(w))
-        first = device[0] * count - RIM + w * QW
-        allowed = (line >= key_range[w, 0] - first) & (line < key_range[w, 1] - first)
+        begin = device[0] * count - RIM + w * QW
+        allowed = (line >= key_range[w, 0] - begin) & (line < key_range[w, 1] - begin)
         bias[w] = jnp.where(allowed, values, NEG_FILL)
         bias_grad[w] = jnp.zeros((KW, KW), F32)
     for copy in copies[1:]:
@@ -238,7 +249,8 @@
 
     def sample(s, carry):
         project_sum, combine_sum = carry
-        x = jnp.concatenate([before[s], atoms[s], after[s]], axis=0).astype(F32)
+        before, after = sides(first[s].astype(F32), second[s].astype(F32))
+        x = jnp.concatenate([before, atoms[s].astype(F32), after], axis=0)
         x_hat, _ = norm(x)
         normed = (x_hat * gain).astype(BF)
         projected = nn(normed, project[...]).astype(BF)
@@ -278,8 +290,9 @@
         grad = jnp.concatenate([query_cols, key_grad, value_grad, gate_cols], axis=1)
         project_sum = project_sum + tn(normed, grad)
         normed_grad = nt(grad, project[...])
-        to_before[s] = normed_grad[:RIM].astype(BF)
-        to_after[s] = normed_grad[RIM + count :].astype(BF)
+        before, after = sides(normed_grad[:RIM], normed_grad[RIM + count :])
+        to_first[s] = before.astype(BF)
+        to_second[s] = after.astype(BF)
         own_grad[s] = normed_grad[RIM : RIM + count]
         return project_sum, combine_sum
 
@@ -299,18 +312,20 @@
         table_grad = table_grad + nt(high, rows) + nt(low, rows)
     entry_grad = entry_grads(table_grad.astype(BF), entries)
     weight_part = tn(entry_grad, pair_norm[...])
-    sums = jnp.concatenate(
-        [project_sum[:, part * width : (part + 1) * width] for part in range(4)] + [combine_sum],
-        axis=0,
-    )
     peers = outgoing.shape[0]
-    for c in range(peers):
+    for p in range(peers):
+        part, row = divmod(16 * p, width)
         weight_row = jnp.zeros((1, width), F32)
-        if c < heads:
-            weight_row = jnp.sum(weight_part[c * 16 : (c + 1) * 16], axis=0, keepdims=True)
-        parts = [sums[c * 40 : (c + 1) * 40], table_grad[3 * c : 3 * c + 3], weight_row]
-        parts = parts + [jnp.zeros((4, width), F32)]
-        outgoing[c] = jnp.concatenate(parts, axis=0).astype(BF)
+        if p < heads:
+            weight_row = jnp.sum(weight_part[p * 16 : (p + 1) * 16], axis=0, keepdims=True)
+        slot = 3 * (p % (peers // 2))
+        parts = [
+            project_sum[row : row + 16, part * width : (part + 1) * width],
+            combine_sum[4 * p : 4 * p + 4],
+            table_grad[slot : slot + 3],
+            weight_row,
+        ]
+        outgoing[p] = jnp.concatenate(parts, axis=0).astype(BF)
 
 
 def last_kernel(
@@ -343,8 +358,8 @@
     )
     for copy in copies:
         copy.wait()
-    chunks = [parts[c].astype(F32) for c in range(parts.shape[0])]
-    rows = jnp.concatenate([x[:40] for x in chunks], axis=0)
+    chunks = [parts[p].astype(F32) for p in range(parts.shape[0])]
+    rows = jnp.concatenate([x[:16] for x in chunks], axis=0)
     width = rows.shape[1]
     dots = jnp.zeros((width, 1), F32)
     for part in range(4):
@@ -352,23 +367,25 @@
         block = rows[part * width : (part + 1) * width]
         project_grad[:, columns] = block.astype(BF)
         dots = dots + jnp.sum(block * project[:, columns].astype(F32), axis=1, keepdims=True)
-    combine_grad[...] = rows[4 * width :].astype(BF)
+    combine_grad[...] = jnp.concatenate([x[16:20] for x in chunks], axis=0).astype(BF)
     dots = jnp.transpose(jnp.broadcast_to(dots, (width, width)))[:1]
     scale_grad[...] = dots / atom_gain[...]
-    tail = jnp.concatenate([x[43:44] for x in chunks[:4]], axis=0)
+    tail = jnp.concatenate([x[23:24] for x in chunks[:4]], axis=0)
     weight_grad[...] = tail.astype(BF)
     dots = jnp.sum(tail * weights[...].astype(F32), axis=0, keepdims=True)
     gain_grad[...] = dots / pair_gain[...]
 
 
-def finish_kernel(atoms, cotangent, own_grad, from_before, from_after, atom_gain, result):
+def finish_kernel(device, atoms, cotangent, own_grad, first, second, atom_gain, result):
     samples, count, width = atoms.shape
+    odd = (device[0] & 1) == 1
     gain = atom_gain[...]
     for s in range(samples):
         x_hat, inv = norm(atoms[s].astype(F32))
         rim = jnp.zeros((count - RIM, width), F32)
-        total = own_grad[s] + jnp.concatenate([from_before[s].astype(F32), rim], axis=0)
-        total = total + jnp.concatenate([rim, from_after[s].astype(F32)], axis=0)
+        one, two = first[s].astype(F32), second[s].astype(F32)
+        total = own_grad[s] + jnp.concatenate([jnp.where(odd, one, two), rim], axis=0)
+        total = total + jnp.concatenate([rim, jnp.where(odd, two, one)], axis=0)
         g = total.astype(BF).astype(F32) * gain
         result[s] = (cotangent[s].astype(F32) + norm_back(g, x_hat, inv)).astype(BF)
 
@@ -410,8 +427,8 @@
     windows = count // QW
     block = pair_band.shape[0] // cols
     keys = pair_band.shape[1]
-    up = [(i, i + 1) for i in range(peers - 1)]
-    down = [(i + 1, i) for i in range(peers - 1)]
+    pairs = [(i, i ^ 1) for i in range(peers)]
+    odd_pairs = [(i + j, i + 1 - j) for i in range(1, peers - 1, 2) for j in range(2)]
 
     shape = jax.ShapeDtypeStruct
 
@@ -426,7 +443,7 @@
     tiles = jnp.transpose(pair_band.reshape(cols, block, keys, width), (0, 2, 1, 3))
     band = lax.all_to_all(tiles, "col", 0, 0, tiled=True).reshape(entries, width)
 
-    to_before, to_after = pl.pallas_call(
+    first, second = pl.pallas_call(
         pack_kernel,
         out_shape=(shape((samples + 1, RIM, width), BF),) * 2,
         in_specs=smem(1) + anywhere(2),
@@ -435,8 +452,8 @@
         compiler_params=LIMIT,
         name="pack",
     )(device, atoms, tokens)
-    before = lax.ppermute(to_after, ("row", "col"), up)
-    after = lax.ppermute(to_before, ("row", "col"), down)
+    first = lax.ppermute(first, ("row", "col"), pairs)
+    second = lax.ppermute(second, ("row", "col"), odd_pairs)
 
     fetched = [band_gain, weights]
     table, pair_norm = pl.pallas_call(
@@ -450,10 +467,10 @@
         name="pair",
     )(band, *fetched)
     fetched = [atoms, cotangent, project, combine, gain, tokens]
-    outgoing, to_before, to_after, own_grad = pl.pallas_call(
+    outgoing, first, second, own_grad = pl.pallas_call(
         attention_kernel,
         out_shape=(
-            shape((cols, RIM, width), BF),
+            shape((2 * cols, 24, width), BF),
             shape((samples, RIM, width), BF),
             shape((samples, RIM, width), BF),
             shape((samples, count, width), F32),
@@ -467,51 +484,42 @@
         + copied(fetched),
         compiler_params=LIMIT,
         name="attention",
-    )(key_range, device, *fetched, before, after, table, pair_norm)
-
-    chunk = outgoing.shape[1]
-    scattered = lax.all_to_all(outgoing, "col", 0, 0, tiled=True)
+    )(key_range, device, *fetched, first, second, table, pair_norm)
+
+    near = [list(range(i, i + 2 * cols)) for i in range(0, peers, 2 * cols)]
+    far = [list(range(i, rows, 2)) for i in range(2)]
+    scattered = lax.all_to_all(
+        outgoing, ("row", "col"), 0, 0, axis_index_groups=near, tiled=True
+    )
     part = jnp.sum(scattered.astype(F32), axis=0).astype(BF)
 
-    def summed(x, groups):
-        x = jnp.broadcast_to(x, (len(groups[0]), chunk, width))
-        x = lax.all_to_all(x, "row", 0, 0, axis_index_groups=groups, tiled=True)
-        return jnp.sum(x.astype(F32), axis=0).astype(BF)
-
-    near = [
-        [y * 8 + z * 2 + core for y in range(rows // 8) for core in range(2)] for z in range(4)
-    ]
-    far = [
-        [y * 8 + z * 2 + core for z in range(4)] for y in range(rows // 8) for core in range(2)
-    ]
-    part = summed(part, near)
+    part, first, second = lax.optimization_barrier((part, first, second))
+    part = jnp.broadcast_to(part, (rows // 2,) + part.shape)
+    part = lax.all_to_all(part, "row", 0, 0, axis_index_groups=far, tiled=True)
+    first = lax.ppermute(first, ("row", "col"), pairs)
+    second = lax.ppermute(second, ("row", "col"), odd_pairs)
+    part = jnp.sum(part.astype(F32), axis=0).astype(BF)
+    part, first, second = lax.optimization_barrier((part, first, second))
+    part = jnp.broadcast_to(part, (2 * cols,) + part.shape)
+    part = lax.all_to_all(part, ("row", "col"), 0, 0, axis_index_groups=near, tiled=True)
     band_grad = pl.pallas_call(
         band_kernel,
         out_shape=shape((entries, width), BF),
-        in_specs=vmem(4),
+        in_specs=smem(1) + vmem(4),
         out_specs=pl.BlockSpec(memory_space=pltpu.VMEM),
         compiler_params=LIMIT,
         name="band",
-    )(tiles.reshape(entries, width), scattered, band_gain, weights)
-    part, band_grad = lax.optimization_barrier((part, band_grad))
+    )(device, tiles.reshape(entries, width), scattered, band_gain, weights)
     band_grad = jnp.transpose(band_grad.reshape(cols, keys, block, width), (0, 2, 1, 3))
     band_grad = band_grad.reshape(pair_band.shape)
-
-    part, to_before, to_after = lax.optimization_barrier((part, to_before, to_after))
-    part = summed(part, far)
-    from_before = lax.ppermute(to_after, ("row", "col"), up)
-    from_after = lax.ppermute(to_before, ("row", "col"), down)
-    part, from_before, from_after = lax.optimization_barrier((part, from_before, from_after))
-    part = jnp.broadcast_to(part, (cols, chunk, width))
-    part = lax.all_to_all(part, "col", 0, 0, tiled=True)
     atoms_grad = pl.pallas_call(
         finish_kernel,
         out_shape=shape(atoms.shape, BF),
-        in_specs=vmem(6),
+        in_specs=smem(1) + vmem(6),
         out_specs=pl.BlockSpec(memory_space=pltpu.VMEM),
         compiler_params=LIMIT,
         name="finish",
-    )(atoms, cotangent, own_grad, from_before, from_after, gain)
+    )(device, atoms, cotangent, own_grad, first, second, gain)
     part, atoms_grad, band_grad = lax.optimization_barrier((part, atoms_grad, band_grad))
     fetched = [part, project, gain, band_gain, weights]
     project_grad, combine_grad, weight_grad, scale_grad, gain_grad = pl.pallas_call(

time: 103 us -> 97.2 us (0.944)
  starting transfers between devices: 53.6 us -> 48.3 us
  waiting for transfers between devices: 12.2 us -> 14.5 us
  blocking collectives: 18.2 us -> 16.6 us
    all_to_all x3 -> x2, starting transfers between devices: 24.4 us -> 20.8 us  [the longest x1 14.4 us: shards(): part = lax.all_to_all(part, 'row', 0, 0, axis_index_groups=far, tiled=True)]
    all_to_all x3 -> x2, waiting for transfers between devices: 12.2 us -> 14.1 us  [the longest x1 8.01 us: shards(): part = lax.all_to_all(part, 'row', 0, 0, axis_index_groups=far, tiled=True)]
    ppermute x4, starting transfers between devices: 20.1 us -> 18.3 us  [the longest x2 12.7 us: shards(): second = lax.ppermute(second, ('row', 'col'), odd_pairs)]
    all_to_all x1, blocking collectives: 18.2 us -> 16.6 us  [shards(): lax.all_to_all(outgoing, ('row', 'col'), 0, 0, axis_index_groups=near, ti...]
  transfers between devices with their start and end apart: 8 -> 7, of which waited for: 3 -> 3; matrix products, arithmetic and copies ran while one was open for 1% -> 1% of each run, Pallas kernels for 3% -> 3%
where the time goes in v5:
time: 97.2 us; the launch traced here: 96.6 us
  starting transfers between devices  48.3 us (50%)
  blocking collectives  16.6 us (17%)
  waiting for transfers between devices  14.5 us (15%)
  Pallas kernels  10.6 us (11%)
  local copies, waits for them, and re-layouts  5.74 us (6%)
    all_to_all x1, blocking collectives, shards(): lax.all_to_all(outgoing, ('row', 'col'), 0, 0, axis_index_groups=near, ti...  16.6 us
    all_to_all x1, starting transfers between devices, shards(): part = lax.all_to_all(part, 'row', 0, 0, axis_index_groups=far, tiled=True)  14.4 us
    ppermute x2, starting transfers between devices, shards(): second = lax.ppermute(second, ('row', 'col'), odd_pairs)  12.7 us
    all_to_all x1, starting transfers between devices, shards(): lax.all_to_all(tiles, 'col', 0, 0, tiled=True).reshape(entries, width)  9.15 us
    all_to_all x1, waiting for transfers between devices, shards(): part = lax.all_to_all(part, 'row', 0, 0, axis_index_groups=far, tiled=True)  8.01 us
    all_to_all x1, starting transfers between devices, shards(): lax.all_to_all(part, ('row', 'col'), 0, 0, axis_index_groups=near, tiled=...  6.38 us
    pallas_call x1, Pallas kernels, shards(): pl.pallas_call(attention_kernel, out_shape=(shape((2 * cols, 24, width),...  6.11 us
    all_to_all x1, waiting for transfers between devices, shards(): lax.all_to_all(part, ('row', 'col'), 0, 0, axis_index_groups=near, tiled=...  6.05 us
  transfers between devices with their start and end apart: 7, of which 3 were waited for; matrix products, arithmetic and copies ran while one was open for 1% of the time, Pallas kernels for 3%

profile of v5, /device:TPU:1, one launch (start us, length us, event | category | flops | bytes accessed | tf_op | source)
XLA Modules:
  0.0 96.6 jit_solution(11383580237874928982)
XLA Ops:
  0.6 1.6 %copy.25 = bf16[16,16,3,128]{3,1,2,0:T(8,128)(2,1)} copy(bf16[16,16,3,128]{3,1,0,2:T(8,128)(2,1)} %bitcast.31) | data formatting | bytes 393216 | tf_op jit(solution)/shard_map/reshape | solution.py:443
  2.3 9.1 %all-to-all-start = ((bf16[16,3,16,128]{3,2,1,0:T(8,128)(2,1)}), bf16[16,3,16,128]{3,2,1,0:T(8,128)(2,1)S(1)}, u32[]{:S(2)}, u32[]{:S(2)}) async-start(bf16[16,3,16,128]{3,2,1,0:T(8,128)(2,1)} %bitcast.17.clone.2), calls=%async_computation | async-start | bytes 393216 | tf_op jit(solution)/shard_map/all_to_all | solution.py:444
  11.4 0.6 copy-done.7
  12.2 3.3 %collective-permute-start = (bf16[5,48,128]{2,1,0:T(8,128)(2,1)S(1)}, bf16[5,48,128]{2,1,0:T(8,128)(2,1)S(1)}, u32[]{:S(2)}, u32[]{:S(2)}) collective-permute-start(bf16[5,48,128]{2,1,0:T(8,128)(2,1)S(1)} %get-tuple-element.29), channel_id=1, source_target_pairs={{0,1},{1,0},{2,3},{3,2},{4,5},{5,4},{6,7},{7,6},{8,9},{9,8},{10,11... | collective-permute-start | bytes 184328 | tf_op jit(solution)/shard_map/ppermute | solution.py:455
  15.4 8.2 %collective-permute-start.1 = (bf16[5,48,128]{2,1,0:T(8,128)(2,1)S(1)}, bf16[5,48,128]{2,1,0:T(8,128)(2,1)S(1)}, u32[]{:S(2)}, u32[]{:S(2)}) collective-permute-start(bf16[5,48,128]{2,1,0:T(8,128)(2,1)S(1)} %get-tuple-element.30), channel_id=1, source_target_pairs={{1,2},{2,1},{3,4},{4,3},{5,6},{6,5},{7,8},{8,7},{9,10},{10,9},{11,... | collective-permute-start | bytes 184328 | tf_op jit(solution)/shard_map/ppermute | solution.py:456
  23.6 0.1 copy.21.key_range
  23.7 0.7 copy-done.5
  24.4 0.7 pair.1
  25.1 0.4 collective-permute-done.1.second
  25.5 0.6 copy-done.4
  26.2 6.1 %attention.1 = (bf16[32,24,128]{2,1,0:T(8,128)(2,1)S(1)}, bf16[4,48,128]{2,1,0:T(8,128)(2,1)S(1)}, bf16[4,48,128]{2,1,0:T(8,128)(2,1)S(1)}, f32[4,128,128]{2,1,0:T(8,128)S(1)}) custom-call(s32[4,2]{1,0:T(4,128)S(1)} %copy.21.key_range, s32[1]{0:T(128)} %bitcast.device, bf16[4,128,128]{2,1,0:T(8,128)(2,1)S(1)} %copy-done, bf16[4,128,128]{2,1,0:T(8,128)(2,1)S(1)} %copy-done.2, ...), custom_call_target="tpu_custom_call" | custom-call | tf_op jit(solution)/shard_map/attention/pallas_call | solution.py:470
  32.3 16.6 %all_to_all.20.scattered = bf16[32,24,128]{2,1,0:T(8,128)(2,1)S(1)} all-to-all(bf16[32,24,128]{2,1,0:T(8,128)(2,1)S(1)} %get-tuple-element.33), channel_id=1, replica_groups={{0,1,2,3,4,5,6,7,8,9,10,11,12,13,14,15,16,17,18,19,20,21,22,23,24,25,26..., dimensions={0} | all-to-all | bytes 393216 | tf_op jit(solution)/shard_map/all_to_all | solution.py:491
  49.0 0.7 broadcast_in_dim.6
  49.6 14.4 %all-to-all-start.2 = ((bf16[16,24,128]{2,1,0:T(8,128)(2,1)}), bf16[16,24,128]{2,1,0:T(8,128)(2,1)S(1)}, u32[]{:S(2)}, u32[]{:S(2)}) async-start(bf16[16,24,128]{2,1,0:T(8,128)(2,1)} %broadcast_in_dim.6), calls=%async_computation.2 | async-start | bytes 196608 | tf_op jit(solution)/shard_map/all_to_all | solution.py:498
  64.1 2.4 %collective-permute-start.2 = (bf16[4,48,128]{2,1,0:T(8,128)(2,1)S(1)}, bf16[4,48,128]{2,1,0:T(8,128)(2,1)S(1)}, u32[]{:S(2)}, u32[]{:S(2)}) collective-permute-start(bf16[4,48,128]{2,1,0:T(8,128)(2,1)S(1)} %get-tuple-element.37), channel_id=1, source_target_pairs={{0,1},{1,0},{2,3},{3,2},{4,5},{5,4},{6,7},{7,6},{8,9},{9,8},{10,11... | collective-permute-start | bytes 147464 | tf_op jit(solution)/shard_map/ppermute | solution.py:499
  66.5 4.5 %collective-permute-start.3 = (bf16[4,48,128]{2,1,0:T(8,128)(2,1)S(1)}, bf16[4,48,128]{2,1,0:T(8,128)(2,1)S(1)}, u32[]{:S(2)}, u32[]{:S(2)}) collective-permute-start(bf16[4,48,128]{2,1,0:T(8,128)(2,1)S(1)} %get-tuple-element.38), channel_id=1, source_target_pairs={{1,2},{2,1},{3,4},{4,3},{5,6},{6,5},{7,8},{8,7},{9,10},{10,9},{11,... | collective-permute-start | bytes 147464 | tf_op jit(solution)/shard_map/ppermute | solution.py:500
  70.9 8.0 %all-to-all-done.2 = bf16[16,24,128]{2,1,0:T(8,128)(2,1)S(1)} async-done(((bf16[16,24,128]{2,1,0:T(8,128)(2,1)}), bf16[16,24,128]{2,1,0:T(8,128)(2,1)S(1)}, u32[]{:S(2)}, u32[]{:S(2)}) %all-to-all-start.2) | async-done | bytes 98336 | tf_op jit(solution)/shard_map/all_to_all | solution.py:498
  79.0 0.7 broadcast_in_dim.7
  79.7 6.4 %all-to-all-start.3 = ((bf16[32,24,128]{2,1,0:T(8,128)(2,1)}), bf16[32,24,128]{2,1,0:T(8,128)(2,1)S(1)}, u32[]{:S(2)}, u32[]{:S(2)}) async-start(bf16[32,24,128]{2,1,0:T(8,128)(2,1)} %broadcast_in_dim.7), calls=%async_computation.3 | async-start | bytes 393216 | tf_op jit(solution)/shard_map/all_to_all | solution.py:504
  86.1 1.5 %band.1 = bf16[768,128]{1,0:T(8,128)(2,1)S(1)} custom-call(s32[1]{0:T(128)} %bitcast.device, bf16[768,128]{1,0:T(8,128)(2,1)} %bitcast.8.band, bf16[32,24,128]{2,1,0:T(8,128)(2,1)S(1)} %all_to_all.20.scattered, f32[1,128]{1,0:T(1,128)S(1)} %bitcast.27, bf16[4,128]{1,0:T(4,128)(2,1)S(1)} %bitcast.24), custom_call_target="tpu_custom_call" | custom-call | tf_op jit(solution)/shard_map/band/pallas_call | solution.py:505
  87.5 0.7 copy.22
  88.2 1.1 %finish.1 = bf16[4,128,128]{2,1,0:T(8,128)(2,1)} custom-call(s32[1]{0:T(128)} %bitcast.device, bf16[4,128,128]{2,1,0:T(8,128)(2,1)S(1)} %copy-done, bf16[4,128,128]{2,1,0:T(8,128)(2,1)S(1)} %copy-done.2, f32[4,128,128]{2,1,0:T(8,128)S(1)} %get-tuple-element.40.own_grad, bf16[4,48,128]{2,1,0:T(8,128)(2,1)S(1)} %collective-permute-done.2.first, ...), custom_call_target="tpu_custom_call" | custom-call | tf_op jit(solution)/shard_map/finish/pallas_call | solution.py:515
  89.3 6.0 %all-to-all-done.3.parts_hbm = bf16[32,24,128]{2,1,0:T(8,128)(2,1)S(1)} async-done(((bf16[32,24,128]{2,1,0:T(8,128)(2,1)}), bf16[32,24,128]{2,1,0:T(8,128)(2,1)S(1)}, u32[]{:S(2)}, u32[]{:S(2)}) %all-to-all-start.3) | async-done | bytes 196640 | tf_op jit(solution)/shard_map/all_to_all | solution.py:504
  95.4 1.2 %last.1 = (bf16[128,512]{1,0:T(8,128)(2,1)}, bf16[128,128]{1,0:T(8,128)(2,1)}, bf16[4,128]{1,0:T(4,128)(2,1)}, f32[1,128]{1,0:T(1,128)}, f32[1,128]{1,0:T(1,128)}) custom-call(bf16[32,24,128]{2,1,0:T(8,128)(2,1)S(1)} %all-to-all-done.3.parts_hbm, bf16[128,512]{1,0:T(8,128)(2,1)S(1)} %copy-done.1, f32[1,128]{1,0:T(1,128)S(1)} %bitcast.22, ...), custom_call_target="tpu_custom_call" | custom-call | tf_op jit(solution)/shard_map/last/pallas_call | solution.py:525
  (22 shorter events, 0.2 us)
Async XLA Ops:
  2.2 9.2 %copy-start = (bf16[4,128,128]{2,1,0:T(8,128)(2,1)S(1)}, bf16[4,128,128]{2,1,0:T(8,128)(2,1)}, u32[]{:S(2)}) copy-start(bf16[4,128,128]{2,1,0:T(8,128)(2,1)} %atoms.3) | copy-start | bytes 393220
  2.3 21.5 %all-to-all-start = ((bf16[16,3,16,128]{3,2,1,0:T(8,128)(2,1)}), bf16[16,3,16,128]{3,2,1,0:T(8,128)(2,1)S(1)}, u32[]{:S(2)}, u32[]{:S(2)}) async-start(bf16[16,3,16,128]{3,2,1,0:T(8,128)(2,1)} %bitcast.17.clone.2), calls=%async_computation | async-start | bytes 393216 | tf_op jit(solution)/shard_map/all_to_all | solution.py:444
  11.4 0.7 copy-start.7
  12.1 11.5 %copy-start.8 = (s32[4,2]{0,1:T(2,128)S(1)}, s32[4,2]{0,1:T(2,128)}, u32[]{:S(2)}) copy-start(s32[4,2]{0,1:T(2,128)} %param.19) | copy-start | bytes 100
  12.2 13.0 %collective-permute-start = (bf16[5,48,128]{2,1,0:T(8,128)(2,1)S(1)}, bf16[5,48,128]{2,1,0:T(8,128)(2,1)S(1)}, u32[]{:S(2)}, u32[]{:S(2)}) collective-permute-start(bf16[5,48,128]{2,1,0:T(8,128)(2,1)S(1)} %get-tuple-element.29), channel_id=1, source_target_pairs={{0,1},{1,0},{2,3},{3,2},{4,5},{5,4},{6,7},{7,6},{8,9},{9,8},{10,11... | collective-permute-start | bytes 184328 | tf_op jit(solution)/shard_map/ppermute | solution.py:455
  15.4 10.1 %collective-permute-start.1 = (bf16[5,48,128]{2,1,0:T(8,128)(2,1)S(1)}, bf16[5,48,128]{2,1,0:T(8,128)(2,1)S(1)}, u32[]{:S(2)}, u32[]{:S(2)}) collective-permute-start(bf16[5,48,128]{2,1,0:T(8,128)(2,1)S(1)} %get-tuple-element.30), channel_id=1, source_target_pairs={{1,2},{2,1},{3,4},{4,3},{5,6},{6,5},{7,8},{8,7},{9,10},{10,9},{11,... | collective-permute-start | bytes 184328 | tf_op jit(solution)/shard_map/ppermute | solution.py:456
  23.7 0.7 copy-start.5
  23.7 0.7 copy-start.6
  24.4 1.1 %copy-start.1 = (bf16[128,512]{1,0:T(8,128)(2,1)S(1)}, bf16[128,512]{1,0:T(8,128)(2,1)}, u32[]{:S(2)}) copy-start(bf16[128,512]{1,0:T(8,128)(2,1)} %project_hbm.3) | copy-start | bytes 393220
  24.4 1.1 %copy-start.2 = (bf16[4,128,128]{2,1,0:T(8,128)(2,1)S(1)}, bf16[4,128,128]{2,1,0:T(8,128)(2,1)}, u32[]{:S(2)}) copy-start(bf16[4,128,128]{2,1,0:T(8,128)(2,1)} %cotangent.1) | copy-start | bytes 393220
  24.4 1.1 %copy-start.3 = (bf16[128,128]{1,0:T(8,128)(2,1)S(1)}, bf16[128,128]{1,0:T(8,128)(2,1)}, u32[]{:S(2)}) copy-start(bf16[128,128]{1,0:T(8,128)(2,1)} %combine_hbm.1) | copy-start | bytes 98308
  25.5 0.7 copy-start.4
  49.6 29.3 %all-to-all-start.2 = ((bf16[16,24,128]{2,1,0:T(8,128)(2,1)}), bf16[16,24,128]{2,1,0:T(8,128)(2,1)S(1)}, u32[]{:S(2)}, u32[]{:S(2)}) async-start(bf16[16,24,128]{2,1,0:T(8,128)(2,1)} %broadcast_in_dim.6), calls=%async_computation.2 | async-start | bytes 196608 | tf_op jit(solution)/shard_map/all_to_all | solution.py:498
  64.1 14.9 %collective-permute-start.2 = (bf16[4,48,128]{2,1,0:T(8,128)(2,1)S(1)}, bf16[4,48,128]{2,1,0:T(8,128)(2,1)S(1)}, u32[]{:S(2)}, u32[]{:S(2)}) collective-permute-start(bf16[4,48,128]{2,1,0:T(8,128)(2,1)S(1)} %get-tuple-element.37), channel_id=1, source_target_pairs={{0,1},{1,0},{2,3},{3,2},{4,5},{5,4},{6,7},{7,6},{8,9},{9,8},{10,11... | collective-permute-start | bytes 147464 | tf_op jit(solution)/shard_map/ppermute | solution.py:499
  66.5 12.5 %collective-permute-start.3 = (bf16[4,48,128]{2,1,0:T(8,128)(2,1)S(1)}, bf16[4,48,128]{2,1,0:T(8,128)(2,1)S(1)}, u32[]{:S(2)}, u32[]{:S(2)}) collective-permute-start(bf16[4,48,128]{2,1,0:T(8,128)(2,1)S(1)} %get-tuple-element.38), channel_id=1, source_target_pairs={{1,2},{2,1},{3,4},{4,3},{5,6},{6,5},{7,8},{8,7},{9,10},{10,9},{11,... | collective-permute-start | bytes 147464 | tf_op jit(solution)/shard_map/ppermute | solution.py:500
  79.7 15.7 %all-to-all-start.3 = ((bf16[32,24,128]{2,1,0:T(8,128)(2,1)}), bf16[32,24,128]{2,1,0:T(8,128)(2,1)S(1)}, u32[]{:S(2)}, u32[]{:S(2)}) async-start(bf16[32,24,128]{2,1,0:T(8,128)(2,1)} %broadcast_in_dim.7), calls=%async_computation.3 | async-start | bytes 393216 | tf_op jit(solution)/shard_map/all_to_all | solution.py:504

commit v6 on v5

--- a/solution.py
+++ b/solution.py
@@ -60,25 +60,28 @@
     return copies
 
 
-def pack_kernel(device, atoms, tokens, first, second, line, sems):
+def start_kernel(device, band, atoms, tokens, tiles, first, second, line, lines, sems):
     samples, count, width = atoms.shape
     odd = device[0] & 1
     low = pl.multiple_of((1 - odd) * (count - RIM), 16)
     high = pl.multiple_of(odd * (count - RIM), 16)
     copies = fetch(
-        [
-            (tokens, line),
+        [(tokens, line)]
+        + [(band.at[k], tiles.at[:, k]) for k in range(band.shape[0])]
+        + [
             (atoms.at[:, pl.ds(low, RIM)], first.at[:samples]),
             (atoms.at[:, pl.ds(high, RIM)], second.at[:samples]),
         ],
-        sems,
+        sems.at[0],
     )
     copies[0].wait()
-    local = jnp.broadcast_to((line[...] - device[0] * 16).astype(F32), (RIM, width)).astype(BF)
-    first[samples] = local
-    second[samples] = local
-    copies[1].wait()
-    copies[2].wait()
+    local = (line[...] - device[0] * 16).astype(F32)
+    lines[...] = jnp.broadcast_to(local, (RIM, width)).astype(BF)
+    copies = copies[1:] + fetch(
+        [(lines, first.at[samples]), (lines, second.at[samples])], sems.at[1]
+    )
+    for copy in copies:
+        copy.wait()
 
 
 def weight_lines(weights):
@@ -104,13 +107,12 @@
     return jnp.where(shown, grad, 0.0).astype(BF)
 
 
-def pair_kernel(band, gain_hbm, weight_hbm, table, pair_norm, gain, weights, sems):
+def pair_kernel(band, gain, weights, atom_gain, tokens, table, pair_norm, atom_gain_out, tokens_out):
     heads = 4
     entries = band.shape[0]
-    copies = fetch([(gain_hbm, gain), (weight_hbm, weights)], sems)
+    atom_gain_out[...] = atom_gain[...]
+    tokens_out[...] = tokens[...]
     hat, _ = norm(band[...].astype(F32))
-    for copy in copies:
-        copy.wait()
     normed = (hat * gain[...]).astype(BF)
     pair_norm[...] = normed
     bias_rows = nt(weight_lines(weights).astype(BF), normed)
@@ -440,33 +442,48 @@
     band_gain = pair_gain.reshape(1, width)
 
     entries = cols * keys * block
-    tiles = jnp.transpose(pair_band.reshape(cols, block, keys, width), (0, 2, 1, 3))
+    tiles, first, second = pl.pallas_call(
+        start_kernel,
+        out_shape=(
+            shape((cols, keys, block, width), BF),
+            shape((samples + 1, RIM, width), BF),
+            shape((samples + 1, RIM, width), BF),
+        ),
+        in_specs=smem(1) + anywhere(3),
+        out_specs=tuple(anywhere(3)),
+        scratch_shapes=[
+            pltpu.VMEM((1, count), jnp.int32),
+            pltpu.VMEM((RIM, width), BF),
+            pltpu.SemaphoreType.DMA((2, 3 + keys)),
+        ],
+        compiler_params=pltpu.CompilerParams(vmem_limit_bytes=60 * 1024 * 1024),
+        name="start",
+    )(
+        device,
+        jnp.transpose(pair_band, (1, 0, 2)).reshape(keys, cols, block, width),
+        atoms,
+        tokens,
+    )
     band = lax.all_to_all(tiles, "col", 0, 0, tiled=True).reshape(entries, width)
 
-    first, second = pl.pallas_call(
-        pack_kernel,
-        out_shape=(shape((samples + 1, RIM, width), BF),) * 2,
-        in_specs=smem(1) + anywhere(2),
-        out_specs=tuple(vmem(2)),
-        scratch_shapes=[pltpu.VMEM((1, count), jnp.int32), pltpu.SemaphoreType.DMA((3,))],
-        compiler_params=LIMIT,
-        name="pack",
-    )(device, atoms, tokens)
     first = lax.ppermute(first, ("row", "col"), pairs)
     second = lax.ppermute(second, ("row", "col"), odd_pairs)
 
-    fetched = [band_gain, weights]
-    table, pair_norm = pl.pallas_call(
+    table, pair_norm, kept_gain, tokens = pl.pallas_call(
         pair_kernel,
-        out_shape=(shape((KW, KW), BF), shape((entries, width), BF)),
-        in_specs=vmem(1) + anywhere(2),
-        out_specs=tuple(vmem(2)),
-        scratch_shapes=copied(fetched),
+        out_shape=(
+            shape((KW, KW), BF),
+            shape((entries, width), BF),
+            shape(gain.shape, F32),
+            shape(tokens.shape, jnp.int32),
+        ),
+        in_specs=vmem(5),
+        out_specs=tuple(vmem(4)),
         cost_estimate=pl.CostEstimate(flops=10**9, bytes_accessed=10**7, transcendentals=0),
         compiler_params=LIMIT,
         name="pair",
-    )(band, *fetched)
-    fetched = [atoms, cotangent, project, combine, gain, tokens]
+    )(band, band_gain, weights, gain, tokens)
+    fetched = [atoms, cotangent, project, combine, kept_gain, tokens]
     outgoing, first, second, own_grad = pl.pallas_call(
         attention_kernel,
         out_shape=(

time: 97.2 us -> 105 us (1.080)
  Pallas kernels: 10.6 us -> 19.7 us
  local copies, waits for them, and re-layouts: 5.74 us -> 2.86 us
    pallas_call x1, Pallas kernels: 0.06 us -> 10.2 us  [shards(): pl.pallas_call(start_kernel, out_shape=(shape((cols, keys, block, width),...]
    reshape x1 -> x0, local copies, waits for them, and re-layouts: 1.62 us -> none  [shards(): pair_band.reshape(cols, block, keys, width)]
    unnamed x19 -> x25, local copies, waits for them, and re-layouts: 2.08 us -> 0.82 us
  transfers between devices with their start and end apart: 7 -> 7, of which waited for: 3 -> 3; matrix products, arithmetic and copies ran while one was open for 1% -> 1% of each run, Pallas kernels for 3% -> 2%
where the time goes in v6:
time: 105 us; the launch traced here: 104 us
  starting transfers between devices  48.4 us (46%)
  Pallas kernels  19.7 us (19%)
  blocking collectives  16.6 us (16%)
  waiting for transfers between devices  15.4 us (15%)
  local copies, waits for them, and re-layouts  2.86 us (3%)
    all_to_all x1, blocking collectives, shards(): lax.all_to_all(outgoing, ('row', 'col'), 0, 0, axis_index_groups=near, ti...  16.6 us
    all_to_all x1, starting transfers between devices, shards(): part = lax.all_to_all(part, 'row', 0, 0, axis_index_groups=far, tiled=True)  14.4 us
    ppermute x2, starting transfers between devices, shards(): second = lax.ppermute(second, ('row', 'col'), odd_pairs)  12.7 us
    pallas_call x1, Pallas kernels, shards(): pl.pallas_call(start_kernel, out_shape=(shape((cols, keys, block, width),...  10.2 us
    all_to_all x1, starting transfers between devices, shards(): lax.all_to_all(tiles, 'col', 0, 0, tiled=True).reshape(entries, width)  9.16 us
    all_to_all x1, waiting for transfers between devices, shards(): part = lax.all_to_all(part, 'row', 0, 0, axis_index_groups=far, tiled=True)  8.01 us
    all_to_all x1, waiting for transfers between devices, shards(): lax.all_to_all(part, ('row', 'col'), 0, 0, axis_index_groups=near, tiled=...  6.96 us
    all_to_all x1, starting transfers between devices, shards(): lax.all_to_all(part, ('row', 'col'), 0, 0, axis_index_groups=near, tiled=...  6.51 us
  transfers between devices with their start and end apart: 7, of which 3 were waited for; matrix products, arithmetic and copies ran while one was open for 1% of the time, Pallas kernels for 2%

profile of v6, /device:TPU:1, one launch (start us, length us, event | category | flops | bytes accessed | tf_op | source)
XLA Modules:
  0.0 104.0 jit_solution(7391252316350009136)
XLA Ops:
  0.6 10.2 %start.1 = (bf16[16,3,16,128]{3,2,1,0:T(8,128)(2,1)}, bf16[5,48,128]{2,1,0:T(8,128)(2,1)}, bf16[5,48,128]{2,1,0:T(8,128)(2,1)}) custom-call(s32[1]{0:T(128)} %bitcast.device, bf16[3,16,16,128]{3,2,1,0:T(8,128)(2,1)} %bitcast.31, bf16[4,128,128]{2,1,0:T(8,128)(2,1)} %atoms.3, s32[1,128]{1,0:T(1,128)} %bitcast.29), custom_call_target="tpu_custom_call" | custom-call | tf_op jit(solution)/shard_map/start/pallas_call | solution.py:445
  10.8 9.2 %all-to-all-start = ((bf16[16,3,16,128]{3,2,1,0:T(8,128)(2,1)}), bf16[16,3,16,128]{3,2,1,0:T(8,128)(2,1)S(1)}, u32[]{:S(2)}, u32[]{:S(2)}) async-start(bf16[16,3,16,128]{3,2,1,0:T(8,128)(2,1)} %get-tuple-element.32), calls=%async_computation | async-start | bytes 393216 | tf_op jit(solution)/shard_map/all_to_all | solution.py:467
  20.0 3.3 %collective-permute-start = (bf16[5,48,128]{2,1,0:T(8,128)(2,1)S(1)}, bf16[5,48,128]{2,1,0:T(8,128)(2,1)S(1)}, u32[]{:S(2)}, u32[]{:S(2)}) collective-permute-start(bf16[5,48,128]{2,1,0:T(8,128)(2,1)S(1)} %copy-done.11), channel_id=1, source_target_pairs={{0,1},{1,0},{2,3},{3,2},{4,5},{5,4},{6,7},{7,6},{8,9},{9,8},{10,11... | collective-permute-start | bytes 184328 | tf_op jit(solution)/shard_map/ppermute | solution.py:469
  23.3 8.2 %collective-permute-start.1 = (bf16[5,48,128]{2,1,0:T(8,128)(2,1)S(1)}, bf16[5,48,128]{2,1,0:T(8,128)(2,1)S(1)}, u32[]{:S(2)}, u32[]{:S(2)}) collective-permute-start(bf16[5,48,128]{2,1,0:T(8,128)(2,1)S(1)} %copy-done.10), channel_id=1, source_target_pairs={{1,2},{2,1},{3,4},{4,3},{5,6},{6,5},{7,8},{8,7},{9,10},{10,9},{11,... | collective-permute-start | bytes 184328 | tf_op jit(solution)/shard_map/ppermute | solution.py:470
  31.5 0.1 copy.19.key_range
  31.6 0.5 copy-done.7
  32.2 0.0 copy-done.8
  32.2 0.1 copy-done.5
  32.3 0.6 pair.1
  32.9 0.5 collective-permute-done.1.second
  33.4 6.1 %attention.1 = (bf16[32,24,128]{2,1,0:T(8,128)(2,1)S(1)}, bf16[4,48,128]{2,1,0:T(8,128)(2,1)S(1)}, bf16[4,48,128]{2,1,0:T(8,128)(2,1)S(1)}, f32[4,128,128]{2,1,0:T(8,128)S(1)}) custom-call(s32[4,2]{1,0:T(4,128)S(1)} %copy.19.key_range, s32[1]{0:T(128)} %bitcast.device, bf16[4,128,128]{2,1,0:T(8,128)(2,1)S(1)} %copy-done, bf16[4,128,128]{2,1,0:T(8,128)(2,1)S(1)} %copy-done.3, ...), custom_call_target="tpu_custom_call" | custom-call | tf_op jit(solution)/shard_map/attention/pallas_call | solution.py:487
  39.5 16.6 %all_to_all.20.scattered = bf16[32,24,128]{2,1,0:T(8,128)(2,1)S(1)} all-to-all(bf16[32,24,128]{2,1,0:T(8,128)(2,1)S(1)} %get-tuple-element.39), channel_id=1, replica_groups={{0,1,2,3,4,5,6,7,8,9,10,11,12,13,14,15,16,17,18,19,20,21,22,23,24,25,26..., dimensions={0} | all-to-all | bytes 393216 | tf_op jit(solution)/shard_map/all_to_all | solution.py:508
  56.2 0.7 broadcast_in_dim.6
  56.9 14.4 %all-to-all-start.2 = ((bf16[16,24,128]{2,1,0:T(8,128)(2,1)}), bf16[16,24,128]{2,1,0:T(8,128)(2,1)S(1)}, u32[]{:S(2)}, u32[]{:S(2)}) async-start(bf16[16,24,128]{2,1,0:T(8,128)(2,1)} %broadcast_in_dim.6), calls=%async_computation.2 | async-start | bytes 196608 | tf_op jit(solution)/shard_map/all_to_all | solution.py:515
  71.3 2.4 %collective-permute-start.2 = (bf16[4,48,128]{2,1,0:T(8,128)(2,1)S(1)}, bf16[4,48,128]{2,1,0:T(8,128)(2,1)S(1)}, u32[]{:S(2)}, u32[]{:S(2)}) collective-permute-start(bf16[4,48,128]{2,1,0:T(8,128)(2,1)S(1)} %get-tuple-element.43), channel_id=1, source_target_pairs={{0,1},{1,0},{2,3},{3,2},{4,5},{5,4},{6,7},{7,6},{8,9},{9,8},{10,11... | collective-permute-start | bytes 147464 | tf_op jit(solution)/shard_map/ppermute | solution.py:516
  73.7 4.5 %collective-permute-start.3 = (bf16[4,48,128]{2,1,0:T(8,128)(2,1)S(1)}, bf16[4,48,128]{2,1,0:T(8,128)(2,1)S(1)}, u32[]{:S(2)}, u32[]{:S(2)}) collective-permute-start(bf16[4,48,128]{2,1,0:T(8,128)(2,1)S(1)} %get-tuple-element.44), channel_id=1, source_target_pairs={{1,2},{2,1},{3,4},{4,3},{5,6},{6,5},{7,8},{8,7},{9,10},{10,9},{11,... | collective-permute-start | bytes 147464 | tf_op jit(solution)/shard_map/ppermute | solution.py:517
  78.2 8.0 %all-to-all-done.2 = bf16[16,24,128]{2,1,0:T(8,128)(2,1)S(1)} async-done(((bf16[16,24,128]{2,1,0:T(8,128)(2,1)}), bf16[16,24,128]{2,1,0:T(8,128)(2,1)S(1)}, u32[]{:S(2)}, u32[]{:S(2)}) %all-to-all-start.2) | async-done | bytes 98336 | tf_op jit(solution)/shard_map/all_to_all | solution.py:515
  86.2 0.7 broadcast_in_dim.7
  86.9 6.5 %all-to-all-start.3 = ((bf16[32,24,128]{2,1,0:T(8,128)(2,1)}), bf16[32,24,128]{2,1,0:T(8,128)(2,1)S(1)}, u32[]{:S(2)}, u32[]{:S(2)}) async-start(bf16[32,24,128]{2,1,0:T(8,128)(2,1)} %broadcast_in_dim.7), calls=%async_computation.3 | async-start | bytes 393216 | tf_op jit(solution)/shard_map/all_to_all | solution.py:521
  93.4 0.5 band.1
  94.0 0.7 copy.20
  94.7 1.1 %finish.1 = bf16[4,128,128]{2,1,0:T(8,128)(2,1)} custom-call(s32[1]{0:T(128)} %bitcast.device, bf16[4,128,128]{2,1,0:T(8,128)(2,1)S(1)} %copy-done, bf16[4,128,128]{2,1,0:T(8,128)(2,1)S(1)} %copy-done.3, f32[4,128,128]{2,1,0:T(8,128)S(1)} %get-tuple-element.46.own_grad, bf16[4,48,128]{2,1,0:T(8,128)(2,1)S(1)} %collective-permute-done.2.first, ...), custom_call_target="tpu_custom_call" | custom-call | tf_op jit(solution)/shard_map/finish/pallas_call | solution.py:532
  95.8 7.0 %all-to-all-done.3.parts_hbm = bf16[32,24,128]{2,1,0:T(8,128)(2,1)S(1)} async-done(((bf16[32,24,128]{2,1,0:T(8,128)(2,1)}), bf16[32,24,128]{2,1,0:T(8,128)(2,1)S(1)}, u32[]{:S(2)}, u32[]{:S(2)}) %all-to-all-start.3) | async-done | bytes 196640 | tf_op jit(solution)/shard_map/all_to_all | solution.py:521
  102.8 1.2 %last.1 = (bf16[128,512]{1,0:T(8,128)(2,1)}, bf16[128,128]{1,0:T(8,128)(2,1)}, bf16[4,128]{1,0:T(4,128)(2,1)}, f32[1,128]{1,0:T(1,128)}, f32[1,128]{1,0:T(1,128)}) custom-call(bf16[32,24,128]{2,1,0:T(8,128)(2,1)S(1)} %all-to-all-done.3.parts_hbm, bf16[128,512]{1,0:T(8,128)(2,1)S(1)} %copy-done.2, f32[1,128]{1,0:T(1,128)S(1)} %bitcast.28, ...), custom_call_target="tpu_custom_call" | custom-call | tf_op jit(solution)/shard_map/last/pallas_call | solution.py:542
  (27 shorter events, 0.1 us)
Async XLA Ops:
  10.8 9.2 %copy-start.11 = (bf16[5,48,128]{2,1,0:T(8,128)(2,1)S(1)}, bf16[5,48,128]{2,1,0:T(8,128)(2,1)}, u32[]{:S(2)}) copy-start(bf16[5,48,128]{2,1,0:T(8,128)(2,1)} %get-tuple-element.35) | copy-start | bytes 184324
  10.8 12.5 %copy-start.10 = (bf16[5,48,128]{2,1,0:T(8,128)(2,1)S(1)}, bf16[5,48,128]{2,1,0:T(8,128)(2,1)}, u32[]{:S(2)}) copy-start(bf16[5,48,128]{2,1,0:T(8,128)(2,1)} %get-tuple-element.36) | copy-start | bytes 184324
  10.8 20.8 %all-to-all-start = ((bf16[16,3,16,128]{3,2,1,0:T(8,128)(2,1)}), bf16[16,3,16,128]{3,2,1,0:T(8,128)(2,1)S(1)}, u32[]{:S(2)}, u32[]{:S(2)}) async-start(bf16[16,3,16,128]{3,2,1,0:T(8,128)(2,1)} %get-tuple-element.32), calls=%async_computation | async-start | bytes 393216 | tf_op jit(solution)/shard_map/all_to_all | solution.py:467
  20.0 11.5 %copy-start.9 = (s32[4,2]{0,1:T(2,128)S(1)}, s32[4,2]{0,1:T(2,128)}, u32[]{:S(2)}) copy-start(s32[4,2]{0,1:T(2,128)} %param.19) | copy-start | bytes 100
  20.0 12.9 %collective-permute-start = (bf16[5,48,128]{2,1,0:T(8,128)(2,1)S(1)}, bf16[5,48,128]{2,1,0:T(8,128)(2,1)S(1)}, u32[]{:S(2)}, u32[]{:S(2)}) collective-permute-start(bf16[5,48,128]{2,1,0:T(8,128)(2,1)S(1)} %copy-done.11), channel_id=1, source_target_pairs={{0,1},{1,0},{2,3},{3,2},{4,5},{5,4},{6,7},{7,6},{8,9},{9,8},{10,11... | collective-permute-start | bytes 184328 | tf_op jit(solution)/shard_map/ppermute | solution.py:469
  23.3 10.1 %collective-permute-start.1 = (bf16[5,48,128]{2,1,0:T(8,128)(2,1)S(1)}, bf16[5,48,128]{2,1,0:T(8,128)(2,1)S(1)}, u32[]{:S(2)}, u32[]{:S(2)}) collective-permute-start(bf16[5,48,128]{2,1,0:T(8,128)(2,1)S(1)} %copy-done.10), channel_id=1, source_target_pairs={{1,2},{2,1},{3,4},{4,3},{5,6},{6,5},{7,8},{8,7},{9,10},{10,9},{11,... | collective-permute-start | bytes 184328 | tf_op jit(solution)/shard_map/ppermute | solution.py:470
  31.5 0.7 copy-start.7
  31.5 0.7 copy-start.8
  31.6 0.7 copy-start.5
  31.6 0.7 copy-start.6
  32.3 1.1 %copy-start = (bf16[4,128,128]{2,1,0:T(8,128)(2,1)S(1)}, bf16[4,128,128]{2,1,0:T(8,128)(2,1)}, u32[]{:S(2)}) copy-start(bf16[4,128,128]{2,1,0:T(8,128)(2,1)} %atoms.3) | copy-start | bytes 393220
  32.3 1.1 %copy-start.2 = (bf16[128,512]{1,0:T(8,128)(2,1)S(1)}, bf16[128,512]{1,0:T(8,128)(2,1)}, u32[]{:S(2)}) copy-start(bf16[128,512]{1,0:T(8,128)(2,1)} %project_hbm.3) | copy-start | bytes 393220
  32.3 1.1 %copy-start.3 = (bf16[4,128,128]{2,1,0:T(8,128)(2,1)S(1)}, bf16[4,128,128]{2,1,0:T(8,128)(2,1)}, u32[]{:S(2)}) copy-start(bf16[4,128,128]{2,1,0:T(8,128)(2,1)} %cotangent.1) | copy-start | bytes 393220
  32.3 1.1 %copy-start.4 = (bf16[128,128]{1,0:T(8,128)(2,1)S(1)}, bf16[128,128]{1,0:T(8,128)(2,1)}, u32[]{:S(2)}) copy-start(bf16[128,128]{1,0:T(8,128)(2,1)} %combine_hbm.1) | copy-start | bytes 98308
  56.9 29.3 %all-to-all-start.2 = ((bf16[16,24,128]{2,1,0:T(8,128)(2,1)}), bf16[16,24,128]{2,1,0:T(8,128)(2,1)S(1)}, u32[]{:S(2)}, u32[]{:S(2)}) async-start(bf16[16,24,128]{2,1,0:T(8,128)(2,1)} %broadcast_in_dim.6), calls=%async_computation.2 | async-start | bytes 196608 | tf_op jit(solution)/shard_map/all_to_all | solution.py:515
  71.3 14.9 %collective-permute-start.2 = (bf16[4,48,128]{2,1,0:T(8,128)(2,1)S(1)}, bf16[4,48,128]{2,1,0:T(8,128)(2,1)S(1)}, u32[]{:S(2)}, u32[]{:S(2)}) collective-permute-start(bf16[4,48,128]{2,1,0:T(8,128)(2,1)S(1)} %get-tuple-element.43), channel_id=1, source_target_pairs={{0,1},{1,0},{2,3},{3,2},{4,5},{5,4},{6,7},{7,6},{8,9},{9,8},{10,11... | collective-permute-start | bytes 147464 | tf_op jit(solution)/shard_map/ppermute | solution.py:516
  73.7 12.5 %collective-permute-start.3 = (bf16[4,48,128]{2,1,0:T(8,128)(2,1)S(1)}, bf16[4,48,128]{2,1,0:T(8,128)(2,1)S(1)}, u32[]{:S(2)}, u32[]{:S(2)}) collective-permute-start(bf16[4,48,128]{2,1,0:T(8,128)(2,1)S(1)} %get-tuple-element.44), channel_id=1, source_target_pairs={{1,2},{2,1},{3,4},{4,3},{5,6},{6,5},{7,8},{8,7},{9,10},{10,9},{11,... | collective-permute-start | bytes 147464 | tf_op jit(solution)/shard_map/ppermute | solution.py:517
  86.9 6.5 %copy-start.1 = (bf16[16,3,16,128]{3,2,1,0:T(8,128)(2,1)S(1)}, bf16[16,3,16,128]{3,2,1,0:T(8,128)(2,1)}, u32[]{:S(2)}) copy-start(bf16[16,3,16,128]{3,2,1,0:T(8,128)(2,1)} %get-tuple-element.32) | copy-start | bytes 589828
  86.9 15.9 %all-to-all-start.3 = ((bf16[32,24,128]{2,1,0:T(8,128)(2,1)}), bf16[32,24,128]{2,1,0:T(8,128)(2,1)S(1)}, u32[]{:S(2)}, u32[]{:S(2)}) async-start(bf16[32,24,128]{2,1,0:T(8,128)(2,1)} %broadcast_in_dim.7), calls=%async_computation.3 | async-start | bytes 393216 | tf_op jit(solution)/shard_map/all_to_all | solution.py:521

commit v7 on v6

--- a/solution.py
+++ b/solution.py
@@ -60,7 +60,7 @@
     return copies
 
 
-def start_kernel(device, band, atoms, tokens, tiles, first, second, line, lines, sems):
+def start_kernel(device, band, atoms, tokens, tiles, first, second, line, sems):
     samples, count, width = atoms.shape
     odd = device[0] & 1
     low = pl.multiple_of((1 - odd) * (count - RIM), 16)
@@ -72,15 +72,13 @@
             (atoms.at[:, pl.ds(low, RIM)], first.at[:samples]),
             (atoms.at[:, pl.ds(high, RIM)], second.at[:samples]),
         ],
-        sems.at[0],
+        sems,
     )
     copies[0].wait()
-    local = (line[...] - device[0] * 16).astype(F32)
-    lines[...] = jnp.broadcast_to(local, (RIM, width)).astype(BF)
-    copies = copies[1:] + fetch(
-        [(lines, first.at[samples]), (lines, second.at[samples])], sems.at[1]
-    )
-    for copy in copies:
+    local = jnp.broadcast_to((line[...] - device[0] * 16).astype(F32), (RIM, width)).astype(BF)
+    first[samples] = local
+    second[samples] = local
+    for copy in copies[1:]:
         copy.wait()
 
 
@@ -125,13 +123,35 @@
     table[...] = nn(both, spread_slots(entries)).astype(BF)
 
 
+def middle_kernel(device, scattered, outgoing):
+    width = scattered.shape[2]
+    total = scattered[0].astype(F32)
+    for p in range(1, scattered.shape[0]):
+        total = total + scattered[p].astype(F32)
+    first = ((device[0] >> 7) & 3) * 8 + ((device[0] >> 4) & 1) * 4
+    blocks = [scattered[first + x].astype(F32)[24:32] for x in range(4)]
+    turned = [pltpu.roll(b, 64, 1) for b in blocks]
+    left = iota((8, width), 1) < 64
+    for z_lo in range(4):
+        rows = slice(3 * (z_lo // 2), 3 * (z_lo // 2) + 3)
+        lows, highs = (blocks, turned) if z_lo % 2 == 0 else (turned, blocks)
+        pairs = [jnp.where(left, lows[x], highs[x + 1])[rows] for x in (0, 2)]
+        tables = pairs + [jnp.zeros((2, width), F32)]
+        result = jnp.concatenate([total[:24]] + tables, axis=0).astype(BF)
+        for z_hi in range(4):
+            outgoing[z_hi * 4 + z_lo] = result
+
+
 def band_kernel(device, band, scattered, pair_gain, weights, band_grad):
     entries = band.shape[0]
     width = band.shape[1]
-    peers = scattered.shape[0] // 2
-    core = (device[0] // peers) & 1
-    rows = [scattered[core * peers + c].astype(F32)[20:23] for c in range(peers)]
-    rows = jnp.concatenate(rows + [jnp.zeros((KW - 3 * len(rows), width), F32)], axis=0).astype(BF)
+    z_hi = (device[0] >> 5) & 3
+    rows = []
+    for z_lo in range(4):
+        block = scattered[z_hi * 4 + z_lo].astype(F32)[24:32]
+        turned = pltpu.roll(block, 64, 1)
+        rows = rows + [block[:3], turned[:3], block[3:6], turned[3:6]]
+    rows = jnp.concatenate(rows + [jnp.zeros((KW - 48, width), F32)], axis=0).astype(BF)
     hat, inv = norm(band[...].astype(F32))
     norm_grad = nn(entry_grads(rows, entries), weight_spread(weights)).astype(BF).astype(F32)
     band_grad[...] = norm_back(norm_grad * pair_gain[...], hat, inv).astype(BF)
@@ -314,18 +334,24 @@
         table_grad = table_grad + nt(high, rows) + nt(low, rows)
     entry_grad = entry_grads(table_grad.astype(BF), entries)
     weight_part = tn(entry_grad, pair_norm[...])
+    left = iota((3, width), 1) < 64
+    tables = []
+    for x in range(4):
+        by_z = [table_grad[3 * (4 * z + x) : 3 * (4 * z + x) + 3] for z in range(4)]
+        pairs = [jnp.where(left, by_z[z], by_z[z + 1]) for z in (0, 2)]
+        tables.append(jnp.concatenate(pairs + [jnp.zeros((2, width), F32)], axis=0))
     peers = outgoing.shape[0]
     for p in range(peers):
         part, row = divmod(16 * p, width)
         weight_row = jnp.zeros((1, width), F32)
         if p < heads:
             weight_row = jnp.sum(weight_part[p * 16 : (p + 1) * 16], axis=0, keepdims=True)
-        slot = 3 * (p % (peers // 2))
         parts = [
             project_sum[row : row + 16, part * width : (part + 1) * width],
             combine_sum[4 * p : 4 * p + 4],
-            table_grad[slot : slot + 3],
             weight_row,
+            jnp.zeros((3, width), F32),
+            tables[p % 4],
         ]
         outgoing[p] = jnp.concatenate(parts, axis=0).astype(BF)
 
@@ -372,7 +398,7 @@
     combine_grad[...] = jnp.concatenate([x[16:20] for x in chunks], axis=0).astype(BF)
     dots = jnp.transpose(jnp.broadcast_to(dots, (width, width)))[:1]
     scale_grad[...] = dots / atom_gain[...]
-    tail = jnp.concatenate([x[23:24] for x in chunks[:4]], axis=0)
+    tail = jnp.concatenate([x[20:21] for x in chunks[:4]], axis=0)
     weight_grad[...] = tail.astype(BF)
     dots = jnp.sum(tail * weights[...].astype(F32), axis=0, keepdims=True)
     gain_grad[...] = dots / pair_gain[...]
@@ -423,8 +449,8 @@
     key_range,
 ):
     samples, count, width = atoms.shape
-    rows, cols = lax.axis_size("row"), lax.axis_size("col")
-    peers = rows * cols
+    cols = lax.axis_size("col")
+    peers = lax.axis_size("row") * cols
     device = lax.axis_index(("row", "col"))
     windows = count // QW
     block = pair_band.shape[0] // cols
@@ -450,11 +476,10 @@
             shape((samples + 1, RIM, width), BF),
         ),
         in_specs=smem(1) + anywhere(3),
-        out_specs=tuple(anywhere(3)),
+        out_specs=tuple(vmem(3)),
         scratch_shapes=[
             pltpu.VMEM((1, count), jnp.int32),
-            pltpu.VMEM((RIM, width), BF),
-            pltpu.SemaphoreType.DMA((2, 3 + keys)),
+            pltpu.SemaphoreType.DMA((3 + keys,)),
         ],
         compiler_params=pltpu.CompilerParams(vmem_limit_bytes=60 * 1024 * 1024),
         name="start",
@@ -487,7 +512,7 @@
     outgoing, first, second, own_grad = pl.pallas_call(
         attention_kernel,
         out_shape=(
-            shape((2 * cols, 24, width), BF),
+            shape((32, 32, width), BF),
             shape((samples, RIM, width), BF),
             shape((samples, RIM, width), BF),
             shape((samples, count, width), F32),
@@ -503,22 +528,40 @@
         name="attention",
     )(key_range, device, *fetched, first, second, table, pair_norm)
 
-    near = [list(range(i, i + 2 * cols)) for i in range(0, peers, 2 * cols)]
-    far = [list(range(i, rows, 2)) for i in range(2)]
-    scattered = lax.all_to_all(
-        outgoing, ("row", "col"), 0, 0, axis_index_groups=near, tiled=True
-    )
-    part = jnp.sum(scattered.astype(F32), axis=0).astype(BF)
+    def place(y, z_hi, core, z_lo, x):
+        return ((y * 4 + z_hi) * 2 + core) * 16 + z_lo * 4 + x
+
+    four = range(4)
+    planes = [
+        [place(y, z_hi, core, z_lo, x) for y in four for core in range(2) for x in four]
+        for z_hi in four
+        for z_lo in four
+    ]
+    lines = [
+        [place(y, z_hi, core, z_lo, x) for z_hi in four for z_lo in four]
+        for y in four
+        for core in range(2)
+        for x in four
+    ]
+    axes = ("row", "col")
+    part = lax.all_to_all(outgoing, axes, 0, 0, axis_index_groups=planes, tiled=True)
+    part = pl.pallas_call(
+        middle_kernel,
+        out_shape=shape((16, 32, width), BF),
+        in_specs=smem(1) + vmem(1),
+        out_specs=pl.BlockSpec(memory_space=pltpu.VMEM),
+        compiler_params=LIMIT,
+        name="middle",
+    )(device, part)
 
     part, first, second = lax.optimization_barrier((part, first, second))
-    part = jnp.broadcast_to(part, (rows // 2,) + part.shape)
-    part = lax.all_to_all(part, "row", 0, 0, axis_index_groups=far, tiled=True)
+    scattered = lax.all_to_all(part, axes, 0, 0, axis_index_groups=lines, tiled=True)
     first = lax.ppermute(first, ("row", "col"), pairs)
     second = lax.ppermute(second, ("row", "col"), odd_pairs)
-    part = jnp.sum(part.astype(F32), axis=0).astype(BF)
+    part = jnp.sum(scattered[:, :24].astype(F32), axis=0).astype(BF)
     part, first, second = lax.optimization_barrier((part, first, second))
-    part = jnp.broadcast_to(part, (2 * cols,) + part.shape)
-    part = lax.all_to_all(part, ("row", "col"), 0, 0, axis_index_groups=near, tiled=True)
+    part = jnp.broadcast_to(part, (32,) + part.shape)
+    part = lax.all_to_all(part, axes, 0, 0, axis_index_groups=planes, tiled=True)
     band_grad = pl.pallas_call(
         band_kernel,
         out_shape=shape((entries, width), BF),

time: 105 us -> 89.6 us (0.85)
  Pallas kernels: 19.7 us -> 12 us
  waiting for transfers between devices: 15.4 us -> 9.55 us
    pallas_call x1, Pallas kernels: 10.2 us -> 1.7 us  [shards(): pl.pallas_call(start_kernel, out_shape=(shape((cols, keys, block, width),...]
    all_to_all x2, waiting for transfers between devices: 15 us -> 8.95 us  [the longest x1 5.83 us: shards(): lax.all_to_all(part, axes, 0, 0, axis_index_groups=planes, tiled=True)]
    all_to_all x2, starting transfers between devices: 21 us -> 17.9 us  [the longest x1 11.1 us: shards(): lax.all_to_all(part, axes, 0, 0, axis_index_groups=lines, tiled=True)]
    ppermute x2, starting transfers between devices: 12.7 us -> 15 us  [shards(): second = lax.ppermute(second, ('row', 'col'), odd_pairs)]
    pallas_call x1 -> x2, Pallas kernels: 6.13 us -> 6.87 us  [the longest x1 6.13 us: shards(): pl.pallas_call(attention_kernel, out_shape=(shape((32, 32, width), BF), s...]
  transfers between devices with their start and end apart: 7 -> 7, of which waited for: 3 -> 4; matrix products, arithmetic and copies ran while one was open for 1% -> 1% of each run, Pallas kernels for 2% -> 3%
where the time goes in v7:
time: 89.6 us; the launch traced here: 89 us
  starting transfers between devices  47.5 us (53%)
  blocking collectives  16.8 us (19%)
  Pallas kernels  12 us (13%)
  waiting for transfers between devices  9.55 us (11%)
  local copies, waits for them, and re-layouts  2.21 us (2%)
    all_to_all x1, blocking collectives, shards(): lax.all_to_all(outgoing, axes, 0, 0, axis_index_groups=planes, tiled=True)  16.8 us
    ppermute x2, starting transfers between devices, shards(): second = lax.ppermute(second, ('row', 'col'), odd_pairs)  15 us
    all_to_all x1, starting transfers between devices, shards(): lax.all_to_all(part, axes, 0, 0, axis_index_groups=lines, tiled=True)  11.1 us
    all_to_all x1, starting transfers between devices, shards(): lax.all_to_all(tiles, 'col', 0, 0, tiled=True).reshape(entries, width)  9.16 us
    all_to_all x1, starting transfers between devices, shards(): lax.all_to_all(part, axes, 0, 0, axis_index_groups=planes, tiled=True)  6.76 us
    pallas_call x1, Pallas kernels, shards(): pl.pallas_call(attention_kernel, out_shape=(shape((32, 32, width), BF), s...  6.13 us
    all_to_all x1, waiting for transfers between devices, shards(): lax.all_to_all(part, axes, 0, 0, axis_index_groups=planes, tiled=True)  5.83 us
    ppermute x2, starting transfers between devices, shards(): first = lax.ppermute(first, ('row', 'col'), pairs)  5.47 us
  transfers between devices with their start and end apart: 7, of which 4 were waited for; matrix products, arithmetic and copies ran while one was open for 1% of the time, Pallas kernels for 3%

profile of v7, /device:TPU:1, one launch (start us, length us, event | category | flops | bytes accessed | tf_op | source)
XLA Modules:
  0.0 89.0 jit_solution(9441008826764975462)
XLA Ops:
  0.6 1.7 %start.1 = (bf16[16,3,16,128]{3,2,1,0:T(8,128)(2,1)}, bf16[5,48,128]{2,1,0:T(8,128)(2,1)}, bf16[5,48,128]{2,1,0:T(8,128)(2,1)}) custom-call(s32[1]{0:T(128)} %bitcast.device, bf16[3,16,16,128]{3,2,1,0:T(8,128)(2,1)} %bitcast.31, bf16[4,128,128]{2,1,0:T(8,128)(2,1)} %atoms.3, s32[1,128]{1,0:T(1,128)} %bitcast.29), custom_call_target="tpu_custom_call" | custom-call | tf_op jit(solution)/shard_map/start/pallas_call | solution.py:471
  2.4 9.2 %all-to-all-start = ((bf16[16,3,16,128]{3,2,1,0:T(8,128)(2,1)}), bf16[16,3,16,128]{3,2,1,0:T(8,128)(2,1)S(1)}, u32[]{:S(2)}, u32[]{:S(2)}) async-start(bf16[16,3,16,128]{3,2,1,0:T(8,128)(2,1)} %get-tuple-element.32), calls=%async_computation | async-start | bytes 393216 | tf_op jit(solution)/shard_map/all_to_all | solution.py:492
  11.6 3.3 %collective-permute-start = (bf16[5,48,128]{2,1,0:T(8,128)(2,1)S(1)}, bf16[5,48,128]{2,1,0:T(8,128)(2,1)S(1)}, u32[]{:S(2)}, u32[]{:S(2)}) collective-permute-start(bf16[5,48,128]{2,1,0:T(8,128)(2,1)S(1)} %copy-done.11), channel_id=1, source_target_pairs={{0,1},{1,0},{2,3},{3,2},{4,5},{5,4},{6,7},{7,6},{8,9},{9,8},{10,11... | collective-permute-start | bytes 184328 | tf_op jit(solution)/shard_map/ppermute | solution.py:494
  14.8 8.2 %collective-permute-start.1 = (bf16[5,48,128]{2,1,0:T(8,128)(2,1)S(1)}, bf16[5,48,128]{2,1,0:T(8,128)(2,1)S(1)}, u32[]{:S(2)}, u32[]{:S(2)}) collective-permute-start(bf16[5,48,128]{2,1,0:T(8,128)(2,1)S(1)} %copy-done.10), channel_id=1, source_target_pairs={{1,2},{2,1},{3,4},{4,3},{5,6},{6,5},{7,8},{8,7},{9,10},{10,9},{11,... | collective-permute-start | bytes 184328 | tf_op jit(solution)/shard_map/ppermute | solution.py:495
  23.1 0.1 copy.17.key_range
  23.2 0.5 copy-done.7
  23.7 0.1 copy-done.5
  23.9 0.6 pair.1
  24.5 0.5 collective-permute-done.1.second
  25.0 6.1 %attention.1 = (bf16[32,32,128]{2,1,0:T(8,128)(2,1)S(1)}, bf16[4,48,128]{2,1,0:T(8,128)(2,1)S(1)}, bf16[4,48,128]{2,1,0:T(8,128)(2,1)S(1)}, f32[4,128,128]{2,1,0:T(8,128)S(1)}) custom-call(s32[4,2]{1,0:T(4,128)S(1)} %copy.17.key_range, s32[1]{0:T(128)} %bitcast.device, bf16[4,128,128]{2,1,0:T(8,128)(2,1)S(1)} %copy-done, bf16[4,128,128]{2,1,0:T(8,128)(2,1)S(1)} %copy-done.3, ...), custom_call_target="tpu_custom_call" | custom-call | tf_op jit(solution)/shard_map/attention/pallas_call | solution.py:512
  31.1 16.8 %all_to_all.20.scattered = bf16[32,32,128]{2,1,0:T(8,128)(2,1)S(1)} all-to-all(bf16[32,32,128]{2,1,0:T(8,128)(2,1)S(1)} %get-tuple-element.39), channel_id=1, replica_groups={{0,1,2,3,16,17,18,19,128,129,130,131,144,145,146,147,256,257,258,259,27..., dimensions={0} | all-to-all | bytes 524288 | tf_op jit(solution)/shard_map/all_to_all | solution.py:547
  47.9 0.7 middle.1
  48.6 11.1 %all-to-all-start.2 = ((bf16[16,32,128]{2,1,0:T(8,128)(2,1)}), bf16[16,32,128]{2,1,0:T(8,128)(2,1)S(1)}, u32[]{:S(2)}, u32[]{:S(2)}) async-start(bf16[16,32,128]{2,1,0:T(8,128)(2,1)} %middle.1), calls=%async_computation.2 | async-start | bytes 262144 | tf_op jit(solution)/shard_map/all_to_all | solution.py:558
  59.7 2.2 %collective-permute-start.2 = (bf16[4,48,128]{2,1,0:T(8,128)(2,1)S(1)}, bf16[4,48,128]{2,1,0:T(8,128)(2,1)S(1)}, u32[]{:S(2)}, u32[]{:S(2)}) collective-permute-start(bf16[4,48,128]{2,1,0:T(8,128)(2,1)S(1)} %get-tuple-element.43), channel_id=1, source_target_pairs={{0,1},{1,0},{2,3},{3,2},{4,5},{5,4},{6,7},{7,6},{8,9},{9,8},{10,11... | collective-permute-start | bytes 147464 | tf_op jit(solution)/shard_map/ppermute | solution.py:559
  62.0 6.8 %collective-permute-start.3 = (bf16[4,48,128]{2,1,0:T(8,128)(2,1)S(1)}, bf16[4,48,128]{2,1,0:T(8,128)(2,1)S(1)}, u32[]{:S(2)}, u32[]{:S(2)}) collective-permute-start(bf16[4,48,128]{2,1,0:T(8,128)(2,1)S(1)} %get-tuple-element.44), channel_id=1, source_target_pairs={{1,2},{2,1},{3,4},{4,3},{5,6},{6,5},{7,8},{8,7},{9,10},{10,9},{11,... | collective-permute-start | bytes 147464 | tf_op jit(solution)/shard_map/ppermute | solution.py:560
  68.8 3.1 %all-to-all-done.2.scattered = bf16[16,32,128]{2,1,0:T(8,128)(2,1)S(1)} async-done(((bf16[16,32,128]{2,1,0:T(8,128)(2,1)}), bf16[16,32,128]{2,1,0:T(8,128)(2,1)S(1)}, u32[]{:S(2)}, u32[]{:S(2)}) %all-to-all-start.2) | async-done | bytes 131104 | tf_op jit(solution)/shard_map/all_to_all | solution.py:558
  71.9 0.1 collective-permute-done.3.second
  72.1 0.7 broadcast_in_dim.3
  72.8 6.8 %all-to-all-start.3 = ((bf16[32,24,128]{2,1,0:T(8,128)(2,1)}), bf16[32,24,128]{2,1,0:T(8,128)(2,1)S(1)}, u32[]{:S(2)}, u32[]{:S(2)}) async-start(bf16[32,24,128]{2,1,0:T(8,128)(2,1)} %broadcast_in_dim.3), calls=%async_computation.3 | async-start | bytes 393216 | tf_op jit(solution)/shard_map/all_to_all | solution.py:564
  79.5 0.6 band.1
  80.1 0.7 copy.18
  80.8 1.1 %finish.1 = bf16[4,128,128]{2,1,0:T(8,128)(2,1)} custom-call(s32[1]{0:T(128)} %bitcast.device, bf16[4,128,128]{2,1,0:T(8,128)(2,1)S(1)} %copy-done, bf16[4,128,128]{2,1,0:T(8,128)(2,1)S(1)} %copy-done.3, f32[4,128,128]{2,1,0:T(8,128)S(1)} %get-tuple-element.46.own_grad, bf16[4,48,128]{2,1,0:T(8,128)(2,1)S(1)} %collective-permute-done.2.first, ...), custom_call_target="tpu_custom_call" | custom-call | tf_op jit(solution)/shard_map/finish/pallas_call | solution.py:575
  82.0 5.8 %all-to-all-done.3.parts_hbm = bf16[32,24,128]{2,1,0:T(8,128)(2,1)S(1)} async-done(((bf16[32,24,128]{2,1,0:T(8,128)(2,1)}), bf16[32,24,128]{2,1,0:T(8,128)(2,1)S(1)}, u32[]{:S(2)}, u32[]{:S(2)}) %all-to-all-start.3) | async-done | bytes 196640 | tf_op jit(solution)/shard_map/all_to_all | solution.py:564
  87.8 1.2 %last.1 = (bf16[128,512]{1,0:T(8,128)(2,1)}, bf16[128,128]{1,0:T(8,128)(2,1)}, bf16[4,128]{1,0:T(4,128)(2,1)}, f32[1,128]{1,0:T(1,128)}, f32[1,128]{1,0:T(1,128)}) custom-call(bf16[32,24,128]{2,1,0:T(8,128)(2,1)S(1)} %all-to-all-done.3.parts_hbm, bf16[128,512]{1,0:T(8,128)(2,1)S(1)} %copy-done.2, f32[1,128]{1,0:T(1,128)S(1)} %bitcast.28, ...), custom_call_target="tpu_custom_call" | custom-call | tf_op jit(solution)/shard_map/last/pallas_call | solution.py:585
  (26 shorter events, 0.1 us)
Async XLA Ops:
  2.3 9.2 %copy-start.11 = (bf16[5,48,128]{2,1,0:T(8,128)(2,1)S(1)}, bf16[5,48,128]{2,1,0:T(8,128)(2,1)}, u32[]{:S(2)}) copy-start(bf16[5,48,128]{2,1,0:T(8,128)(2,1)} %get-tuple-element.35) | copy-start | bytes 184324
  2.4 12.5 %copy-start.10 = (bf16[5,48,128]{2,1,0:T(8,128)(2,1)S(1)}, bf16[5,48,128]{2,1,0:T(8,128)(2,1)}, u32[]{:S(2)}) copy-start(bf16[5,48,128]{2,1,0:T(8,128)(2,1)} %get-tuple-element.36) | copy-start | bytes 184324
  2.4 20.8 %all-to-all-start = ((bf16[16,3,16,128]{3,2,1,0:T(8,128)(2,1)}), bf16[16,3,16,128]{3,2,1,0:T(8,128)(2,1)S(1)}, u32[]{:S(2)}, u32[]{:S(2)}) async-start(bf16[16,3,16,128]{3,2,1,0:T(8,128)(2,1)} %get-tuple-element.32), calls=%async_computation | async-start | bytes 393216 | tf_op jit(solution)/shard_map/all_to_all | solution.py:492
  11.5 11.5 %copy-start.9 = (s32[4,2]{0,1:T(2,128)S(1)}, s32[4,2]{0,1:T(2,128)}, u32[]{:S(2)}) copy-start(s32[4,2]{0,1:T(2,128)} %param.19) | copy-start | bytes 100
  11.6 12.9 %collective-permute-start = (bf16[5,48,128]{2,1,0:T(8,128)(2,1)S(1)}, bf16[5,48,128]{2,1,0:T(8,128)(2,1)S(1)}, u32[]{:S(2)}, u32[]{:S(2)}) collective-permute-start(bf16[5,48,128]{2,1,0:T(8,128)(2,1)S(1)} %copy-done.11), channel_id=1, source_target_pairs={{0,1},{1,0},{2,3},{3,2},{4,5},{5,4},{6,7},{7,6},{8,9},{9,8},{10,11... | collective-permute-start | bytes 184328 | tf_op jit(solution)/shard_map/ppermute | solution.py:494
  14.8 10.1 %collective-permute-start.1 = (bf16[5,48,128]{2,1,0:T(8,128)(2,1)S(1)}, bf16[5,48,128]{2,1,0:T(8,128)(2,1)S(1)}, u32[]{:S(2)}, u32[]{:S(2)}) collective-permute-start(bf16[5,48,128]{2,1,0:T(8,128)(2,1)S(1)} %copy-done.10), channel_id=1, source_target_pairs={{1,2},{2,1},{3,4},{4,3},{5,6},{6,5},{7,8},{8,7},{9,10},{10,9},{11,... | collective-permute-start | bytes 184328 | tf_op jit(solution)/shard_map/ppermute | solution.py:495
  23.1 0.7 copy-start.7
  23.1 0.7 copy-start.8
  23.2 0.7 copy-start.5
  23.2 0.7 copy-start.6
  23.9 1.1 %copy-start = (bf16[4,128,128]{2,1,0:T(8,128)(2,1)S(1)}, bf16[4,128,128]{2,1,0:T(8,128)(2,1)}, u32[]{:S(2)}) copy-start(bf16[4,128,128]{2,1,0:T(8,128)(2,1)} %atoms.3) | copy-start | bytes 393220
  23.9 1.1 %copy-start.2 = (bf16[128,512]{1,0:T(8,128)(2,1)S(1)}, bf16[128,512]{1,0:T(8,128)(2,1)}, u32[]{:S(2)}) copy-start(bf16[128,512]{1,0:T(8,128)(2,1)} %project_hbm.3) | copy-start | bytes 393220
  23.9 1.1 %copy-start.3 = (bf16[4,128,128]{2,1,0:T(8,128)(2,1)S(1)}, bf16[4,128,128]{2,1,0:T(8,128)(2,1)}, u32[]{:S(2)}) copy-start(bf16[4,128,128]{2,1,0:T(8,128)(2,1)} %cotangent.1) | copy-start | bytes 393220
  23.9 1.1 %copy-start.4 = (bf16[128,128]{1,0:T(8,128)(2,1)S(1)}, bf16[128,128]{1,0:T(8,128)(2,1)}, u32[]{:S(2)}) copy-start(bf16[128,128]{1,0:T(8,128)(2,1)} %combine_hbm.1) | copy-start | bytes 98308
  48.6 23.3 %all-to-all-start.2 = ((bf16[16,32,128]{2,1,0:T(8,128)(2,1)}), bf16[16,32,128]{2,1,0:T(8,128)(2,1)S(1)}, u32[]{:S(2)}, u32[]{:S(2)}) async-start(bf16[16,32,128]{2,1,0:T(8,128)(2,1)} %middle.1), calls=%async_computation.2 | async-start | bytes 262144 | tf_op jit(solution)/shard_map/all_to_all | solution.py:558
  59.7 12.2 %collective-permute-start.2 = (bf16[4,48,128]{2,1,0:T(8,128)(2,1)S(1)}, bf16[4,48,128]{2,1,0:T(8,128)(2,1)S(1)}, u32[]{:S(2)}, u32[]{:S(2)}) collective-permute-start(bf16[4,48,128]{2,1,0:T(8,128)(2,1)S(1)} %get-tuple-element.43), channel_id=1, source_target_pairs={{0,1},{1,0},{2,3},{3,2},{4,5},{5,4},{6,7},{7,6},{8,9},{9,8},{10,11... | collective-permute-start | bytes 147464 | tf_op jit(solution)/shard_map/ppermute | solution.py:559
  62.0 10.1 %collective-permute-start.3 = (bf16[4,48,128]{2,1,0:T(8,128)(2,1)S(1)}, bf16[4,48,128]{2,1,0:T(8,128)(2,1)S(1)}, u32[]{:S(2)}, u32[]{:S(2)}) collective-permute-start(bf16[4,48,128]{2,1,0:T(8,128)(2,1)S(1)} %get-tuple-element.44), channel_id=1, source_target_pairs={{1,2},{2,1},{3,4},{4,3},{5,6},{6,5},{7,8},{8,7},{9,10},{10,9},{11,... | collective-permute-start | bytes 147464 | tf_op jit(solution)/shard_map/ppermute | solution.py:560
  72.8 6.8 %copy-start.1 = (bf16[16,3,16,128]{3,2,1,0:T(8,128)(2,1)S(1)}, bf16[16,3,16,128]{3,2,1,0:T(8,128)(2,1)}, u32[]{:S(2)}) copy-start(bf16[16,3,16,128]{3,2,1,0:T(8,128)(2,1)} %get-tuple-element.32) | copy-start | bytes 589828
  72.8 15.0 %all-to-all-start.3 = ((bf16[32,24,128]{2,1,0:T(8,128)(2,1)}), bf16[32,24,128]{2,1,0:T(8,128)(2,1)S(1)}, u32[]{:S(2)}, u32[]{:S(2)}) async-start(bf16[32,24,128]{2,1,0:T(8,128)(2,1)} %broadcast_in_dim.3), calls=%async_computation.3 | async-start | bytes 393216 | tf_op jit(solution)/shard_map/all_to_all | solution.py:564

commit v8 on v7

--- a/solution.py
+++ b/solution.py
@@ -62,7 +62,7 @@
 
 def start_kernel(device, band, atoms, tokens, tiles, first, second, line, sems):
     samples, count, width = atoms.shape
-    odd = device[0] & 1
+    odd = (device[0] + 1) & 1
     low = pl.multiple_of((1 - odd) * (count - RIM), 16)
     high = pl.multiple_of(odd * (count - RIM), 16)
     copies = fetch(
@@ -105,11 +105,15 @@
     return jnp.where(shown, grad, 0.0).astype(BF)
 
 
-def pair_kernel(band, gain, weights, atom_gain, tokens, table, pair_norm, atom_gain_out, tokens_out):
+def keep_kernel(*refs):
+    half = len(refs) // 2
+    for source, kept in zip(refs[:half], refs[half:]):
+        kept[...] = source[...]
+
+
+def pair_kernel(band, gain, weights, table, pair_norm):
     heads = 4
     entries = band.shape[0]
-    atom_gain_out[...] = atom_gain[...]
-    tokens_out[...] = tokens[...]
     hat, _ = norm(band[...].astype(F32))
     normed = (hat * gain[...]).astype(BF)
     pair_norm[...] = normed
@@ -154,18 +158,22 @@
     rows = jnp.concatenate(rows + [jnp.zeros((KW - 48, width), F32)], axis=0).astype(BF)
     hat, inv = norm(band[...].astype(F32))
     norm_grad = nn(entry_grads(rows, entries), weight_spread(weights)).astype(BF).astype(F32)
-    band_grad[...] = norm_back(norm_grad * pair_gain[...], hat, inv).astype(BF)
+    result = norm_back(norm_grad * pair_gain[...], hat, inv).astype(BF)
+    slots = band_grad.shape[0]
+    for n in range(entries // 16):
+        block, slot = divmod(n, slots)
+        band_grad[slot, 16 * block : 16 * block + 16, :] = result[16 * n : 16 * n + 16]
 
 
 def attention_kernel(
     key_range,
     device,
-    atoms_hbm,
-    cotangent_hbm,
-    project_hbm,
-    combine_hbm,
-    gain_hbm,
-    tokens_hbm,
+    atoms,
+    cotangent,
+    project,
+    combine,
+    atom_gain,
+    tokens,
     first,
     second,
     table,
@@ -176,36 +184,17 @@
     own_grad,
     bias,
     bias_grad,
-    atoms,
-    cotangent,
-    project,
-    combine,
-    atom_gain,
-    tokens,
-    sems,
 ):
     samples, count, width = atoms.shape
     heads = 4
     windows = count // QW
     entries = pair_norm.shape[0]
     scale = 1.0 / math.sqrt(width // heads)
-    copies = fetch(
-        [
-            (tokens_hbm, tokens),
-            (gain_hbm, atom_gain),
-            (atoms_hbm, atoms),
-            (project_hbm, project),
-            (cotangent_hbm, cotangent),
-            (combine_hbm, combine),
-        ],
-        sems,
-    )
-    copies[0].wait()
     lane = iota((KW, KW), 1)
     line = iota((KW, KW), 0)
 
     own = jnp.broadcast_to((tokens[...] - device[0] * 16).astype(F32), (8, KW))
-    odd = (device[0] & 1) == 1
+    odd = (device[0] & 1) == 0
 
     def sides(x, y):
         return jnp.where(odd, x, y), jnp.where(odd, y, x)
@@ -243,8 +232,6 @@
         allowed = (line >= key_range[w, 0] - begin) & (line < key_range[w, 1] - begin)
         bias[w] = jnp.where(allowed, values, NEG_FILL)
         bias_grad[w] = jnp.zeros((KW, KW), F32)
-    for copy in copies[1:]:
-        copy.wait()
     gain = atom_gain[...]
     diag = jnp.where((line >> 5) == (lane >> 5), 1.0, 0.0).astype(BF)
     head_of = iota((QW, width), 1) >> 5
@@ -332,8 +319,12 @@
         high, low = split2(by_slot)
         rows = query_hot(w)
         table_grad = table_grad + nt(high, rows) + nt(low, rows)
-    entry_grad = entry_grads(table_grad.astype(BF), entries)
-    weight_part = tn(entry_grad, pair_norm[...])
+    spread = iota((KW, entries), 0) == (iota((KW, entries), 1) >> 4)
+    spread = jnp.where(spread, 1.0, 0.0).astype(BF)
+    entry_grad = tn(table_grad.astype(BF), spread)
+    shown = (iota((KW, entries), 0) & 15) == (iota((KW, entries), 1) & 15)
+    entry_grad = jnp.where(shown, entry_grad, 0.0).astype(BF)
+    weight_part = nn(entry_grad, pair_norm[...])
     left = iota((3, width), 1) < 64
     tables = []
     for x in range(4):
@@ -357,35 +348,17 @@
 
 
 def last_kernel(
-    parts_hbm,
-    project_hbm,
-    atom_gain_hbm,
-    pair_gain_hbm,
-    weight_hbm,
+    parts,
+    project,
+    atom_gain,
+    pair_gain,
+    weights,
     project_grad,
     combine_grad,
     weight_grad,
     scale_grad,
     gain_grad,
-    parts,
-    project,
-    atom_gain,
-    pair_gain,
-    weights,
-    sems,
 ):
-    copies = fetch(
-        [
-            (parts_hbm, parts),
-            (project_hbm, project),
-            (atom_gain_hbm, atom_gain),
-            (pair_gain_hbm, pair_gain),
-            (weight_hbm, weights),
-        ],
-        sems,
-    )
-    for copy in copies:
-        copy.wait()
     chunks = [parts[p].astype(F32) for p in range(parts.shape[0])]
     rows = jnp.concatenate([x[:16] for x in chunks], axis=0)
     width = rows.shape[1]
@@ -406,7 +379,7 @@
 
 def finish_kernel(device, atoms, cotangent, own_grad, first, second, atom_gain, result):
     samples, count, width = atoms.shape
-    odd = (device[0] & 1) == 1
+    odd = (device[0] & 1) == 0
     gain = atom_gain[...]
     for s in range(samples):
         x_hat, inv = norm(atoms[s].astype(F32))
@@ -428,12 +401,6 @@
 
 def anywhere(n):
     return [pl.BlockSpec(memory_space=pl.ANY)] * n
-
-
-def copied(arrays):
-    return [pltpu.VMEM(x.shape, x.dtype) for x in arrays] + [
-        pltpu.SemaphoreType.DMA((len(arrays),))
-    ]
 
 
 def shards(
@@ -455,8 +422,8 @@
     windows = count // QW
     block = pair_band.shape[0] // cols
     keys = pair_band.shape[1]
-    pairs = [(i, i ^ 1) for i in range(peers)]
-    odd_pairs = [(i + j, i + 1 - j) for i in range(1, peers - 1, 2) for j in range(2)]
+    pairs = [(i + j, i + 1 - j) for i in range(1, peers - 1, 2) for j in range(2)]
+    odd_pairs = [(i, i ^ 1) for i in range(peers)]
 
     shape = jax.ShapeDtypeStruct
 
@@ -494,21 +461,24 @@
     first = lax.ppermute(first, ("row", "col"), pairs)
     second = lax.ppermute(second, ("row", "col"), odd_pairs)
 
-    table, pair_norm, kept_gain, tokens = pl.pallas_call(
+    small = [band_gain, weights, gain, tokens]
+    band_gain, weights, gain, tokens = pl.pallas_call(
+        keep_kernel,
+        out_shape=tuple(shape(x.shape, x.dtype) for x in small),
+        in_specs=vmem(4),
+        out_specs=tuple(vmem(4)),
+        compiler_params=LIMIT,
+        name="keep",
+    )(*small)
+    table, pair_norm = pl.pallas_call(
         pair_kernel,
-        out_shape=(
-            shape((KW, KW), BF),
-            shape((entries, width), BF),
-            shape(gain.shape, F32),
-            shape(tokens.shape, jnp.int32),
-        ),
-        in_specs=vmem(5),
-        out_specs=tuple(vmem(4)),
+        out_shape=(shape((KW, KW), BF), shape((entries, width), BF)),
+        in_specs=vmem(3),
+        out_specs=tuple(vmem(2)),
         cost_estimate=pl.CostEstimate(flops=10**9, bytes_accessed=10**7, transcendentals=0),
         compiler_params=LIMIT,
         name="pair",
-    )(band, band_gain, weights, gain, tokens)
-    fetched = [atoms, cotangent, project, combine, kept_gain, tokens]
+    )(band, band_gain, weights)
     outgoing, first, second, own_grad = pl.pallas_call(
         attention_kernel,
         out_shape=(
@@ -517,16 +487,28 @@
             shape((samples, RIM, width), BF),
             shape((samples, count, width), F32),
         ),
-        in_specs=smem(2) + anywhere(len(fetched)) + vmem(4),
+        in_specs=smem(2) + vmem(10),
         out_specs=tuple(vmem(4)),
         scratch_shapes=[
             pltpu.VMEM((windows, KW, KW), F32),
             pltpu.VMEM((windows, KW, KW), F32),
-        ]
-        + copied(fetched),
+        ],
         compiler_params=LIMIT,
         name="attention",
-    )(key_range, device, *fetched, first, second, table, pair_norm)
+    )(
+        key_range,
+        device,
+        atoms,
+        cotangent,
+        project,
+        combine,
+        gain,
+        tokens,
+        first,
+        second,
+        table,
+        pair_norm,
+    )
 
     def place(y, z_hi, core, z_lo, x):
         return ((y * 4 + z_hi) * 2 + core) * 16 + z_lo * 4 + x
@@ -564,14 +546,13 @@
     part = lax.all_to_all(part, axes, 0, 0, axis_index_groups=planes, tiled=True)
     band_grad = pl.pallas_call(
         band_kernel,
-        out_shape=shape((entries, width), BF),
+        out_shape=shape((keys, cols * block, width), BF),
         in_specs=smem(1) + vmem(4),
         out_specs=pl.BlockSpec(memory_space=pltpu.VMEM),
         compiler_params=LIMIT,
         name="band",
     )(device, tiles.reshape(entries, width), scattered, band_gain, weights)
-    band_grad = jnp.transpose(band_grad.reshape(cols, keys, block, width), (0, 2, 1, 3))
-    band_grad = band_grad.reshape(pair_band.shape)
+    band_grad = jnp.transpose(band_grad, (1, 0, 2))
     atoms_grad = pl.pallas_call(
         finish_kernel,
         out_shape=shape(atoms.shape, BF),
@@ -581,7 +562,6 @@
         name="finish",
     )(device, atoms, cotangent, own_grad, first, second, gain)
     part, atoms_grad, band_grad = lax.optimization_barrier((part, atoms_grad, band_grad))
-    fetched = [part, project, gain, band_gain, weights]
     project_grad, combine_grad, weight_grad, scale_grad, gain_grad = pl.pallas_call(
         last_kernel,
         out_shape=(
@@ -591,12 +571,11 @@
             shape((1, width), F32),
             shape((1, width), F32),
         ),
-        in_specs=anywhere(5),
+        in_specs=vmem(5),
         out_specs=tuple(vmem(5)),
-        scratch_shapes=copied(fetched),
         compiler_params=LIMIT,
         name="last",
-    )(*fetched)
+    )(part, project, gain, band_gain, weights)
     return (
         atoms_grad,
         project_grad,

time: 89.6 us -> 85.7 us (0.956)
  starting transfers between devices: 47.5 us -> 42.4 us
  blocking collectives: 16.8 us -> 18.2 us
  waiting for transfers between devices: 9.55 us -> 10.9 us
    ppermute x2, starting transfers between devices: 15 us -> 3.84 us  [shards(): second = lax.ppermute(second, ('row', 'col'), odd_pairs)]
    ppermute x2, starting transfers between devices: 5.47 us -> 15.5 us  [shards(): first = lax.ppermute(first, ('row', 'col'), pairs)]
    all_to_all x1, starting transfers between devices: 11.1 us -> 7.03 us  [shards(): lax.all_to_all(part, axes, 0, 0, axis_index_groups=lines, tiled=True)]
    all_to_all x1, blocking collectives: 16.8 us -> 18.2 us  [shards(): lax.all_to_all(outgoing, axes, 0, 0, axis_index_groups=planes, tiled=True)]
    pallas_call x1, Pallas kernels: 6.13 us -> 5.08 us  [shards(): pl.pallas_call(attention_kernel, out_shape=(shape((32, 32, width), BF), s...]
    ppermute x2, waiting for transfers between devices: 0.59 us -> 1.6 us  [shards(): second = lax.ppermute(second, ('row', 'col'), odd_pairs)]
  transfers between devices with their start and end apart: 7 -> 7, of which waited for: 4 -> 3; matrix products, arithmetic and copies ran while one was open for 1% -> 0% of each run, Pallas kernels for 3% -> 4%
where the time goes in v8:
time: 85.7 us; the launch traced here: 85.1 us
  starting transfers between devices  42.4 us (49%)
  blocking collectives  18.2 us (21%)
  Pallas kernels  11.3 us (13%)
  waiting for transfers between devices  10.9 us (13%)
  local copies, waits for them, and re-layouts  1.55 us (2%)
  between operations  0.86 us (1%)
    all_to_all x1, blocking collectives, shards(): lax.all_to_all(outgoing, axes, 0, 0, axis_index_groups=planes, tiled=True)  18.2 us
    ppermute x2, starting transfers between devices, shards(): first = lax.ppermute(first, ('row', 'col'), pairs)  15.5 us
    all_to_all x1, starting transfers between devices, shards(): lax.all_to_all(tiles, 'col', 0, 0, tiled=True).reshape(entries, width)  9.16 us
    all_to_all x1, starting transfers between devices, shards(): lax.all_to_all(part, axes, 0, 0, axis_index_groups=lines, tiled=True)  7.03 us
    all_to_all x1, starting transfers between devices, shards(): lax.all_to_all(part, axes, 0, 0, axis_index_groups=planes, tiled=True)  6.82 us
    all_to_all x1, waiting for transfers between devices, shards(): lax.all_to_all(part, axes, 0, 0, axis_index_groups=planes, tiled=True)  5.84 us
    pallas_call x1, Pallas kernels, shards(): pl.pallas_call(attention_kernel, out_shape=(shape((32, 32, width), BF), s...  5.08 us
    ppermute x2, starting transfers between devices, shards(): second = lax.ppermute(second, ('row', 'col'), odd_pairs)  3.84 us
  transfers between devices with their start and end apart: 7, of which 3 were waited for; matrix products, arithmetic and copies ran while one was open for 0% of the time, Pallas kernels for 4%

profile of v8, /device:TPU:1, one launch (start us, length us, event | category | flops | bytes accessed | tf_op | source)
XLA Modules:
  0.0 85.1 jit_solution(3747703610842188435)
XLA Ops:
  0.6 1.7 %start.1 = (bf16[16,3,16,128]{3,2,1,0:T(8,128)(2,1)}, bf16[5,48,128]{2,1,0:T(8,128)(2,1)}, bf16[5,48,128]{2,1,0:T(8,128)(2,1)}) custom-call(s32[1]{0:T(128)} %bitcast.device, bf16[3,16,16,128]{3,2,1,0:T(8,128)(2,1)} %bitcast.21, bf16[4,128,128]{2,1,0:T(8,128)(2,1)} %atoms.5, s32[1,128]{1,0:T(1,128)} %bitcast.16), custom_call_target="tpu_custom_call" | custom-call | tf_op jit(solution)/shard_map/start/pallas_call | solution.py:438
  2.3 0.0 copy-start.11
  2.4 9.2 %all-to-all-start = ((bf16[16,3,16,128]{3,2,1,0:T(8,128)(2,1)}), bf16[16,3,16,128]{3,2,1,0:T(8,128)(2,1)S(1)}, u32[]{:S(2)}, u32[]{:S(2)}) async-start(bf16[16,3,16,128]{3,2,1,0:T(8,128)(2,1)} %get-tuple-element.38), calls=%async_computation | async-start | bytes 393216 | tf_op jit(solution)/shard_map/all_to_all | solution.py:459
  11.6 8.7 %collective-permute-start = (bf16[5,48,128]{2,1,0:T(8,128)(2,1)S(1)}, bf16[5,48,128]{2,1,0:T(8,128)(2,1)S(1)}, u32[]{:S(2)}, u32[]{:S(2)}) collective-permute-start(bf16[5,48,128]{2,1,0:T(8,128)(2,1)S(1)} %copy-done.11), channel_id=1, source_target_pairs={{1,2},{2,1},{3,4},{4,3},{5,6},{6,5},{7,8},{8,7},{9,10},{10,9},{11,... | collective-permute-start | bytes 184328 | tf_op jit(solution)/shard_map/ppermute | solution.py:461
  20.3 0.0 copy-start.7
  20.3 1.9 %collective-permute-start.1 = (bf16[5,48,128]{2,1,0:T(8,128)(2,1)S(1)}, bf16[5,48,128]{2,1,0:T(8,128)(2,1)S(1)}, u32[]{:S(2)}, u32[]{:S(2)}) collective-permute-start(bf16[5,48,128]{2,1,0:T(8,128)(2,1)S(1)} %copy-done.10), channel_id=1, source_target_pairs={{0,1},{1,0},{2,3},{3,2},{4,5},{5,4},{6,7},{7,6},{8,9},{9,8},{10,11... | collective-permute-start | bytes 184328 | tf_op jit(solution)/shard_map/ppermute | solution.py:462
  22.2 0.1 copy.17.key_range
  22.3 0.6 copy-done.5
  23.0 0.0 copy-done.6
  23.1 0.6 pair.1
  23.7 1.6 %collective-permute-done.1.second = bf16[5,48,128]{2,1,0:T(8,128)(2,1)S(1)} collective-permute-done((bf16[5,48,128]{2,1,0:T(8,128)(2,1)S(1)}, bf16[5,48,128]{2,1,0:T(8,128)(2,1)S(1)}, u32[]{:S(2)}, u32[]{:S(2)}) %collective-permute-start.1) | collective-permute-done | bytes 61472 | tf_op jit(solution)/shard_map/ppermute | solution.py:462
  25.3 5.1 %attention.1 = (bf16[32,32,128]{2,1,0:T(8,128)(2,1)S(1)}, bf16[4,48,128]{2,1,0:T(8,128)(2,1)S(1)}, bf16[4,48,128]{2,1,0:T(8,128)(2,1)S(1)}, f32[4,128,128]{2,1,0:T(8,128)S(1)}) custom-call(s32[4,2]{1,0:T(4,128)S(1)} %copy.17.key_range, s32[1]{0:T(128)} %bitcast.device, bf16[4,128,128]{2,1,0:T(8,128)(2,1)S(1)} %copy-done, bf16[4,128,128]{2,1,0:T(8,128)(2,1)S(1)} %copy-done.3, ...), custom_call_target="tpu_custom_call" | custom-call | tf_op jit(solution)/shard_map/attention/pallas_call | solution.py:482
  30.4 18.2 %all_to_all.20.scattered = bf16[32,32,128]{2,1,0:T(8,128)(2,1)S(1)} all-to-all(bf16[32,32,128]{2,1,0:T(8,128)(2,1)S(1)} %get-tuple-element.43), channel_id=1, replica_groups={{0,1,2,3,16,17,18,19,128,129,130,131,144,145,146,147,256,257,258,259,27..., dimensions={0} | all-to-all | bytes 524288 | tf_op jit(solution)/shard_map/all_to_all | solution.py:529
  48.6 0.7 middle.1
  49.3 7.0 %all-to-all-start.2 = ((bf16[16,32,128]{2,1,0:T(8,128)(2,1)}), bf16[16,32,128]{2,1,0:T(8,128)(2,1)S(1)}, u32[]{:S(2)}, u32[]{:S(2)}) async-start(bf16[16,32,128]{2,1,0:T(8,128)(2,1)} %middle.1), calls=%async_computation.2 | async-start | bytes 262144 | tf_op jit(solution)/shard_map/all_to_all | solution.py:540
  56.4 6.8 %collective-permute-start.2 = (bf16[4,48,128]{2,1,0:T(8,128)(2,1)S(1)}, bf16[4,48,128]{2,1,0:T(8,128)(2,1)S(1)}, u32[]{:S(2)}, u32[]{:S(2)}) collective-permute-start(bf16[4,48,128]{2,1,0:T(8,128)(2,1)S(1)} %get-tuple-element.47), channel_id=1, source_target_pairs={{1,2},{2,1},{3,4},{4,3},{5,6},{6,5},{7,8},{8,7},{9,10},{10,9},{11,... | collective-permute-start | bytes 147464 | tf_op jit(solution)/shard_map/ppermute | solution.py:541
  63.2 1.9 %collective-permute-start.3 = (bf16[4,48,128]{2,1,0:T(8,128)(2,1)S(1)}, bf16[4,48,128]{2,1,0:T(8,128)(2,1)S(1)}, u32[]{:S(2)}, u32[]{:S(2)}) collective-permute-start(bf16[4,48,128]{2,1,0:T(8,128)(2,1)S(1)} %get-tuple-element.48), channel_id=1, source_target_pairs={{0,1},{1,0},{2,3},{3,2},{4,5},{5,4},{6,7},{7,6},{8,9},{9,8},{10,11... | collective-permute-start | bytes 147464 | tf_op jit(solution)/shard_map/ppermute | solution.py:542
  65.1 3.4 %all-to-all-done.2.scattered = bf16[16,32,128]{2,1,0:T(8,128)(2,1)S(1)} async-done(((bf16[16,32,128]{2,1,0:T(8,128)(2,1)}), bf16[16,32,128]{2,1,0:T(8,128)(2,1)S(1)}, u32[]{:S(2)}, u32[]{:S(2)}) %all-to-all-start.2) | async-done | bytes 131104 | tf_op jit(solution)/shard_map/all_to_all | solution.py:540
  68.6 0.7 broadcast_in_dim.3
  69.3 6.8 %all-to-all-start.3 = ((bf16[32,24,128]{2,1,0:T(8,128)(2,1)}), bf16[32,24,128]{2,1,0:T(8,128)(2,1)S(1)}, u32[]{:S(2)}, u32[]{:S(2)}) async-start(bf16[32,24,128]{2,1,0:T(8,128)(2,1)} %broadcast_in_dim.3), calls=%async_computation.3 | async-start | bytes 393216 | tf_op jit(solution)/shard_map/all_to_all | solution.py:546
  76.1 1.1 %finish.1 = bf16[4,128,128]{2,1,0:T(8,128)(2,1)} custom-call(s32[1]{0:T(128)} %bitcast.device, bf16[4,128,128]{2,1,0:T(8,128)(2,1)S(1)} %copy-done, bf16[4,128,128]{2,1,0:T(8,128)(2,1)S(1)} %copy-done.3, f32[4,128,128]{2,1,0:T(8,128)S(1)} %get-tuple-element.50.own_grad, bf16[4,48,128]{2,1,0:T(8,128)(2,1)S(1)} %collective-permute-done.2.first, ...), custom_call_target="tpu_custom_call" | custom-call | tf_op jit(solution)/shard_map/finish/pallas_call | solution.py:556
  77.2 1.3 %band.1 = bf16[3,256,128]{2,1,0:T(8,128)(2,1)} custom-call(s32[1]{0:T(128)} %bitcast.device, bf16[768,128]{1,0:T(8,128)(2,1)S(1)} %bitcast.14, bf16[16,32,128]{2,1,0:T(8,128)(2,1)S(1)} %all-to-all-done.2.scattered, f32[1,128]{1,0:T(1,128)S(1)} %get-tuple-element.39.gain.pair_gain, bf16[4,128]{1,0:T(4,128)(2,1)S(1)} %get-tuple-element.40.weights), custom_call_target="tpu_custom_call" | custom-call | tf_op jit(solution)/shard_map/band/pallas_call | solution.py:547
  78.5 5.8 %all-to-all-done.3.parts = bf16[32,24,128]{2,1,0:T(8,128)(2,1)S(1)} async-done(((bf16[32,24,128]{2,1,0:T(8,128)(2,1)}), bf16[32,24,128]{2,1,0:T(8,128)(2,1)S(1)}, u32[]{:S(2)}, u32[]{:S(2)}) %all-to-all-start.3) | async-done | bytes 196640 | tf_op jit(solution)/shard_map/all_to_all | solution.py:546
  84.4 0.8 last.1
  (26 shorter events, 0.1 us)
Async XLA Ops:
  2.3 9.2 %copy-start.11 = (bf16[5,48,128]{2,1,0:T(8,128)(2,1)S(1)}, bf16[5,48,128]{2,1,0:T(8,128)(2,1)}, u32[]{:S(2)}) copy-start(bf16[5,48,128]{2,1,0:T(8,128)(2,1)} %get-tuple-element.36) | copy-start | bytes 184324
  2.4 17.9 %copy-start.10 = (bf16[5,48,128]{2,1,0:T(8,128)(2,1)S(1)}, bf16[5,48,128]{2,1,0:T(8,128)(2,1)}, u32[]{:S(2)}) copy-start(bf16[5,48,128]{2,1,0:T(8,128)(2,1)} %get-tuple-element.37) | copy-start | bytes 184324
  2.4 20.7 %all-to-all-start = ((bf16[16,3,16,128]{3,2,1,0:T(8,128)(2,1)}), bf16[16,3,16,128]{3,2,1,0:T(8,128)(2,1)S(1)}, u32[]{:S(2)}, u32[]{:S(2)}) async-start(bf16[16,3,16,128]{3,2,1,0:T(8,128)(2,1)} %get-tuple-element.38), calls=%async_computation | async-start | bytes 393216 | tf_op jit(solution)/shard_map/all_to_all | solution.py:459
  11.5 10.7 %copy-start.9 = (s32[4,2]{0,1:T(2,128)S(1)}, s32[4,2]{0,1:T(2,128)}, u32[]{:S(2)}) copy-start(s32[4,2]{0,1:T(2,128)} %param.19) | copy-start | bytes 100
  11.6 12.1 %collective-permute-start = (bf16[5,48,128]{2,1,0:T(8,128)(2,1)S(1)}, bf16[5,48,128]{2,1,0:T(8,128)(2,1)S(1)}, u32[]{:S(2)}, u32[]{:S(2)}) collective-permute-start(bf16[5,48,128]{2,1,0:T(8,128)(2,1)S(1)} %copy-done.11), channel_id=1, source_target_pairs={{1,2},{2,1},{3,4},{4,3},{5,6},{6,5},{7,8},{8,7},{9,10},{10,9},{11,... | collective-permute-start | bytes 184328 | tf_op jit(solution)/shard_map/ppermute | solution.py:461
  20.3 2.1 %copy-start.7 = (f32[128]{0:T(128)S(1)}, f32[128]{0:T(128)}, u32[]{:S(2)}) copy-start(f32[128]{0:T(128)} %param.16) | copy-start | bytes 1540
  20.3 2.1 %copy-start.8 = (f32[128]{0:T(128)S(1)}, f32[128]{0:T(128)}, u32[]{:S(2)}) copy-start(f32[128]{0:T(128)} %param.14) | copy-start | bytes 1540
  20.3 5.0 %collective-permute-start.1 = (bf16[5,48,128]{2,1,0:T(8,128)(2,1)S(1)}, bf16[5,48,128]{2,1,0:T(8,128)(2,1)S(1)}, u32[]{:S(2)}, u32[]{:S(2)}) collective-permute-start(bf16[5,48,128]{2,1,0:T(8,128)(2,1)S(1)} %copy-done.10), channel_id=1, source_target_pairs={{0,1},{1,0},{2,3},{3,2},{4,5},{5,4},{6,7},{7,6},{8,9},{9,8},{10,11... | collective-permute-start | bytes 184328 | tf_op jit(solution)/shard_map/ppermute | solution.py:462
  22.3 0.7 copy-start.5
  22.3 0.7 copy-start.6
  23.0 2.2 %copy-start = (bf16[4,128,128]{2,1,0:T(8,128)(2,1)S(1)}, bf16[4,128,128]{2,1,0:T(8,128)(2,1)}, u32[]{:S(2)}) copy-start(bf16[4,128,128]{2,1,0:T(8,128)(2,1)} %atoms.5) | copy-start | bytes 393220
  23.0 2.2 %copy-start.2 = (bf16[128,512]{1,0:T(8,128)(2,1)S(1)}, bf16[128,512]{1,0:T(8,128)(2,1)}, u32[]{:S(2)}) copy-start(bf16[128,512]{1,0:T(8,128)(2,1)} %project.3) | copy-start | bytes 393220
  23.1 2.2 %copy-start.3 = (bf16[4,128,128]{2,1,0:T(8,128)(2,1)S(1)}, bf16[4,128,128]{2,1,0:T(8,128)(2,1)}, u32[]{:S(2)}) copy-start(bf16[4,128,128]{2,1,0:T(8,128)(2,1)} %cotangent.3) | copy-start | bytes 393220
  23.1 2.2 %copy-start.4 = (bf16[128,128]{1,0:T(8,128)(2,1)S(1)}, bf16[128,128]{1,0:T(8,128)(2,1)}, u32[]{:S(2)}) copy-start(bf16[128,128]{1,0:T(8,128)(2,1)} %combine.1) | copy-start | bytes 98308
  49.3 19.2 %all-to-all-start.2 = ((bf16[16,32,128]{2,1,0:T(8,128)(2,1)}), bf16[16,32,128]{2,1,0:T(8,128)(2,1)S(1)}, u32[]{:S(2)}, u32[]{:S(2)}) async-start(bf16[16,32,128]{2,1,0:T(8,128)(2,1)} %middle.1), calls=%async_computation.2 | async-start | bytes 262144 | tf_op jit(solution)/shard_map/all_to_all | solution.py:540
  56.4 12.2 %collective-permute-start.2 = (bf16[4,48,128]{2,1,0:T(8,128)(2,1)S(1)}, bf16[4,48,128]{2,1,0:T(8,128)(2,1)S(1)}, u32[]{:S(2)}, u32[]{:S(2)}) collective-permute-start(bf16[4,48,128]{2,1,0:T(8,128)(2,1)S(1)} %get-tuple-element.47), channel_id=1, source_target_pairs={{1,2},{2,1},{3,4},{4,3},{5,6},{6,5},{7,8},{8,7},{9,10},{10,9},{11,... | collective-permute-start | bytes 147464 | tf_op jit(solution)/shard_map/ppermute | solution.py:541
  63.2 5.4 %collective-permute-start.3 = (bf16[4,48,128]{2,1,0:T(8,128)(2,1)S(1)}, bf16[4,48,128]{2,1,0:T(8,128)(2,1)S(1)}, u32[]{:S(2)}, u32[]{:S(2)}) collective-permute-start(bf16[4,48,128]{2,1,0:T(8,128)(2,1)S(1)} %get-tuple-element.48), channel_id=1, source_target_pairs={{0,1},{1,0},{2,3},{3,2},{4,5},{5,4},{6,7},{7,6},{8,9},{9,8},{10,11... | collective-permute-start | bytes 147464 | tf_op jit(solution)/shard_map/ppermute | solution.py:542
  69.3 15.1 %all-to-all-start.3 = ((bf16[32,24,128]{2,1,0:T(8,128)(2,1)}), bf16[32,24,128]{2,1,0:T(8,128)(2,1)S(1)}, u32[]{:S(2)}, u32[]{:S(2)}) async-start(bf16[32,24,128]{2,1,0:T(8,128)(2,1)} %broadcast_in_dim.3), calls=%async_computation.3 | async-start | bytes 393216 | tf_op jit(solution)/shard_map/all_to_all | solution.py:546
  76.1 1.1 %copy-start.1 = (bf16[16,3,16,128]{3,2,1,0:T(8,128)(2,1)S(1)}, bf16[16,3,16,128]{3,2,1,0:T(8,128)(2,1)}, u32[]{:S(2)}) copy-start(bf16[16,3,16,128]{3,2,1,0:T(8,128)(2,1)} %get-tuple-element.38) | copy-start | bytes 589828

commit v9 on v8

--- a/solution.py
+++ b/solution.py
@@ -60,13 +60,47 @@
     return copies
 
 
-def start_kernel(device, band, atoms, tokens, tiles, first, second, line, sems):
+def split3(x):
+    high = x.astype(BF).astype(F32)
+    middle = (x - high).astype(BF).astype(F32)
+    return [high, middle, x - high - middle]
+
+
+def small(sent):
+    block = sent[sent.shape[0] - 1].astype(F32)
+    atom_gain = block[20:21] + block[21:22] + block[22:23]
+    pair_gain = block[23:24] + block[24:25] + block[25:26]
+    return block[:1], block[16:20], atom_gain, pair_gain
+
+
+def start_kernel(
+    device,
+    band,
+    atoms,
+    tokens,
+    weights_hbm,
+    atom_gain_hbm,
+    pair_gain_hbm,
+    tiles,
+    first,
+    second,
+    line,
+    weights,
+    atom_gain,
+    pair_gain,
+    sems,
+):
     samples, count, width = atoms.shape
     odd = (device[0] + 1) & 1
     low = pl.multiple_of((1 - odd) * (count - RIM), 16)
     high = pl.multiple_of(odd * (count - RIM), 16)
     copies = fetch(
-        [(tokens, line)]
+        [
+            (tokens, line),
+            (weights_hbm, weights),
+            (atom_gain_hbm, atom_gain),
+            (pair_gain_hbm, pair_gain),
+        ]
         + [(band.at[k], tiles.at[:, k]) for k in range(band.shape[0])]
         + [
             (atoms.at[:, pl.ds(low, RIM)], first.at[:samples]),
@@ -74,21 +108,22 @@
         ],
         sems,
     )
-    copies[0].wait()
-    local = jnp.broadcast_to((line[...] - device[0] * 16).astype(F32), (RIM, width)).astype(BF)
-    first[samples] = local
-    second[samples] = local
-    for copy in copies[1:]:
+    for copy in copies[:4]:
         copy.wait()
-
-
-def weight_lines(weights):
-    rows = weights[...].astype(F32)
+    local = jnp.broadcast_to((line[...] - device[0] * 16).astype(F32), (16, width))
+    rows = [local, weights[...].astype(F32)] + split3(atom_gain[...]) + split3(pair_gain[...])
+    block = jnp.concatenate(rows + [jnp.zeros((RIM - 26, width), F32)], axis=0).astype(BF)
+    first[samples] = block
+    second[samples] = block
+    for copy in copies[4:]:
+        copy.wait()
+
+
+def weight_lines(rows):
     return jnp.concatenate([rows, jnp.zeros((16 - rows.shape[0], rows.shape[1]), F32)], axis=0)
 
 
-def weight_spread(weights):
-    rows = weights[...].astype(F32)
+def weight_spread(rows):
     rows = [jnp.broadcast_to(rows[h : h + 1], (16, rows.shape[1])) for h in range(4)]
     return jnp.concatenate(rows * 2, axis=0).astype(BF)
 
@@ -105,17 +140,12 @@
     return jnp.where(shown, grad, 0.0).astype(BF)
 
 
-def keep_kernel(*refs):
-    half = len(refs) // 2
-    for source, kept in zip(refs[:half], refs[half:]):
-        kept[...] = source[...]
-
-
-def pair_kernel(band, gain, weights, table, pair_norm):
+def pair_kernel(band, sent, table, pair_norm):
     heads = 4
     entries = band.shape[0]
+    _, weights, _, gain = small(sent)
     hat, _ = norm(band[...].astype(F32))
-    normed = (hat * gain[...]).astype(BF)
+    normed = (hat * gain).astype(BF)
     pair_norm[...] = normed
     bias_rows = nt(weight_lines(weights).astype(BF), normed)
     stacked = jnp.concatenate(
@@ -146,7 +176,7 @@
             outgoing[z_hi * 4 + z_lo] = result
 
 
-def band_kernel(device, band, scattered, pair_gain, weights, band_grad):
+def band_kernel(device, band, scattered, sent, band_grad):
     entries = band.shape[0]
     width = band.shape[1]
     z_hi = (device[0] >> 5) & 3
@@ -157,26 +187,62 @@
         rows = rows + [block[:3], turned[:3], block[3:6], turned[3:6]]
     rows = jnp.concatenate(rows + [jnp.zeros((KW - 48, width), F32)], axis=0).astype(BF)
     hat, inv = norm(band[...].astype(F32))
+    _, weights, _, pair_gain = small(sent)
     norm_grad = nn(entry_grads(rows, entries), weight_spread(weights)).astype(BF).astype(F32)
-    result = norm_back(norm_grad * pair_gain[...], hat, inv).astype(BF)
+    result = norm_back(norm_grad * pair_gain, hat, inv).astype(BF)
     slots = band_grad.shape[0]
     for n in range(entries // 16):
         block, slot = divmod(n, slots)
         band_grad[slot, 16 * block : 16 * block + 16, :] = result[16 * n : 16 * n + 16]
 
 
+def head_tokens(own, w):
+    lane = iota((8, KW), 1)
+    row = pltpu.roll(own, (-w % 4) * QW, 1)
+    for h in range(1, 4):
+        row = jnp.where((lane >> 5) == h, pltpu.roll(own, ((h - w) % 4) * QW, 1), row)
+    return row.astype(jnp.int32)[:1]
+
+
+def query_hot(own, w):
+    lane = iota((KW, KW), 1)
+    line = iota((KW, KW), 0)
+    hit = ((line & 15) == head_tokens(own, w)) & (((line >> 4) & 3) == (lane >> 5))
+    return jnp.where(hit, 1.0, 0.0).astype(BF)
+
+
+def prepare_kernel(
+    table, sent, atoms, cotangent, project, combine, rows, normed, projected, gates, gated_grad
+):
+    samples, count, width = atoms.shape
+    tokens, _, gain, _ = small(sent)
+    own = jnp.broadcast_to(tokens, (8, KW))
+    for w in range(count // QW):
+        high, low = split2(tn(table[...], query_hot(own, w)))
+        rows[w] = jnp.concatenate([high, low], axis=0)
+    for s in range(samples):
+        x_hat, _ = norm(atoms[s].astype(F32))
+        x = (x_hat * gain).astype(BF)
+        normed[s] = x
+        columns = nn(x, project[...]).astype(BF)
+        projected[s] = columns
+        gates[s] = jax.nn.sigmoid(columns[:, 3 * width :].astype(F32))
+        gated_grad[s] = nt(cotangent[s], combine[...]).astype(BF)
+
+
 def attention_kernel(
     key_range,
     device,
-    atoms,
     cotangent,
     project,
-    combine,
-    atom_gain,
-    tokens,
+    sent,
     first,
     second,
-    table,
+    rows,
+    normed_own,
+    projected_own,
+    gates,
+    gated_grads,
     pair_norm,
     outgoing,
     to_first,
@@ -185,7 +251,7 @@
     bias,
     bias_grad,
 ):
-    samples, count, width = atoms.shape
+    samples, count, width = cotangent.shape
     heads = 4
     windows = count // QW
     entries = pair_norm.shape[0]
@@ -193,7 +259,8 @@
     lane = iota((KW, KW), 1)
     line = iota((KW, KW), 0)
 
-    own = jnp.broadcast_to((tokens[...] - device[0] * 16).astype(F32), (8, KW))
+    tokens, _, gain, _ = small(sent)
+    own = jnp.broadcast_to(tokens, (8, KW))
     odd = (device[0] & 1) == 0
 
     def sides(x, y):
@@ -203,13 +270,6 @@
     left = left[:8] - 16.0
     right = right[:8] + 16.0
     row_lane = iota((8, KW), 1)
-    turned = [own] + [pltpu.roll(own, h * QW, 1) for h in range(1, heads)]
-
-    def query_row(w):
-        row = turned[(-w) % heads]
-        for h in range(1, heads):
-            row = jnp.where((row_lane >> 5) == h, turned[(h - w) % heads], row)
-        return row.astype(jnp.int32)[:1]
 
     def key_row(w):
         shift = RIM - w * QW
@@ -218,21 +278,16 @@
         row = jnp.where(row_lane < shift, pltpu.roll(one, shift, 1), pltpu.roll(two, shift, 1))
         return row.astype(jnp.int32)[:1] + 16
 
-    def query_hot(w):
-        hit = ((line & 15) == query_row(w)) & (((line >> 4) & 3) == (lane >> 5))
-        return jnp.where(hit, 1.0, 0.0).astype(BF)
-
     def key_hot(w):
         return jnp.where(line == key_row(w), 1.0, 0.0).astype(BF)
 
     for w in range(windows):
-        by_key = nn(table[...], key_hot(w)).astype(BF)
-        values = tn(by_key, query_hot(w))
+        hot = key_hot(w)
+        values = tn(jnp.concatenate([hot, hot], axis=0), rows[w])
         begin = device[0] * count - RIM + w * QW
         allowed = (line >= key_range[w, 0] - begin) & (line < key_range[w, 1] - begin)
         bias[w] = jnp.where(allowed, values, NEG_FILL)
         bias_grad[w] = jnp.zeros((KW, KW), F32)
-    gain = atom_gain[...]
     diag = jnp.where((line >> 5) == (lane >> 5), 1.0, 0.0).astype(BF)
     head_of = iota((QW, width), 1) >> 5
 
@@ -259,17 +314,26 @@
     def sample(s, carry):
         project_sum, combine_sum = carry
         before, after = sides(first[s].astype(F32), second[s].astype(F32))
-        x = jnp.concatenate([before, atoms[s].astype(F32), after], axis=0)
-        x_hat, _ = norm(x)
-        normed = (x_hat * gain).astype(BF)
-        projected = nn(normed, project[...]).astype(BF)
-        query = projected[RIM : RIM + count, :width]
-        key = projected[:, width : 2 * width]
-        value = projected[:, 2 * width : 3 * width]
-        gate = projected[RIM : RIM + count, 3 * width :].astype(F32)
+        x_hat, _ = norm(jnp.concatenate([before, after], axis=0))
+        rims = (x_hat * gain).astype(BF)
+        columns = nn(rims, project[:, width : 3 * width]).astype(BF)
+        own_columns = projected_own[s]
+        normed = jnp.concatenate([rims[:RIM], normed_own[s], rims[RIM:]], axis=0)
+        query = own_columns[:, :width]
+        key, value = [
+            jnp.concatenate(
+                [
+                    columns[:RIM, n * width : (n + 1) * width],
+                    own_columns[:, (n + 1) * width : (n + 2) * width],
+                    columns[RIM:, n * width : (n + 1) * width],
+                ],
+                axis=0,
+            )
+            for n in range(2)
+        ]
         out = cotangent[s]
-        sigmoid = jax.nn.sigmoid(gate)
-        gated_grad = nt(out, combine[...]).astype(BF).astype(F32)
+        sigmoid = gates[s]
+        gated_grad = gated_grads[s].astype(F32)
         mixture_grad = (gated_grad * sigmoid).astype(BF)
         span = range(windows)
         q = [spread_heads(query[w * QW : (w + 1) * QW]) for w in span]
@@ -317,8 +381,8 @@
         hot = key_hot(w)
         by_slot = nn(hot, high) + nn(hot, low)
         high, low = split2(by_slot)
-        rows = query_hot(w)
-        table_grad = table_grad + nt(high, rows) + nt(low, rows)
+        queries = query_hot(own, w)
+        table_grad = table_grad + nt(high, queries) + nt(low, queries)
     spread = iota((KW, entries), 0) == (iota((KW, entries), 1) >> 4)
     spread = jnp.where(spread, 1.0, 0.0).astype(BF)
     entry_grad = tn(table_grad.astype(BF), spread)
@@ -350,15 +414,14 @@
 def last_kernel(
     parts,
     project,
-    atom_gain,
-    pair_gain,
-    weights,
+    sent,
     project_grad,
     combine_grad,
     weight_grad,
     scale_grad,
     gain_grad,
 ):
+    _, weights, atom_gain, pair_gain = small(sent)
     chunks = [parts[p].astype(F32) for p in range(parts.shape[0])]
     rows = jnp.concatenate([x[:16] for x in chunks], axis=0)
     width = rows.shape[1]
@@ -370,17 +433,17 @@
         dots = dots + jnp.sum(block * project[:, columns].astype(F32), axis=1, keepdims=True)
     combine_grad[...] = jnp.concatenate([x[16:20] for x in chunks], axis=0).astype(BF)
     dots = jnp.transpose(jnp.broadcast_to(dots, (width, width)))[:1]
-    scale_grad[...] = dots / atom_gain[...]
+    scale_grad[...] = dots / atom_gain
     tail = jnp.concatenate([x[20:21] for x in chunks[:4]], axis=0)
     weight_grad[...] = tail.astype(BF)
-    dots = jnp.sum(tail * weights[...].astype(F32), axis=0, keepdims=True)
-    gain_grad[...] = dots / pair_gain[...]
-
-
-def finish_kernel(device, atoms, cotangent, own_grad, first, second, atom_gain, result):
+    dots = jnp.sum(tail * weights, axis=0, keepdims=True)
+    gain_grad[...] = dots / pair_gain
+
+
+def finish_kernel(device, atoms, cotangent, own_grad, first, second, sent, result):
     samples, count, width = atoms.shape
     odd = (device[0] & 1) == 0
-    gain = atom_gain[...]
+    _, _, gain, _ = small(sent)
     for s in range(samples):
         x_hat, inv = norm(atoms[s].astype(F32))
         rim = jnp.zeros((count - RIM, width), F32)
@@ -435,18 +498,21 @@
     band_gain = pair_gain.reshape(1, width)
 
     entries = cols * keys * block
-    tiles, first, second = pl.pallas_call(
+    tiles, first, sent = pl.pallas_call(
         start_kernel,
         out_shape=(
             shape((cols, keys, block, width), BF),
             shape((samples + 1, RIM, width), BF),
             shape((samples + 1, RIM, width), BF),
         ),
-        in_specs=smem(1) + anywhere(3),
+        in_specs=smem(1) + anywhere(6),
         out_specs=tuple(vmem(3)),
         scratch_shapes=[
             pltpu.VMEM((1, count), jnp.int32),
-            pltpu.SemaphoreType.DMA((3 + keys,)),
+            pltpu.VMEM(weights.shape, BF),
+            pltpu.VMEM(gain.shape, F32),
+            pltpu.VMEM(band_gain.shape, F32),
+            pltpu.SemaphoreType.DMA((6 + keys,)),
         ],
         compiler_params=pltpu.CompilerParams(vmem_limit_bytes=60 * 1024 * 1024),
         name="start",
@@ -455,30 +521,39 @@
         jnp.transpose(pair_band, (1, 0, 2)).reshape(keys, cols, block, width),
         atoms,
         tokens,
+        weights,
+        gain,
+        band_gain,
     )
     band = lax.all_to_all(tiles, "col", 0, 0, tiled=True).reshape(entries, width)
 
     first = lax.ppermute(first, ("row", "col"), pairs)
-    second = lax.ppermute(second, ("row", "col"), odd_pairs)
-
-    small = [band_gain, weights, gain, tokens]
-    band_gain, weights, gain, tokens = pl.pallas_call(
-        keep_kernel,
-        out_shape=tuple(shape(x.shape, x.dtype) for x in small),
-        in_specs=vmem(4),
-        out_specs=tuple(vmem(4)),
-        compiler_params=LIMIT,
-        name="keep",
-    )(*small)
+    second = lax.ppermute(sent, ("row", "col"), odd_pairs)
+
     table, pair_norm = pl.pallas_call(
         pair_kernel,
         out_shape=(shape((KW, KW), BF), shape((entries, width), BF)),
-        in_specs=vmem(3),
+        in_specs=vmem(2),
         out_specs=tuple(vmem(2)),
         cost_estimate=pl.CostEstimate(flops=10**9, bytes_accessed=10**7, transcendentals=0),
         compiler_params=LIMIT,
         name="pair",
-    )(band, band_gain, weights)
+    )(band, sent)
+    rows, normed, projected, gates, gated_grads = pl.pallas_call(
+        prepare_kernel,
+        out_shape=(
+            shape((windows, 2 * KW, KW), BF),
+            shape((samples, count, width), BF),
+            shape((samples, count, 4 * width), BF),
+            shape((samples, count, width), F32),
+            shape((samples, count, width), BF),
+        ),
+        in_specs=vmem(6),
+        out_specs=tuple(vmem(5)),
+        cost_estimate=pl.CostEstimate(flops=10**9, bytes_accessed=10**7, transcendentals=0),
+        compiler_params=LIMIT,
+        name="prepare",
+    )(table, sent, atoms, cotangent, project, combine)
     outgoing, first, second, own_grad = pl.pallas_call(
         attention_kernel,
         out_shape=(
@@ -487,7 +562,7 @@
             shape((samples, RIM, width), BF),
             shape((samples, count, width), F32),
         ),
-        in_specs=smem(2) + vmem(10),
+        in_specs=smem(2) + vmem(11),
         out_specs=tuple(vmem(4)),
         scratch_shapes=[
             pltpu.VMEM((windows, KW, KW), F32),
@@ -498,15 +573,16 @@
     )(
         key_range,
         device,
-        atoms,
         cotangent,
         project,
-        combine,
-        gain,
-        tokens,
+        sent,
         first,
         second,
-        table,
+        rows,
+        normed,
+        projected,
+        gates,
+        gated_grads,
         pair_norm,
     )
 
@@ -547,11 +623,11 @@
     band_grad = pl.pallas_call(
         band_kernel,
         out_shape=shape((keys, cols * block, width), BF),
-        in_specs=smem(1) + vmem(4),
+        in_specs=smem(1) + vmem(3),
         out_specs=pl.BlockSpec(memory_space=pltpu.VMEM),
         compiler_params=LIMIT,
         name="band",
-    )(device, tiles.reshape(entries, width), scattered, band_gain, weights)
+    )(device, tiles.reshape(entries, width), scattered, sent)
     band_grad = jnp.transpose(band_grad, (1, 0, 2))
     atoms_grad = pl.pallas_call(
         finish_kernel,
@@ -560,7 +636,7 @@
         out_specs=pl.BlockSpec(memory_space=pltpu.VMEM),
         compiler_params=LIMIT,
         name="finish",
-    )(device, atoms, cotangent, own_grad, first, second, gain)
+    )(device, atoms, cotangent, own_grad, first, second, sent)
     part, atoms_grad, band_grad = lax.optimization_barrier((part, atoms_grad, band_grad))
     project_grad, combine_grad, weight_grad, scale_grad, gain_grad = pl.pallas_call(
         last_kernel,
@@ -571,11 +647,11 @@
             shape((1, width), F32),
             shape((1, width), F32),
         ),
-        in_specs=vmem(5),
+        in_specs=vmem(3),
         out_specs=tuple(vmem(5)),
         compiler_params=LIMIT,
         name="last",
-    )(part, project, gain, band_gain, weights)
+    )(part, project, sent)
     return (
         atoms_grad,
         project_grad,

time: 85.7 us -> 85.4 us (level)
    ppermute x0 -> x1, starting transfers between devices: none -> 1.92 us  [shards(): second = lax.ppermute(sent, ('row', 'col'), odd_pairs)]
    ppermute x2 -> x1, starting transfers between devices: 3.84 us -> 1.92 us  [shards(): second = lax.ppermute(second, ('row', 'col'), odd_pairs)]
    ppermute x2 -> x1, waiting for transfers between devices: 1.6 us -> 0.01 us  [shards(): second = lax.ppermute(second, ('row', 'col'), odd_pairs)]
    ppermute x0 -> x1, waiting for transfers between devices: none -> 1.23 us  [shards(): second = lax.ppermute(sent, ('row', 'col'), odd_pairs)]
where the time goes in v9:
time: 85.4 us; the launch traced here: 84.8 us
  starting transfers between devices  42.3 us (50%)
  blocking collectives  18.2 us (21%)
  Pallas kernels  11.7 us (14%)
  waiting for transfers between devices  10.5 us (12%)
  local copies, waits for them, and re-layouts  1.25 us (1%)
    all_to_all x1, blocking collectives, shards(): lax.all_to_all(outgoing, axes, 0, 0, axis_index_groups=planes, tiled=True)  18.2 us
    ppermute x2, starting transfers between devices, shards(): first = lax.ppermute(first, ('row', 'col'), pairs)  15.5 us
    all_to_all x1, starting transfers between devices, shards(): lax.all_to_all(tiles, 'col', 0, 0, tiled=True).reshape(entries, width)  9.16 us
    all_to_all x1, starting transfers between devices, shards(): lax.all_to_all(part, axes, 0, 0, axis_index_groups=lines, tiled=True)  7.03 us
    all_to_all x1, starting transfers between devices, shards(): lax.all_to_all(part, axes, 0, 0, axis_index_groups=planes, tiled=True)  6.81 us
    all_to_all x1, waiting for transfers between devices, shards(): lax.all_to_all(part, axes, 0, 0, axis_index_groups=planes, tiled=True)  5.83 us
    pallas_call x1, Pallas kernels, shards(): pl.pallas_call(attention_kernel, out_shape=(shape((32, 32, width), BF), s...  4.78 us
    all_to_all x1, waiting for transfers between devices, shards(): lax.all_to_all(part, axes, 0, 0, axis_index_groups=lines, tiled=True)  3.42 us
  transfers between devices with their start and end apart: 7, of which 3 were waited for; matrix products, arithmetic and copies ran while one was open for 0% of the time, Pallas kernels for 4%

profile of v9, /device:TPU:1, one launch (start us, length us, event | category | flops | bytes accessed | tf_op | source)
XLA Modules:
  0.0 84.8 jit_solution(12260264860631099102)
XLA Ops:
  0.6 1.8 %start.1 = (bf16[16,3,16,128]{3,2,1,0:T(8,128)(2,1)}, bf16[5,48,128]{2,1,0:T(8,128)(2,1)}, bf16[5,48,128]{2,1,0:T(8,128)(2,1)}) custom-call(s32[1]{0:T(128)} %bitcast.device, bf16[3,16,16,128]{3,2,1,0:T(8,128)(2,1)} %bitcast.16, bf16[4,128,128]{2,1,0:T(8,128)(2,1)} %atoms.5, s32[1,128]{1,0:T(1,128)} %bitcast.19, bf16[4,128]{1,0:T(4,128)(2,1)} %bitcast.18, ...), custom_call_target="tpu_custom_call" | custom-call | tf_op jit(solution)/shard_map/start/pallas_call | solution.py:501
  2.4 9.2 %all-to-all-start = ((bf16[16,3,16,128]{3,2,1,0:T(8,128)(2,1)}), bf16[16,3,16,128]{3,2,1,0:T(8,128)(2,1)S(1)}, u32[]{:S(2)}, u32[]{:S(2)}) async-start(bf16[16,3,16,128]{3,2,1,0:T(8,128)(2,1)} %get-tuple-element.37), calls=%async_computation | async-start | bytes 393216 | tf_op jit(solution)/shard_map/all_to_all | solution.py:528
  11.6 8.7 %collective-permute-start = (bf16[5,48,128]{2,1,0:T(8,128)(2,1)S(1)}, bf16[5,48,128]{2,1,0:T(8,128)(2,1)S(1)}, u32[]{:S(2)}, u32[]{:S(2)}) collective-permute-start(bf16[5,48,128]{2,1,0:T(8,128)(2,1)S(1)} %copy-done.7), channel_id=1, source_target_pairs={{1,2},{2,1},{3,4},{4,3},{5,6},{6,5},{7,8},{8,7},{9,10},{10,9},{11,... | collective-permute-start | bytes 184328 | tf_op jit(solution)/shard_map/ppermute | solution.py:530
  20.4 1.9 %collective-permute-start.1 = (bf16[5,48,128]{2,1,0:T(8,128)(2,1)S(1)}, bf16[5,48,128]{2,1,0:T(8,128)(2,1)S(1)}, u32[]{:S(2)}, u32[]{:S(2)}) collective-permute-start(bf16[5,48,128]{2,1,0:T(8,128)(2,1)S(1)} %copy-done), channel_id=1, source_target_pairs={{0,1},{1,0},{2,3},{3,2},{4,5},{5,4},{6,7},{7,6},{8,9},{9,8},{10,11... | collective-permute-start | bytes 184328 | tf_op jit(solution)/shard_map/ppermute | solution.py:531
  22.3 0.1 copy.17.key_range
  22.4 0.6 pair.1
  23.0 0.3 copy-done.2
  23.3 0.1 copy-done.3
  23.4 0.1 copy-done.4
  23.4 0.7 prepare.1
  24.1 1.2 %collective-permute-done.1.second = bf16[5,48,128]{2,1,0:T(8,128)(2,1)S(1)} collective-permute-done((bf16[5,48,128]{2,1,0:T(8,128)(2,1)S(1)}, bf16[5,48,128]{2,1,0:T(8,128)(2,1)S(1)}, u32[]{:S(2)}, u32[]{:S(2)}) %collective-permute-start.1) | collective-permute-done | bytes 61472 | tf_op jit(solution)/shard_map/ppermute | solution.py:531
  25.3 4.8 %attention.1 = (bf16[32,32,128]{2,1,0:T(8,128)(2,1)S(1)}, bf16[4,48,128]{2,1,0:T(8,128)(2,1)S(1)}, bf16[4,48,128]{2,1,0:T(8,128)(2,1)S(1)}, f32[4,128,128]{2,1,0:T(8,128)S(1)}) custom-call(s32[4,2]{1,0:T(4,128)S(1)} %copy.17.key_range, s32[1]{0:T(128)} %bitcast.device, bf16[4,128,128]{2,1,0:T(8,128)(2,1)S(1)} %copy-done.3, bf16[128,512]{1,0:T(8,128)(2,1)S(1)} %copy-done.2, ...), custom_call_target="tpu_custom_call" | custom-call | tf_op jit(solution)/shard_map/attention/pallas_call | solution.py:557
  30.1 18.2 %all_to_all.20.scattered = bf16[32,32,128]{2,1,0:T(8,128)(2,1)S(1)} all-to-all(bf16[32,32,128]{2,1,0:T(8,128)(2,1)S(1)} %get-tuple-element.45), channel_id=1, replica_groups={{0,1,2,3,16,17,18,19,128,129,130,131,144,145,146,147,256,257,258,259,27..., dimensions={0} | all-to-all | bytes 524288 | tf_op jit(solution)/shard_map/all_to_all | solution.py:605
  48.3 0.7 middle.1
  49.1 7.0 %all-to-all-start.2 = ((bf16[16,32,128]{2,1,0:T(8,128)(2,1)}), bf16[16,32,128]{2,1,0:T(8,128)(2,1)S(1)}, u32[]{:S(2)}, u32[]{:S(2)}) async-start(bf16[16,32,128]{2,1,0:T(8,128)(2,1)} %middle.1), calls=%async_computation.2 | async-start | bytes 262144 | tf_op jit(solution)/shard_map/all_to_all | solution.py:616
  56.1 6.8 %collective-permute-start.2 = (bf16[4,48,128]{2,1,0:T(8,128)(2,1)S(1)}, bf16[4,48,128]{2,1,0:T(8,128)(2,1)S(1)}, u32[]{:S(2)}, u32[]{:S(2)}) collective-permute-start(bf16[4,48,128]{2,1,0:T(8,128)(2,1)S(1)} %get-tuple-element.49), channel_id=1, source_target_pairs={{1,2},{2,1},{3,4},{4,3},{5,6},{6,5},{7,8},{8,7},{9,10},{10,9},{11,... | collective-permute-start | bytes 147464 | tf_op jit(solution)/shard_map/ppermute | solution.py:617
  62.9 1.9 %collective-permute-start.3 = (bf16[4,48,128]{2,1,0:T(8,128)(2,1)S(1)}, bf16[4,48,128]{2,1,0:T(8,128)(2,1)S(1)}, u32[]{:S(2)}, u32[]{:S(2)}) collective-permute-start(bf16[4,48,128]{2,1,0:T(8,128)(2,1)S(1)} %get-tuple-element.50), channel_id=1, source_target_pairs={{0,1},{1,0},{2,3},{3,2},{4,5},{5,4},{6,7},{7,6},{8,9},{9,8},{10,11... | collective-permute-start | bytes 147464 | tf_op jit(solution)/shard_map/ppermute | solution.py:618
  64.8 3.4 %all-to-all-done.2.scattered = bf16[16,32,128]{2,1,0:T(8,128)(2,1)S(1)} async-done(((bf16[16,32,128]{2,1,0:T(8,128)(2,1)}), bf16[16,32,128]{2,1,0:T(8,128)(2,1)S(1)}, u32[]{:S(2)}, u32[]{:S(2)}) %all-to-all-start.2) | async-done | bytes 131104 | tf_op jit(solution)/shard_map/all_to_all | solution.py:616
  68.3 0.7 broadcast_in_dim.3
  69.0 6.8 %all-to-all-start.3 = ((bf16[32,24,128]{2,1,0:T(8,128)(2,1)}), bf16[32,24,128]{2,1,0:T(8,128)(2,1)S(1)}, u32[]{:S(2)}, u32[]{:S(2)}) async-start(bf16[32,24,128]{2,1,0:T(8,128)(2,1)} %broadcast_in_dim.3), calls=%async_computation.3 | async-start | bytes 393216 | tf_op jit(solution)/shard_map/all_to_all | solution.py:622
  75.8 1.1 %finish.1 = bf16[4,128,128]{2,1,0:T(8,128)(2,1)} custom-call(s32[1]{0:T(128)} %bitcast.device, bf16[4,128,128]{2,1,0:T(8,128)(2,1)S(1)} %copy-done.4, bf16[4,128,128]{2,1,0:T(8,128)(2,1)S(1)} %copy-done.3, f32[4,128,128]{2,1,0:T(8,128)S(1)} %get-tuple-element.52.own_grad, bf16[4,48,128]{2,1,0:T(8,128)(2,1)S(1)} %collective-permute-done.2.first, ...), custom_call_target="tpu_custom_call" | custom-call | tf_op jit(solution)/shard_map/finish/pallas_call | solution.py:632
  76.9 1.3 %band.1 = bf16[3,256,128]{2,1,0:T(8,128)(2,1)} custom-call(s32[1]{0:T(128)} %bitcast.device, bf16[768,128]{1,0:T(8,128)(2,1)S(1)} %bitcast.14, bf16[16,32,128]{2,1,0:T(8,128)(2,1)S(1)} %all-to-all-done.2.scattered, bf16[5,48,128]{2,1,0:T(8,128)(2,1)S(1)} %copy-done), custom_call_target="tpu_custom_call" | custom-call | tf_op jit(solution)/shard_map/band/pallas_call | solution.py:623
  78.2 5.8 %all-to-all-done.3.parts = bf16[32,24,128]{2,1,0:T(8,128)(2,1)S(1)} async-done(((bf16[32,24,128]{2,1,0:T(8,128)(2,1)}), bf16[32,24,128]{2,1,0:T(8,128)(2,1)S(1)}, u32[]{:S(2)}, u32[]{:S(2)}) %all-to-all-start.3) | async-done | bytes 196640 | tf_op jit(solution)/shard_map/all_to_all | solution.py:622
  84.1 0.8 last.1
  (18 shorter events, 0.1 us)
Async XLA Ops:
  2.4 9.2 %copy-start.7 = (bf16[5,48,128]{2,1,0:T(8,128)(2,1)S(1)}, bf16[5,48,128]{2,1,0:T(8,128)(2,1)}, u32[]{:S(2)}) copy-start(bf16[5,48,128]{2,1,0:T(8,128)(2,1)} %get-tuple-element.36) | copy-start | bytes 184324
  2.4 17.9 %copy-start = (bf16[5,48,128]{2,1,0:T(8,128)(2,1)S(1)}, bf16[5,48,128]{2,1,0:T(8,128)(2,1)}, u32[]{:S(2)}) copy-start(bf16[5,48,128]{2,1,0:T(8,128)(2,1)} %get-tuple-element.35.sent) | copy-start | bytes 184324
  2.4 19.9 %all-to-all-start = ((bf16[16,3,16,128]{3,2,1,0:T(8,128)(2,1)}), bf16[16,3,16,128]{3,2,1,0:T(8,128)(2,1)S(1)}, u32[]{:S(2)}, u32[]{:S(2)}) async-start(bf16[16,3,16,128]{3,2,1,0:T(8,128)(2,1)} %get-tuple-element.37), calls=%async_computation | async-start | bytes 393216 | tf_op jit(solution)/shard_map/all_to_all | solution.py:528
  11.6 10.7 %copy-start.6 = (s32[4,2]{0,1:T(2,128)S(1)}, s32[4,2]{0,1:T(2,128)}, u32[]{:S(2)}) copy-start(s32[4,2]{0,1:T(2,128)} %param.19) | copy-start | bytes 100
  11.6 12.5 %collective-permute-start = (bf16[5,48,128]{2,1,0:T(8,128)(2,1)S(1)}, bf16[5,48,128]{2,1,0:T(8,128)(2,1)S(1)}, u32[]{:S(2)}, u32[]{:S(2)}) collective-permute-start(bf16[5,48,128]{2,1,0:T(8,128)(2,1)S(1)} %copy-done.7), channel_id=1, source_target_pairs={{1,2},{2,1},{3,4},{4,3},{5,6},{6,5},{7,8},{8,7},{9,10},{10,9},{11,... | collective-permute-start | bytes 184328 | tf_op jit(solution)/shard_map/ppermute | solution.py:530
  20.4 5.0 %collective-permute-start.1 = (bf16[5,48,128]{2,1,0:T(8,128)(2,1)S(1)}, bf16[5,48,128]{2,1,0:T(8,128)(2,1)S(1)}, u32[]{:S(2)}, u32[]{:S(2)}) collective-permute-start(bf16[5,48,128]{2,1,0:T(8,128)(2,1)S(1)} %copy-done), channel_id=1, source_target_pairs={{0,1},{1,0},{2,3},{3,2},{4,5},{5,4},{6,7},{7,6},{8,9},{9,8},{10,11... | collective-permute-start | bytes 184328 | tf_op jit(solution)/shard_map/ppermute | solution.py:531
  22.4 0.9 %copy-start.2 = (bf16[128,512]{1,0:T(8,128)(2,1)S(1)}, bf16[128,512]{1,0:T(8,128)(2,1)}, u32[]{:S(2)}) copy-start(bf16[128,512]{1,0:T(8,128)(2,1)} %project.5) | copy-start | bytes 393220
  22.4 1.0 %copy-start.3 = (bf16[4,128,128]{2,1,0:T(8,128)(2,1)S(1)}, bf16[4,128,128]{2,1,0:T(8,128)(2,1)}, u32[]{:S(2)}) copy-start(bf16[4,128,128]{2,1,0:T(8,128)(2,1)} %cotangent.5) | copy-start | bytes 393220
  22.4 1.0 %copy-start.4 = (bf16[4,128,128]{2,1,0:T(8,128)(2,1)S(1)}, bf16[4,128,128]{2,1,0:T(8,128)(2,1)}, u32[]{:S(2)}) copy-start(bf16[4,128,128]{2,1,0:T(8,128)(2,1)} %atoms.5) | copy-start | bytes 393220
  22.4 1.0 %copy-start.5 = (bf16[128,128]{1,0:T(8,128)(2,1)S(1)}, bf16[128,128]{1,0:T(8,128)(2,1)}, u32[]{:S(2)}) copy-start(bf16[128,128]{1,0:T(8,128)(2,1)} %combine.1) | copy-start | bytes 98308
  49.1 19.2 %all-to-all-start.2 = ((bf16[16,32,128]{2,1,0:T(8,128)(2,1)}), bf16[16,32,128]{2,1,0:T(8,128)(2,1)S(1)}, u32[]{:S(2)}, u32[]{:S(2)}) async-start(bf16[16,32,128]{2,1,0:T(8,128)(2,1)} %middle.1), calls=%async_computation.2 | async-start | bytes 262144 | tf_op jit(solution)/shard_map/all_to_all | solution.py:616
  56.1 12.2 %collective-permute-start.2 = (bf16[4,48,128]{2,1,0:T(8,128)(2,1)S(1)}, bf16[4,48,128]{2,1,0:T(8,128)(2,1)S(1)}, u32[]{:S(2)}, u32[]{:S(2)}) collective-permute-start(bf16[4,48,128]{2,1,0:T(8,128)(2,1)S(1)} %get-tuple-element.49), channel_id=1, source_target_pairs={{1,2},{2,1},{3,4},{4,3},{5,6},{6,5},{7,8},{8,7},{9,10},{10,9},{11,... | collective-permute-start | bytes 147464 | tf_op jit(solution)/shard_map/ppermute | solution.py:617
  62.9 5.4 %collective-permute-start.3 = (bf16[4,48,128]{2,1,0:T(8,128)(2,1)S(1)}, bf16[4,48,128]{2,1,0:T(8,128)(2,1)S(1)}, u32[]{:S(2)}, u32[]{:S(2)}) collective-permute-start(bf16[4,48,128]{2,1,0:T(8,128)(2,1)S(1)} %get-tuple-element.50), channel_id=1, source_target_pairs={{0,1},{1,0},{2,3},{3,2},{4,5},{5,4},{6,7},{7,6},{8,9},{9,8},{10,11... | collective-permute-start | bytes 147464 | tf_op jit(solution)/shard_map/ppermute | solution.py:618
  69.0 15.1 %all-to-all-start.3 = ((bf16[32,24,128]{2,1,0:T(8,128)(2,1)}), bf16[32,24,128]{2,1,0:T(8,128)(2,1)S(1)}, u32[]{:S(2)}, u32[]{:S(2)}) async-start(bf16[32,24,128]{2,1,0:T(8,128)(2,1)} %broadcast_in_dim.3), calls=%async_computation.3 | async-start | bytes 393216 | tf_op jit(solution)/shard_map/all_to_all | solution.py:622
  75.8 1.1 %copy-start.1 = (bf16[16,3,16,128]{3,2,1,0:T(8,128)(2,1)S(1)}, bf16[16,3,16,128]{3,2,1,0:T(8,128)(2,1)}, u32[]{:S(2)}) copy-start(bf16[16,3,16,128]{3,2,1,0:T(8,128)(2,1)} %get-tuple-element.37) | copy-start | bytes 589828

commit v10 on v9

--- a/solution.py
+++ b/solution.py
@@ -174,6 +174,15 @@
         result = jnp.concatenate([total[:24]] + tables, axis=0).astype(BF)
         for z_hi in range(4):
             outgoing[z_hi * 4 + z_lo] = result
+
+
+def spread_kernel(scattered, outgoing):
+    total = scattered[0].astype(F32)
+    for q in range(1, scattered.shape[0]):
+        total = total + scattered[q].astype(F32)
+    total = total[:24].astype(BF)
+    for p in range(outgoing.shape[0]):
+        outgoing[p] = total
 
 
 def band_kernel(device, band, scattered, sent, band_grad):
@@ -364,8 +373,8 @@
         project_sum = project_sum + tn(normed, grad)
         normed_grad = nt(grad, project[...])
         before, after = sides(normed_grad[:RIM], normed_grad[RIM + count :])
-        to_first[s] = before.astype(BF)
-        to_second[s] = after.astype(BF)
+        to_first[s] = after.astype(BF)
+        to_second[s] = before.astype(BF)
         own_grad[s] = normed_grad[RIM : RIM + count]
         return project_sum, combine_sum
 
@@ -442,7 +451,7 @@
 
 def finish_kernel(device, atoms, cotangent, own_grad, first, second, sent, result):
     samples, count, width = atoms.shape
-    odd = (device[0] & 1) == 0
+    odd = (device[0] & 1) == 1
     _, _, gain, _ = small(sent)
     for s in range(samples):
         x_hat, inv = norm(atoms[s].astype(F32))
@@ -614,11 +623,17 @@
 
     part, first, second = lax.optimization_barrier((part, first, second))
     scattered = lax.all_to_all(part, axes, 0, 0, axis_index_groups=lines, tiled=True)
-    first = lax.ppermute(first, ("row", "col"), pairs)
-    second = lax.ppermute(second, ("row", "col"), odd_pairs)
-    part = jnp.sum(scattered[:, :24].astype(F32), axis=0).astype(BF)
-    part, first, second = lax.optimization_barrier((part, first, second))
-    part = jnp.broadcast_to(part, (32,) + part.shape)
+    first = lax.ppermute(first, ("row", "col"), odd_pairs)
+    second = lax.ppermute(second, ("row", "col"), pairs)
+    scattered, first, second = lax.optimization_barrier((scattered, first, second))
+    part = pl.pallas_call(
+        spread_kernel,
+        out_shape=shape((32, 24, width), BF),
+        in_specs=vmem(1),
+        out_specs=pl.BlockSpec(memory_space=pltpu.VMEM),
+        compiler_params=LIMIT,
+        name="spread",
+    )(scattered)
     part = lax.all_to_all(part, axes, 0, 0, axis_index_groups=planes, tiled=True)
     band_grad = pl.pallas_call(
         band_kernel,

time: 85.4 us -> 85.4 us (level)
    ppermute x1 -> x2, starting transfers between devices: 1.92 us -> 9.01 us  [the longest x1 6.82 us: shards(): second = lax.ppermute(second, ('row', 'col'), pairs)]
    ppermute x2 -> x1, starting transfers between devices: 15.5 us -> 8.7 us  [shards(): first = lax.ppermute(first, ('row', 'col'), pairs)]
    all_to_all x1, waiting for transfers between devices: 3.42 us -> 0.01 us  [shards(): lax.all_to_all(part, axes, 0, 0, axis_index_groups=lines, tiled=True)]
    ppermute x1 -> x2, waiting for transfers between devices: 0.01 us -> 3.28 us  [the longest x1 3.27 us: shards(): second = lax.ppermute(second, ('row', 'col'), pairs)]
where the time goes in v10:
time: 85.4 us; the launch traced here: 84.9 us
  starting transfers between devices  42.5 us (50%)
  blocking collectives  18.2 us (21%)
  Pallas kernels  12.4 us (15%)
  waiting for transfers between devices  10.3 us (12%)
    all_to_all x1, blocking collectives, shards(): lax.all_to_all(outgoing, axes, 0, 0, axis_index_groups=planes, tiled=True)  18.2 us
    all_to_all x1, starting transfers between devices, shards(): lax.all_to_all(tiles, 'col', 0, 0, tiled=True).reshape(entries, width)  9.16 us
    ppermute x1, starting transfers between devices, shards(): first = lax.ppermute(first, ('row', 'col'), pairs)  8.7 us
    all_to_all x1, starting transfers between devices, shards(): lax.all_to_all(part, axes, 0, 0, axis_index_groups=lines, tiled=True)  7.03 us
    ppermute x1, starting transfers between devices, shards(): second = lax.ppermute(second, ('row', 'col'), pairs)  6.82 us
    all_to_all x1, starting transfers between devices, shards(): lax.all_to_all(part, axes, 0, 0, axis_index_groups=planes, tiled=True)  6.71 us
    all_to_all x1, waiting for transfers between devices, shards(): lax.all_to_all(part, axes, 0, 0, axis_index_groups=planes, tiled=True)  5.84 us
    pallas_call x1, Pallas kernels, shards(): pl.pallas_call(attention_kernel, out_shape=(shape((32, 32, width), BF), s...  4.78 us
  transfers between devices with their start and end apart: 7, of which 3 were waited for; matrix products, arithmetic and copies ran while one was open for 0% of the time, Pallas kernels for 4%

profile of v10, /device:TPU:1, one launch (start us, length us, event | category | flops | bytes accessed | tf_op | source)
XLA Modules:
  0.0 84.9 jit_solution(4616154820324290789)
XLA Ops:
  0.6 1.8 %start.1 = (bf16[16,3,16,128]{3,2,1,0:T(8,128)(2,1)}, bf16[5,48,128]{2,1,0:T(8,128)(2,1)}, bf16[5,48,128]{2,1,0:T(8,128)(2,1)}) custom-call(s32[1]{0:T(128)} %bitcast.device, bf16[3,16,16,128]{3,2,1,0:T(8,128)(2,1)} %bitcast.16, bf16[4,128,128]{2,1,0:T(8,128)(2,1)} %atoms.5, s32[1,128]{1,0:T(1,128)} %bitcast.19, bf16[4,128]{1,0:T(4,128)(2,1)} %bitcast.18, ...), custom_call_target="tpu_custom_call" | custom-call | tf_op jit(solution)/shard_map/start/pallas_call | solution.py:510
  2.4 9.2 %all-to-all-start = ((bf16[16,3,16,128]{3,2,1,0:T(8,128)(2,1)}), bf16[16,3,16,128]{3,2,1,0:T(8,128)(2,1)S(1)}, u32[]{:S(2)}, u32[]{:S(2)}) async-start(bf16[16,3,16,128]{3,2,1,0:T(8,128)(2,1)} %get-tuple-element.37), calls=%async_computation | async-start | bytes 393216 | tf_op jit(solution)/shard_map/all_to_all | solution.py:537
  11.6 8.7 %collective-permute-start = (bf16[5,48,128]{2,1,0:T(8,128)(2,1)S(1)}, bf16[5,48,128]{2,1,0:T(8,128)(2,1)S(1)}, u32[]{:S(2)}, u32[]{:S(2)}) collective-permute-start(bf16[5,48,128]{2,1,0:T(8,128)(2,1)S(1)} %copy-done.7), channel_id=1, source_target_pairs={{1,2},{2,1},{3,4},{4,3},{5,6},{6,5},{7,8},{8,7},{9,10},{10,9},{11,... | collective-permute-start | bytes 184328 | tf_op jit(solution)/shard_map/ppermute | solution.py:539
  20.4 1.9 %collective-permute-start.1 = (bf16[5,48,128]{2,1,0:T(8,128)(2,1)S(1)}, bf16[5,48,128]{2,1,0:T(8,128)(2,1)S(1)}, u32[]{:S(2)}, u32[]{:S(2)}) collective-permute-start(bf16[5,48,128]{2,1,0:T(8,128)(2,1)S(1)} %copy-done), channel_id=1, source_target_pairs={{0,1},{1,0},{2,3},{3,2},{4,5},{5,4},{6,7},{7,6},{8,9},{9,8},{10,11... | collective-permute-start | bytes 184328 | tf_op jit(solution)/shard_map/ppermute | solution.py:540
  22.3 0.1 copy.17.key_range
  22.4 0.6 pair.1
  23.0 0.3 copy-done.2
  23.3 0.1 copy-done.3
  23.4 0.1 copy-done.4
  23.4 0.7 prepare.1
  24.1 1.2 %collective-permute-done.1.second = bf16[5,48,128]{2,1,0:T(8,128)(2,1)S(1)} collective-permute-done((bf16[5,48,128]{2,1,0:T(8,128)(2,1)S(1)}, bf16[5,48,128]{2,1,0:T(8,128)(2,1)S(1)}, u32[]{:S(2)}, u32[]{:S(2)}) %collective-permute-start.1) | collective-permute-done | bytes 61472 | tf_op jit(solution)/shard_map/ppermute | solution.py:540
  25.3 4.8 %attention.1 = (bf16[32,32,128]{2,1,0:T(8,128)(2,1)S(1)}, bf16[4,48,128]{2,1,0:T(8,128)(2,1)S(1)}, bf16[4,48,128]{2,1,0:T(8,128)(2,1)S(1)}, f32[4,128,128]{2,1,0:T(8,128)S(1)}) custom-call(s32[4,2]{1,0:T(4,128)S(1)} %copy.17.key_range, s32[1]{0:T(128)} %bitcast.device, bf16[4,128,128]{2,1,0:T(8,128)(2,1)S(1)} %copy-done.3, bf16[128,512]{1,0:T(8,128)(2,1)S(1)} %copy-done.2, ...), custom_call_target="tpu_custom_call" | custom-call | tf_op jit(solution)/shard_map/attention/pallas_call | solution.py:566
  30.1 18.2 %all_to_all.20.scattered = bf16[32,32,128]{2,1,0:T(8,128)(2,1)S(1)} all-to-all(bf16[32,32,128]{2,1,0:T(8,128)(2,1)S(1)} %get-tuple-element.45), channel_id=1, replica_groups={{0,1,2,3,16,17,18,19,128,129,130,131,144,145,146,147,256,257,258,259,27..., dimensions={0} | all-to-all | bytes 524288 | tf_op jit(solution)/shard_map/all_to_all | solution.py:614
  48.3 0.7 middle.1
  49.1 7.0 %all-to-all-start.2 = ((bf16[16,32,128]{2,1,0:T(8,128)(2,1)}), bf16[16,32,128]{2,1,0:T(8,128)(2,1)S(1)}, u32[]{:S(2)}, u32[]{:S(2)}) async-start(bf16[16,32,128]{2,1,0:T(8,128)(2,1)} %middle.1), calls=%async_computation.2 | async-start | bytes 262144 | tf_op jit(solution)/shard_map/all_to_all | solution.py:625
  56.1 2.2 %collective-permute-start.2 = (bf16[4,48,128]{2,1,0:T(8,128)(2,1)S(1)}, bf16[4,48,128]{2,1,0:T(8,128)(2,1)S(1)}, u32[]{:S(2)}, u32[]{:S(2)}) collective-permute-start(bf16[4,48,128]{2,1,0:T(8,128)(2,1)S(1)} %get-tuple-element.49), channel_id=1, source_target_pairs={{0,1},{1,0},{2,3},{3,2},{4,5},{5,4},{6,7},{7,6},{8,9},{9,8},{10,11... | collective-permute-start | bytes 147464 | tf_op jit(solution)/shard_map/ppermute | solution.py:626
  58.3 6.8 %collective-permute-start.3 = (bf16[4,48,128]{2,1,0:T(8,128)(2,1)S(1)}, bf16[4,48,128]{2,1,0:T(8,128)(2,1)S(1)}, u32[]{:S(2)}, u32[]{:S(2)}) collective-permute-start(bf16[4,48,128]{2,1,0:T(8,128)(2,1)S(1)} %get-tuple-element.50), channel_id=1, source_target_pairs={{1,2},{2,1},{3,4},{4,3},{5,6},{6,5},{7,8},{8,7},{9,10},{10,9},{11,... | collective-permute-start | bytes 147464 | tf_op jit(solution)/shard_map/ppermute | solution.py:627
  65.1 3.3 %collective-permute-done.3.second = bf16[4,48,128]{2,1,0:T(8,128)(2,1)S(1)} collective-permute-done((bf16[4,48,128]{2,1,0:T(8,128)(2,1)S(1)}, bf16[4,48,128]{2,1,0:T(8,128)(2,1)S(1)}, u32[]{:S(2)}, u32[]{:S(2)}) %collective-permute-start.3) | collective-permute-done | bytes 49184 | tf_op jit(solution)/shard_map/ppermute | solution.py:627
  68.4 0.7 spread.1
  69.1 6.7 %all-to-all-start.3 = ((bf16[32,24,128]{2,1,0:T(8,128)(2,1)}), bf16[32,24,128]{2,1,0:T(8,128)(2,1)S(1)}, u32[]{:S(2)}, u32[]{:S(2)}) async-start(bf16[32,24,128]{2,1,0:T(8,128)(2,1)} %spread.1), calls=%async_computation.3 | async-start | bytes 393216 | tf_op jit(solution)/shard_map/all_to_all | solution.py:637
  75.8 1.3 %band.1 = bf16[3,256,128]{2,1,0:T(8,128)(2,1)} custom-call(s32[1]{0:T(128)} %bitcast.device, bf16[768,128]{1,0:T(8,128)(2,1)S(1)} %bitcast.14, bf16[16,32,128]{2,1,0:T(8,128)(2,1)S(1)} %all-to-all-done.2.scattered, bf16[5,48,128]{2,1,0:T(8,128)(2,1)S(1)} %copy-done), custom_call_target="tpu_custom_call" | custom-call | tf_op jit(solution)/shard_map/band/pallas_call | solution.py:638
  77.1 1.1 %finish.1 = bf16[4,128,128]{2,1,0:T(8,128)(2,1)} custom-call(s32[1]{0:T(128)} %bitcast.device, bf16[4,128,128]{2,1,0:T(8,128)(2,1)S(1)} %copy-done.4, bf16[4,128,128]{2,1,0:T(8,128)(2,1)S(1)} %copy-done.3, f32[4,128,128]{2,1,0:T(8,128)S(1)} %get-tuple-element.52.own_grad, bf16[4,48,128]{2,1,0:T(8,128)(2,1)S(1)} %collective-permute-done.2.first, ...), custom_call_target="tpu_custom_call" | custom-call | tf_op jit(solution)/shard_map/finish/pallas_call | solution.py:647
  78.3 5.8 %all-to-all-done.3.parts = bf16[32,24,128]{2,1,0:T(8,128)(2,1)S(1)} async-done(((bf16[32,24,128]{2,1,0:T(8,128)(2,1)}), bf16[32,24,128]{2,1,0:T(8,128)(2,1)S(1)}, u32[]{:S(2)}, u32[]{:S(2)}) %all-to-all-start.3) | async-done | bytes 196640 | tf_op jit(solution)/shard_map/all_to_all | solution.py:637
  84.1 0.8 last.1
  (17 shorter events, 0.0 us)
Async XLA Ops:
  2.4 9.2 %copy-start.7 = (bf16[5,48,128]{2,1,0:T(8,128)(2,1)S(1)}, bf16[5,48,128]{2,1,0:T(8,128)(2,1)}, u32[]{:S(2)}) copy-start(bf16[5,48,128]{2,1,0:T(8,128)(2,1)} %get-tuple-element.36) | copy-start | bytes 184324
  2.4 17.9 %copy-start = (bf16[5,48,128]{2,1,0:T(8,128)(2,1)S(1)}, bf16[5,48,128]{2,1,0:T(8,128)(2,1)}, u32[]{:S(2)}) copy-start(bf16[5,48,128]{2,1,0:T(8,128)(2,1)} %get-tuple-element.35.sent) | copy-start | bytes 184324
  2.4 19.9 %all-to-all-start = ((bf16[16,3,16,128]{3,2,1,0:T(8,128)(2,1)}), bf16[16,3,16,128]{3,2,1,0:T(8,128)(2,1)S(1)}, u32[]{:S(2)}, u32[]{:S(2)}) async-start(bf16[16,3,16,128]{3,2,1,0:T(8,128)(2,1)} %get-tuple-element.37), calls=%async_computation | async-start | bytes 393216 | tf_op jit(solution)/shard_map/all_to_all | solution.py:537
  11.6 10.7 %copy-start.6 = (s32[4,2]{0,1:T(2,128)S(1)}, s32[4,2]{0,1:T(2,128)}, u32[]{:S(2)}) copy-start(s32[4,2]{0,1:T(2,128)} %param.19) | copy-start | bytes 100
  11.6 12.5 %collective-permute-start = (bf16[5,48,128]{2,1,0:T(8,128)(2,1)S(1)}, bf16[5,48,128]{2,1,0:T(8,128)(2,1)S(1)}, u32[]{:S(2)}, u32[]{:S(2)}) collective-permute-start(bf16[5,48,128]{2,1,0:T(8,128)(2,1)S(1)} %copy-done.7), channel_id=1, source_target_pairs={{1,2},{2,1},{3,4},{4,3},{5,6},{6,5},{7,8},{8,7},{9,10},{10,9},{11,... | collective-permute-start | bytes 184328 | tf_op jit(solution)/shard_map/ppermute | solution.py:539
  20.4 5.0 %collective-permute-start.1 = (bf16[5,48,128]{2,1,0:T(8,128)(2,1)S(1)}, bf16[5,48,128]{2,1,0:T(8,128)(2,1)S(1)}, u32[]{:S(2)}, u32[]{:S(2)}) collective-permute-start(bf16[5,48,128]{2,1,0:T(8,128)(2,1)S(1)} %copy-done), channel_id=1, source_target_pairs={{0,1},{1,0},{2,3},{3,2},{4,5},{5,4},{6,7},{7,6},{8,9},{9,8},{10,11... | collective-permute-start | bytes 184328 | tf_op jit(solution)/shard_map/ppermute | solution.py:540
  22.4 0.9 %copy-start.2 = (bf16[128,512]{1,0:T(8,128)(2,1)S(1)}, bf16[128,512]{1,0:T(8,128)(2,1)}, u32[]{:S(2)}) copy-start(bf16[128,512]{1,0:T(8,128)(2,1)} %project.5) | copy-start | bytes 393220
  22.4 1.0 %copy-start.3 = (bf16[4,128,128]{2,1,0:T(8,128)(2,1)S(1)}, bf16[4,128,128]{2,1,0:T(8,128)(2,1)}, u32[]{:S(2)}) copy-start(bf16[4,128,128]{2,1,0:T(8,128)(2,1)} %cotangent.5) | copy-start | bytes 393220
  22.4 1.0 %copy-start.4 = (bf16[4,128,128]{2,1,0:T(8,128)(2,1)S(1)}, bf16[4,128,128]{2,1,0:T(8,128)(2,1)}, u32[]{:S(2)}) copy-start(bf16[4,128,128]{2,1,0:T(8,128)(2,1)} %atoms.5) | copy-start | bytes 393220
  22.4 1.0 %copy-start.5 = (bf16[128,128]{1,0:T(8,128)(2,1)S(1)}, bf16[128,128]{1,0:T(8,128)(2,1)}, u32[]{:S(2)}) copy-start(bf16[128,128]{1,0:T(8,128)(2,1)} %combine.1) | copy-start | bytes 98308
  49.1 19.4 %all-to-all-start.2 = ((bf16[16,32,128]{2,1,0:T(8,128)(2,1)}), bf16[16,32,128]{2,1,0:T(8,128)(2,1)S(1)}, u32[]{:S(2)}, u32[]{:S(2)}) async-start(bf16[16,32,128]{2,1,0:T(8,128)(2,1)} %middle.1), calls=%async_computation.2 | async-start | bytes 262144 | tf_op jit(solution)/shard_map/all_to_all | solution.py:625
  56.1 9.0 %collective-permute-start.2 = (bf16[4,48,128]{2,1,0:T(8,128)(2,1)S(1)}, bf16[4,48,128]{2,1,0:T(8,128)(2,1)S(1)}, u32[]{:S(2)}, u32[]{:S(2)}) collective-permute-start(bf16[4,48,128]{2,1,0:T(8,128)(2,1)S(1)} %get-tuple-element.49), channel_id=1, source_target_pairs={{0,1},{1,0},{2,3},{3,2},{4,5},{5,4},{6,7},{7,6},{8,9},{9,8},{10,11... | collective-permute-start | bytes 147464 | tf_op jit(solution)/shard_map/ppermute | solution.py:626
  58.3 10.1 %collective-permute-start.3 = (bf16[4,48,128]{2,1,0:T(8,128)(2,1)S(1)}, bf16[4,48,128]{2,1,0:T(8,128)(2,1)S(1)}, u32[]{:S(2)}, u32[]{:S(2)}) collective-permute-start(bf16[4,48,128]{2,1,0:T(8,128)(2,1)S(1)} %get-tuple-element.50), channel_id=1, source_target_pairs={{1,2},{2,1},{3,4},{4,3},{5,6},{6,5},{7,8},{8,7},{9,10},{10,9},{11,... | collective-permute-start | bytes 147464 | tf_op jit(solution)/shard_map/ppermute | solution.py:627
  69.1 6.7 %copy-start.1 = (bf16[16,3,16,128]{3,2,1,0:T(8,128)(2,1)S(1)}, bf16[16,3,16,128]{3,2,1,0:T(8,128)(2,1)}, u32[]{:S(2)}) copy-start(bf16[16,3,16,128]{3,2,1,0:T(8,128)(2,1)} %get-tuple-element.37) | copy-start | bytes 589828
  69.1 15.0 %all-to-all-start.3 = ((bf16[32,24,128]{2,1,0:T(8,128)(2,1)}), bf16[32,24,128]{2,1,0:T(8,128)(2,1)S(1)}, u32[]{:S(2)}, u32[]{:S(2)}) async-start(bf16[32,24,128]{2,1,0:T(8,128)(2,1)} %spread.1), calls=%async_computation.3 | async-start | bytes 393216 | tf_op jit(solution)/shard_map/all_to_all | solution.py:637

commit v11 on v9

--- a/solution.py
+++ b/solution.py
@@ -249,7 +249,6 @@
     to_second,
     own_grad,
     bias,
-    bias_grad,
 ):
     samples, count, width = cotangent.shape
     heads = 4
@@ -287,7 +286,6 @@
         begin = device[0] * count - RIM + w * QW
         allowed = (line >= key_range[w, 0] - begin) & (line < key_range[w, 1] - begin)
         bias[w] = jnp.where(allowed, values, NEG_FILL)
-        bias_grad[w] = jnp.zeros((KW, KW), F32)
     diag = jnp.where((line >> 5) == (lane >> 5), 1.0, 0.0).astype(BF)
     head_of = iota((QW, width), 1) >> 5
 
@@ -312,7 +310,7 @@
         return jnp.concatenate(sums, axis=0).astype(BF)
 
     def sample(s, carry):
-        project_sum, combine_sum = carry
+        project_sum, combine_sum, bias_sums = carry
         before, after = sides(first[s].astype(F32), second[s].astype(F32))
         x_hat, _ = norm(jnp.concatenate([before, after], axis=0))
         rims = (x_hat * gain).astype(BF)
@@ -348,8 +346,7 @@
         mixture = jnp.concatenate([gather_heads(tn(low[w], v[w])) for w in span], axis=0)
         row_dot = [jnp.sum(weights[w] * weights_grad[w], axis=0, keepdims=True) for w in span]
         score_grad = [weights[w] * (weights_grad[w] - row_dot[w]) for w in span]
-        for w in span:
-            bias_grad[w] += score_grad[w]
+        bias_sums = tuple(bias_sums[w] + score_grad[w] for w in span)
         score_low = [(x * scale).astype(BF) for x in score_grad]
         query_grads = [gather_heads(tn(score_low[w], k[w])).astype(BF) for w in span]
         key_grad = overlap([nn(score_low[w], q[w]) for w in span])
@@ -367,17 +364,18 @@
         to_first[s] = before.astype(BF)
         to_second[s] = after.astype(BF)
         own_grad[s] = normed_grad[RIM : RIM + count]
-        return project_sum, combine_sum
+        return project_sum, combine_sum, bias_sums
 
     start = (
         jnp.zeros((width, 4 * width), F32),
         jnp.zeros((width, width), F32),
+        tuple(jnp.zeros((KW, KW), F32) for _ in range(windows)),
     )
-    project_sum, combine_sum = lax.fori_loop(0, samples, sample, start, unroll=True)
+    project_sum, combine_sum, bias_sums = lax.fori_loop(0, samples, sample, start, unroll=True)
 
     table_grad = jnp.zeros((KW, KW), F32)
     for w in range(windows):
-        high, low = split2(bias_grad[w])
+        high, low = split2(bias_sums[w])
         hot = key_hot(w)
         by_slot = nn(hot, high) + nn(hot, low)
         high, low = split2(by_slot)
@@ -565,7 +563,6 @@
         in_specs=smem(2) + vmem(11),
         out_specs=tuple(vmem(4)),
         scratch_shapes=[
-            pltpu.VMEM((windows, KW, KW), F32),
             pltpu.VMEM((windows, KW, KW), F32),
         ],
         compiler_params=LIMIT,

time: 85.4 us -> 85.4 us (level)
  no operation moved by 1% of the time
where the time goes in v11:
time: 85.4 us; the launch traced here: 84.8 us
  starting transfers between devices  42.3 us (50%)
  blocking collectives  18.2 us (21%)
  Pallas kernels  11.7 us (14%)
  waiting for transfers between devices  10.5 us (12%)
  local copies, waits for them, and re-layouts  1.25 us (1%)
    all_to_all x1, blocking collectives, shards(): lax.all_to_all(outgoing, axes, 0, 0, axis_index_groups=planes, tiled=True)  18.2 us
    ppermute x2, starting transfers between devices, shards(): first = lax.ppermute(first, ('row', 'col'), pairs)  15.5 us
    all_to_all x1, starting transfers between devices, shards(): lax.all_to_all(tiles, 'col', 0, 0, tiled=True).reshape(entries, width)  9.16 us
    all_to_all x1, starting transfers between devices, shards(): lax.all_to_all(part, axes, 0, 0, axis_index_groups=lines, tiled=True)  7.03 us
    all_to_all x1, starting transfers between devices, shards(): lax.all_to_all(part, axes, 0, 0, axis_index_groups=planes, tiled=True)  6.81 us
    all_to_all x1, waiting for transfers between devices, shards(): lax.all_to_all(part, axes, 0, 0, axis_index_groups=planes, tiled=True)  5.83 us
    pallas_call x1, Pallas kernels, shards(): pl.pallas_call(attention_kernel, out_shape=(shape((32, 32, width), BF), s...  4.78 us
    all_to_all x1, waiting for transfers between devices, shards(): lax.all_to_all(part, axes, 0, 0, axis_index_groups=lines, tiled=True)  3.42 us
  transfers between devices with their start and end apart: 7, of which 3 were waited for; matrix products, arithmetic and copies ran while one was open for 0% of the time, Pallas kernels for 4%

profile of v11, /device:TPU:1, one launch (start us, length us, event | category | flops | bytes accessed | tf_op | source)
XLA Modules:
  0.0 84.8 jit_solution(12260264860631099102)
XLA Ops:
  0.6 1.8 %start.1 = (bf16[16,3,16,128]{3,2,1,0:T(8,128)(2,1)}, bf16[5,48,128]{2,1,0:T(8,128)(2,1)}, bf16[5,48,128]{2,1,0:T(8,128)(2,1)}) custom-call(s32[1]{0:T(128)} %bitcast.device, bf16[3,16,16,128]{3,2,1,0:T(8,128)(2,1)} %bitcast.16, bf16[4,128,128]{2,1,0:T(8,128)(2,1)} %atoms.5, s32[1,128]{1,0:T(1,128)} %bitcast.19, bf16[4,128]{1,0:T(4,128)(2,1)} %bitcast.18, ...), custom_call_target="tpu_custom_call" | custom-call | tf_op jit(solution)/shard_map/start/pallas_call | solution.py:499
  2.4 9.2 %all-to-all-start = ((bf16[16,3,16,128]{3,2,1,0:T(8,128)(2,1)}), bf16[16,3,16,128]{3,2,1,0:T(8,128)(2,1)S(1)}, u32[]{:S(2)}, u32[]{:S(2)}) async-start(bf16[16,3,16,128]{3,2,1,0:T(8,128)(2,1)} %get-tuple-element.37), calls=%async_computation | async-start | bytes 393216 | tf_op jit(solution)/shard_map/all_to_all | solution.py:526
  11.6 8.7 %collective-permute-start = (bf16[5,48,128]{2,1,0:T(8,128)(2,1)S(1)}, bf16[5,48,128]{2,1,0:T(8,128)(2,1)S(1)}, u32[]{:S(2)}, u32[]{:S(2)}) collective-permute-start(bf16[5,48,128]{2,1,0:T(8,128)(2,1)S(1)} %copy-done.7), channel_id=1, source_target_pairs={{1,2},{2,1},{3,4},{4,3},{5,6},{6,5},{7,8},{8,7},{9,10},{10,9},{11,... | collective-permute-start | bytes 184328 | tf_op jit(solution)/shard_map/ppermute | solution.py:528
  20.4 1.9 %collective-permute-start.1 = (bf16[5,48,128]{2,1,0:T(8,128)(2,1)S(1)}, bf16[5,48,128]{2,1,0:T(8,128)(2,1)S(1)}, u32[]{:S(2)}, u32[]{:S(2)}) collective-permute-start(bf16[5,48,128]{2,1,0:T(8,128)(2,1)S(1)} %copy-done), channel_id=1, source_target_pairs={{0,1},{1,0},{2,3},{3,2},{4,5},{5,4},{6,7},{7,6},{8,9},{9,8},{10,11... | collective-permute-start | bytes 184328 | tf_op jit(solution)/shard_map/ppermute | solution.py:529
  22.3 0.1 copy.17.key_range
  22.4 0.6 pair.1
  23.0 0.3 copy-done.2
  23.3 0.1 copy-done.3
  23.4 0.1 copy-done.4
  23.4 0.7 prepare.1
  24.1 1.2 %collective-permute-done.1.second = bf16[5,48,128]{2,1,0:T(8,128)(2,1)S(1)} collective-permute-done((bf16[5,48,128]{2,1,0:T(8,128)(2,1)S(1)}, bf16[5,48,128]{2,1,0:T(8,128)(2,1)S(1)}, u32[]{:S(2)}, u32[]{:S(2)}) %collective-permute-start.1) | collective-permute-done | bytes 61472 | tf_op jit(solution)/shard_map/ppermute | solution.py:529
  25.3 4.8 %attention.1 = (bf16[32,32,128]{2,1,0:T(8,128)(2,1)S(1)}, bf16[4,48,128]{2,1,0:T(8,128)(2,1)S(1)}, bf16[4,48,128]{2,1,0:T(8,128)(2,1)S(1)}, f32[4,128,128]{2,1,0:T(8,128)S(1)}) custom-call(s32[4,2]{1,0:T(4,128)S(1)} %copy.17.key_range, s32[1]{0:T(128)} %bitcast.device, bf16[4,128,128]{2,1,0:T(8,128)(2,1)S(1)} %copy-done.3, bf16[128,512]{1,0:T(8,128)(2,1)S(1)} %copy-done.2, ...), custom_call_target="tpu_custom_call" | custom-call | tf_op jit(solution)/shard_map/attention/pallas_call | solution.py:555
  30.1 18.2 %all_to_all.20.scattered = bf16[32,32,128]{2,1,0:T(8,128)(2,1)S(1)} all-to-all(bf16[32,32,128]{2,1,0:T(8,128)(2,1)S(1)} %get-tuple-element.45), channel_id=1, replica_groups={{0,1,2,3,16,17,18,19,128,129,130,131,144,145,146,147,256,257,258,259,27..., dimensions={0} | all-to-all | bytes 524288 | tf_op jit(solution)/shard_map/all_to_all | solution.py:602
  48.3 0.7 middle.1
  49.1 7.0 %all-to-all-start.2 = ((bf16[16,32,128]{2,1,0:T(8,128)(2,1)}), bf16[16,32,128]{2,1,0:T(8,128)(2,1)S(1)}, u32[]{:S(2)}, u32[]{:S(2)}) async-start(bf16[16,32,128]{2,1,0:T(8,128)(2,1)} %middle.1), calls=%async_computation.2 | async-start | bytes 262144 | tf_op jit(solution)/shard_map/all_to_all | solution.py:613
  56.1 6.8 %collective-permute-start.2 = (bf16[4,48,128]{2,1,0:T(8,128)(2,1)S(1)}, bf16[4,48,128]{2,1,0:T(8,128)(2,1)S(1)}, u32[]{:S(2)}, u32[]{:S(2)}) collective-permute-start(bf16[4,48,128]{2,1,0:T(8,128)(2,1)S(1)} %get-tuple-element.49), channel_id=1, source_target_pairs={{1,2},{2,1},{3,4},{4,3},{5,6},{6,5},{7,8},{8,7},{9,10},{10,9},{11,... | collective-permute-start | bytes 147464 | tf_op jit(solution)/shard_map/ppermute | solution.py:614
  62.9 1.9 %collective-permute-start.3 = (bf16[4,48,128]{2,1,0:T(8,128)(2,1)S(1)}, bf16[4,48,128]{2,1,0:T(8,128)(2,1)S(1)}, u32[]{:S(2)}, u32[]{:S(2)}) collective-permute-start(bf16[4,48,128]{2,1,0:T(8,128)(2,1)S(1)} %get-tuple-element.50), channel_id=1, source_target_pairs={{0,1},{1,0},{2,3},{3,2},{4,5},{5,4},{6,7},{7,6},{8,9},{9,8},{10,11... | collective-permute-start | bytes 147464 | tf_op jit(solution)/shard_map/ppermute | solution.py:615
  64.8 3.4 %all-to-all-done.2.scattered = bf16[16,32,128]{2,1,0:T(8,128)(2,1)S(1)} async-done(((bf16[16,32,128]{2,1,0:T(8,128)(2,1)}), bf16[16,32,128]{2,1,0:T(8,128)(2,1)S(1)}, u32[]{:S(2)}, u32[]{:S(2)}) %all-to-all-start.2) | async-done | bytes 131104 | tf_op jit(solution)/shard_map/all_to_all | solution.py:613
  68.3 0.7 broadcast_in_dim.3
  69.0 6.8 %all-to-all-start.3 = ((bf16[32,24,128]{2,1,0:T(8,128)(2,1)}), bf16[32,24,128]{2,1,0:T(8,128)(2,1)S(1)}, u32[]{:S(2)}, u32[]{:S(2)}) async-start(bf16[32,24,128]{2,1,0:T(8,128)(2,1)} %broadcast_in_dim.3), calls=%async_computation.3 | async-start | bytes 393216 | tf_op jit(solution)/shard_map/all_to_all | solution.py:619
  75.8 1.1 %finish.1 = bf16[4,128,128]{2,1,0:T(8,128)(2,1)} custom-call(s32[1]{0:T(128)} %bitcast.device, bf16[4,128,128]{2,1,0:T(8,128)(2,1)S(1)} %copy-done.4, bf16[4,128,128]{2,1,0:T(8,128)(2,1)S(1)} %copy-done.3, f32[4,128,128]{2,1,0:T(8,128)S(1)} %get-tuple-element.52.own_grad, bf16[4,48,128]{2,1,0:T(8,128)(2,1)S(1)} %collective-permute-done.2.first, ...), custom_call_target="tpu_custom_call" | custom-call | tf_op jit(solution)/shard_map/finish/pallas_call | solution.py:629
  76.9 1.3 %band.1 = bf16[3,256,128]{2,1,0:T(8,128)(2,1)} custom-call(s32[1]{0:T(128)} %bitcast.device, bf16[768,128]{1,0:T(8,128)(2,1)S(1)} %bitcast.14, bf16[16,32,128]{2,1,0:T(8,128)(2,1)S(1)} %all-to-all-done.2.scattered, bf16[5,48,128]{2,1,0:T(8,128)(2,1)S(1)} %copy-done), custom_call_target="tpu_custom_call" | custom-call | tf_op jit(solution)/shard_map/band/pallas_call | solution.py:620
  78.2 5.8 %all-to-all-done.3.parts = bf16[32,24,128]{2,1,0:T(8,128)(2,1)S(1)} async-done(((bf16[32,24,128]{2,1,0:T(8,128)(2,1)}), bf16[32,24,128]{2,1,0:T(8,128)(2,1)S(1)}, u32[]{:S(2)}, u32[]{:S(2)}) %all-to-all-start.3) | async-done | bytes 196640 | tf_op jit(solution)/shard_map/all_to_all | solution.py:619
  84.1 0.8 last.1
  (18 shorter events, 0.1 us)
Async XLA Ops:
  2.4 9.2 %copy-start.7 = (bf16[5,48,128]{2,1,0:T(8,128)(2,1)S(1)}, bf16[5,48,128]{2,1,0:T(8,128)(2,1)}, u32[]{:S(2)}) copy-start(bf16[5,48,128]{2,1,0:T(8,128)(2,1)} %get-tuple-element.36) | copy-start | bytes 184324
  2.4 17.9 %copy-start = (bf16[5,48,128]{2,1,0:T(8,128)(2,1)S(1)}, bf16[5,48,128]{2,1,0:T(8,128)(2,1)}, u32[]{:S(2)}) copy-start(bf16[5,48,128]{2,1,0:T(8,128)(2,1)} %get-tuple-element.35.sent) | copy-start | bytes 184324
  2.4 19.9 %all-to-all-start = ((bf16[16,3,16,128]{3,2,1,0:T(8,128)(2,1)}), bf16[16,3,16,128]{3,2,1,0:T(8,128)(2,1)S(1)}, u32[]{:S(2)}, u32[]{:S(2)}) async-start(bf16[16,3,16,128]{3,2,1,0:T(8,128)(2,1)} %get-tuple-element.37), calls=%async_computation | async-start | bytes 393216 | tf_op jit(solution)/shard_map/all_to_all | solution.py:526
  11.6 10.7 %copy-start.6 = (s32[4,2]{0,1:T(2,128)S(1)}, s32[4,2]{0,1:T(2,128)}, u32[]{:S(2)}) copy-start(s32[4,2]{0,1:T(2,128)} %param.19) | copy-start | bytes 100
  11.6 12.5 %collective-permute-start = (bf16[5,48,128]{2,1,0:T(8,128)(2,1)S(1)}, bf16[5,48,128]{2,1,0:T(8,128)(2,1)S(1)}, u32[]{:S(2)}, u32[]{:S(2)}) collective-permute-start(bf16[5,48,128]{2,1,0:T(8,128)(2,1)S(1)} %copy-done.7), channel_id=1, source_target_pairs={{1,2},{2,1},{3,4},{4,3},{5,6},{6,5},{7,8},{8,7},{9,10},{10,9},{11,... | collective-permute-start | bytes 184328 | tf_op jit(solution)/shard_map/ppermute | solution.py:528
  20.4 5.0 %collective-permute-start.1 = (bf16[5,48,128]{2,1,0:T(8,128)(2,1)S(1)}, bf16[5,48,128]{2,1,0:T(8,128)(2,1)S(1)}, u32[]{:S(2)}, u32[]{:S(2)}) collective-permute-start(bf16[5,48,128]{2,1,0:T(8,128)(2,1)S(1)} %copy-done), channel_id=1, source_target_pairs={{0,1},{1,0},{2,3},{3,2},{4,5},{5,4},{6,7},{7,6},{8,9},{9,8},{10,11... | collective-permute-start | bytes 184328 | tf_op jit(solution)/shard_map/ppermute | solution.py:529
  22.4 0.9 %copy-start.2 = (bf16[128,512]{1,0:T(8,128)(2,1)S(1)}, bf16[128,512]{1,0:T(8,128)(2,1)}, u32[]{:S(2)}) copy-start(bf16[128,512]{1,0:T(8,128)(2,1)} %project.5) | copy-start | bytes 393220
  22.4 1.0 %copy-start.3 = (bf16[4,128,128]{2,1,0:T(8,128)(2,1)S(1)}, bf16[4,128,128]{2,1,0:T(8,128)(2,1)}, u32[]{:S(2)}) copy-start(bf16[4,128,128]{2,1,0:T(8,128)(2,1)} %cotangent.5) | copy-start | bytes 393220
  22.4 1.0 %copy-start.4 = (bf16[4,128,128]{2,1,0:T(8,128)(2,1)S(1)}, bf16[4,128,128]{2,1,0:T(8,128)(2,1)}, u32[]{:S(2)}) copy-start(bf16[4,128,128]{2,1,0:T(8,128)(2,1)} %atoms.5) | copy-start | bytes 393220
  22.4 1.0 %copy-start.5 = (bf16[128,128]{1,0:T(8,128)(2,1)S(1)}, bf16[128,128]{1,0:T(8,128)(2,1)}, u32[]{:S(2)}) copy-start(bf16[128,128]{1,0:T(8,128)(2,1)} %combine.1) | copy-start | bytes 98308
  49.1 19.2 %all-to-all-start.2 = ((bf16[16,32,128]{2,1,0:T(8,128)(2,1)}), bf16[16,32,128]{2,1,0:T(8,128)(2,1)S(1)}, u32[]{:S(2)}, u32[]{:S(2)}) async-start(bf16[16,32,128]{2,1,0:T(8,128)(2,1)} %middle.1), calls=%async_computation.2 | async-start | bytes 262144 | tf_op jit(solution)/shard_map/all_to_all | solution.py:613
  56.1 12.2 %collective-permute-start.2 = (bf16[4,48,128]{2,1,0:T(8,128)(2,1)S(1)}, bf16[4,48,128]{2,1,0:T(8,128)(2,1)S(1)}, u32[]{:S(2)}, u32[]{:S(2)}) collective-permute-start(bf16[4,48,128]{2,1,0:T(8,128)(2,1)S(1)} %get-tuple-element.49), channel_id=1, source_target_pairs={{1,2},{2,1},{3,4},{4,3},{5,6},{6,5},{7,8},{8,7},{9,10},{10,9},{11,... | collective-permute-start | bytes 147464 | tf_op jit(solution)/shard_map/ppermute | solution.py:614
  62.9 5.4 %collective-permute-start.3 = (bf16[4,48,128]{2,1,0:T(8,128)(2,1)S(1)}, bf16[4,48,128]{2,1,0:T(8,128)(2,1)S(1)}, u32[]{:S(2)}, u32[]{:S(2)}) collective-permute-start(bf16[4,48,128]{2,1,0:T(8,128)(2,1)S(1)} %get-tuple-element.50), channel_id=1, source_target_pairs={{0,1},{1,0},{2,3},{3,2},{4,5},{5,4},{6,7},{7,6},{8,9},{9,8},{10,11... | collective-permute-start | bytes 147464 | tf_op jit(solution)/shard_map/ppermute | solution.py:615
  69.0 15.1 %all-to-all-start.3 = ((bf16[32,24,128]{2,1,0:T(8,128)(2,1)}), bf16[32,24,128]{2,1,0:T(8,128)(2,1)S(1)}, u32[]{:S(2)}, u32[]{:S(2)}) async-start(bf16[32,24,128]{2,1,0:T(8,128)(2,1)} %broadcast_in_dim.3), calls=%async_computation.3 | async-start | bytes 393216 | tf_op jit(solution)/shard_map/all_to_all | solution.py:619
  75.8 1.1 %copy-start.1 = (bf16[16,3,16,128]{3,2,1,0:T(8,128)(2,1)S(1)}, bf16[16,3,16,128]{3,2,1,0:T(8,128)(2,1)}, u32[]{:S(2)}) copy-start(bf16[16,3,16,128]{3,2,1,0:T(8,128)(2,1)} %get-tuple-element.37) | copy-start | bytes 589828
